TPU v7x, 32 devices: a whole 2x2x4 slice. The times are simulated.
32 devices in a mesh: narrow: 4 (over y, x), wide: 8 (over z, core).
Axes of the slice: x: 2, y: 2, z: 4, core: 2. Of those that a mesh axis runs over, the one named last changes fastest.
Arguments:
- tokens: bfloat16 [8, 2048, 768], P('wide', 'narrow'), may hold values from -6 to 6
- condition: bfloat16 [8, 2, 128], P('wide'), may hold values from -6 to 6
- docs_per_row: int32 [8], P('wide'), may hold values from 1 to 2, as said below
- w_ada: bfloat16 [128, 4608], replicated, may hold values from -0.5 to 0.5
- b_ada: bfloat16 [4608], replicated, may hold values from -3 to 3
- gain_one: bfloat16 [768], replicated, may hold values from 0.25 to 1.75
- w_qkv: bfloat16 [768, 2304], replicated, may hold values from -0.21875 to 0.21875
- w_out: bfloat16 [768, 768], replicated, may hold values from -1.75 to 1.75
- gain_two: bfloat16 [768], replicated, may hold values from 0.25 to 1.75
- w_up: bfloat16 [768, 3072], replicated, may hold values from -0.21875 to 0.21875
- b_up: bfloat16 [3072], replicated, may hold values from -3 to 3
- w_down: bfloat16 [3072, 768], replicated, may hold values from -0.109375 to 0.109375
- b_down: bfloat16 [768], replicated, may hold values from -3 to 3
- cotangent: bfloat16 [8, 2048, 768], P('wide', 'narrow'), may hold values from -6 to 6
Outputs:
- output: bfloat16 [8, 2048, 768], P('wide', 'narrow')
- grad_tokens: float32 [8, 2048, 768], P('wide', 'narrow')
- grad_condition: float32 [8, 2, 128], P('wide')
- grad_w_ada: float32 [128, 4608], P(None, 'wide')
- grad_b_ada: float32 [4608], P('wide')
- grad_gain_one: float32 [768], P('wide')
- grad_w_qkv: float32 [768, 2304], P('wide')
- grad_w_out: float32 [768, 768], P('wide')
- grad_gain_two: float32 [768], P('wide')
- grad_w_up: float32 [768, 3072], P('wide')
- grad_b_up: float32 [3072], P('wide')
- grad_w_down: float32 [3072, 768], P('wide')
- grad_b_down: float32 [768], P('wide')
Inputs may be any that keep to these rules, and one draw needn't show every extreme that they name: `docs_per_row`: each entry is 1 (the row is one sequence of 2048 tokens) or 2 (the row holds 2 sequences of 1024 tokens). In every draw the rows of some index of wide are all of the first kind and those of another index all of the second.
All inputs are finite; a program needn't handle non-finite values.
Results may differ from a plain program's by a relative error of at most 0.014.
The roundings to bfloat16 on the way count: a program that leaves them out, or rounds other values in their place, can miss the bound.
Values may be sent and summed in bfloat16 or wider, within the bound.
A program may use at most 192 MiB of HBM per device.

v0:
```python
import jax
import jax.numpy as jnp
from jax import lax
from jax.sharding import PartitionSpec as P

HEADS = 12
HEAD_DIM = 64
DOCS = 2


EPS = 1e-05
HIGH = lax.Precision.HIGHEST


def normalize(values):
    mean = jnp.mean(values, axis=-1, keepdims=True)
    centred = values - mean
    spread = jnp.mean(centred * centred, axis=-1, keepdims=True)
    return centred * lax.rsqrt(spread + EPS)


def modulated(values, gain, shift, scale):
    return normalize(values) * gain * (1.0 + scale) + shift


def gelu_tanh(values):
    return (
        0.5
        * values
        * (1.0 + jnp.tanh(0.7978845608028654 * (values + 0.044715 * values * values * values)))
    )


def rotate(values, cosine, sine):
    half = values.shape[-1] // 2
    turned = jnp.concatenate([-values[..., half:], values[..., :half]], axis=-1)
    return values * cosine + turned * sine


def angles(position, head_dim):
    freq = 10000.0 ** (-jnp.arange(head_dim // 2, dtype=jnp.float32) * 2.0 / head_dim)
    angle = position.astype(jnp.float32)[..., None] * freq
    angle = jnp.concatenate([angle, angle], axis=-1)
    return (jnp.cos(angle), jnp.sin(angle))


def attend(query, keys, values, docs):
    length, group, head_dim = query.shape
    count = length // docs
    block = min(512, count)
    factor = head_dim ** (-0.5)
    keys_doc = keys.reshape(count, docs, group, head_dim)
    values_doc = values.reshape(count, docs, group, head_dim)
    pieces = query.reshape(count // block, block, docs, group, head_dim)

    def one_block(piece):
        scores = (
            jnp.einsum("qshd,kshd->shqk", piece, keys_doc, preferred_element_type=jnp.float32)
            * factor
        )
        top = jnp.max(scores, axis=-1, keepdims=True)
        weights = jnp.exp(scores - top)
        total = jnp.sum(weights, axis=-1, keepdims=True)
        probs = (weights / total).astype(jnp.bfloat16)
        mixed = jnp.einsum("shqk,kshd->qshd", probs, values_doc, preferred_element_type=jnp.float32)
        return (mixed.astype(jnp.bfloat16), (top + jnp.log(total))[..., 0])

    mixed, logsum = lax.map(one_block, pieces)
    logsum = jnp.transpose(logsum, (0, 3, 1, 2)).reshape(length, group)
    return (mixed.reshape(length, group, head_dim), logsum)


def attend_back(query, keys, values, logsum, grad_out, docs):
    length, group, head_dim = query.shape
    count = length // docs
    block = min(512, count)
    factor = head_dim ** (-0.5)
    keys_doc = keys.reshape(count, docs, group, head_dim)
    values_doc = values.reshape(count, docs, group, head_dim)
    pieces = query.reshape(count // block, block, docs, group, head_dim)
    sum_pieces = logsum.reshape(count // block, block, docs, group)
    grad_pieces = grad_out.reshape(count // block, block, docs, group, head_dim)

    def step(carry, item):
        grad_keys, grad_values = carry
        piece, sum_piece, grad_piece = item
        scores = (
            jnp.einsum("qshd,kshd->shqk", piece, keys_doc, preferred_element_type=jnp.float32)
            * factor
        )
        probs = jnp.exp(scores - jnp.transpose(sum_piece, (1, 2, 0))[..., None])
        low_probs = probs.astype(jnp.bfloat16)
        grad_values = grad_values + jnp.einsum(
            "shqk,qshd->kshd", low_probs, grad_piece, preferred_element_type=jnp.float32
        )
        grad_probs = jnp.einsum(
            "qshd,kshd->shqk", grad_piece, values_doc, preferred_element_type=jnp.float32
        )
        centre = jnp.sum(grad_probs * probs, axis=-1, keepdims=True)
        grad_scores = (probs * (grad_probs - centre)).astype(jnp.bfloat16)
        grad_query = (
            jnp.einsum("shqk,kshd->qshd", grad_scores, keys_doc, preferred_element_type=jnp.float32)
            * factor
        )
        grad_keys = (
            grad_keys
            + jnp.einsum("shqk,qshd->kshd", grad_scores, piece, preferred_element_type=jnp.float32)
            * factor
        )
        return ((grad_keys, grad_values), grad_query)

    zeros = jnp.zeros((count, docs, group, head_dim), jnp.float32)
    (grad_keys, grad_values), grad_query = lax.scan(
        step, (zeros, zeros), (pieces, sum_pieces, grad_pieces)
    )
    shape = (length, group, head_dim)
    return (
        grad_query.reshape(shape).astype(jnp.bfloat16),
        grad_keys.reshape(shape).astype(jnp.bfloat16),
        grad_values.reshape(shape).astype(jnp.bfloat16),
    )


def attend_row(item):
    query, keys, values, docs = item
    return lax.cond(
        docs == 1, lambda: attend(query, keys, values, 1), lambda: attend(query, keys, values, DOCS)
    )


def back_row(item):
    query, keys, values, logsum, grad_out, docs = item
    return lax.cond(
        docs == 1,
        lambda: attend_back(query, keys, values, logsum, grad_out, 1),
        lambda: attend_back(query, keys, values, logsum, grad_out, DOCS),
    )


def body(
    tokens,
    condition,
    docs_per_row,
    w_ada,
    b_ada,
    gain_one,
    w_qkv,
    w_out,
    gain_two,
    w_up,
    b_up,
    w_down,
    b_down,
    cotangent,
):
    count_rows, local, width = tokens.shape
    shards = lax.axis_size("narrow")
    group = HEADS // shards
    head_dim = HEAD_DIM
    length = local * shards
    index = lax.axis_index("narrow") * local + jnp.arange(local, dtype=jnp.int32)
    kinds = docs_per_row[:, None]
    segment = index[None, :] % kinds
    position = index[None, :] // kinds
    cosine, sine = angles(position, head_dim)
    cosine = cosine[:, :, None, :]
    sine = sine[:, :, None, :]
    onehot = (segment[:, :, None] == jnp.arange(DOCS, dtype=jnp.int32)).astype(jnp.float32)
    mods = jnp.einsum(
        "rsc,cm->rsm", condition, w_ada, preferred_element_type=jnp.float32
    ) + b_ada.astype(jnp.float32)
    per_token = jnp.einsum("rls,rsm->rlm", onehot, mods, precision=HIGH)
    shift_one, scale_one, gate_one, shift_two, scale_two, gate_two = jnp.split(
        per_token, 6, axis=-1
    )
    inputs = tokens.astype(jnp.float32)
    first_in, first_back = jax.vjp(
        modulated, inputs, gain_one.astype(jnp.float32), shift_one, scale_one
    )
    first_low = first_in.astype(jnp.bfloat16).reshape(-1, width)
    projected = jnp.dot(first_low, w_qkv, preferred_element_type=jnp.float32).reshape(
        count_rows, local, 3, HEADS, head_dim
    )
    query_rot, turn_back = jax.vjp(lambda values: rotate(values, cosine, sine), projected[:, :, 0])
    key_rot = rotate(projected[:, :, 1], cosine, sine)

    def to_heads(values):
        return values.astype(jnp.bfloat16).reshape(count_rows, local, shards, group * head_dim)

    def head_view(values):
        return values.reshape(count_rows, length, group, head_dim)

    query_h, key_h, value_h = (
        lax.all_to_all(to_heads(query_rot), "narrow", split_axis=2, concat_axis=1, tiled=True),
        lax.all_to_all(to_heads(key_rot), "narrow", split_axis=2, concat_axis=1, tiled=True),
        lax.all_to_all(
            to_heads(projected[:, :, 2]), "narrow", split_axis=2, concat_axis=1, tiled=True
        ),
    )
    query_h = head_view(query_h)
    key_h = head_view(key_h)
    value_h = head_view(value_h)
    mixed_h, logsum = lax.map(attend_row, (query_h, key_h, value_h, docs_per_row))
    mixed = lax.all_to_all(
        mixed_h.reshape(count_rows, length, 1, group * head_dim),
        "narrow",
        split_axis=1,
        concat_axis=2,
        tiled=True,
    )
    attended = mixed.reshape(count_rows * local, width)
    branch = jnp.dot(attended, w_out, preferred_element_type=jnp.float32).reshape(
        count_rows, local, width
    )
    middle = inputs + gate_one * branch
    second_in, second_back = jax.vjp(
        modulated, middle, gain_two.astype(jnp.float32), shift_two, scale_two
    )
    second_low = second_in.astype(jnp.bfloat16).reshape(-1, width)
    hidden = jnp.dot(second_low, w_up, preferred_element_type=jnp.float32) + b_up.astype(
        jnp.float32
    )
    active, active_back = jax.vjp(gelu_tanh, hidden)
    active_low = active.astype(jnp.bfloat16)
    down = (
        jnp.dot(active_low, w_down, preferred_element_type=jnp.float32) + b_down.astype(jnp.float32)
    ).reshape(count_rows, local, width)
    output = (middle + gate_two * down).astype(jnp.bfloat16)
    grad_y = cotangent.astype(jnp.float32)
    grad_gate_two = grad_y * down
    grad_down = (grad_y * gate_two).astype(jnp.bfloat16).reshape(-1, width)
    sum_b_down = jnp.sum(grad_down.astype(jnp.float32), axis=0)
    sum_w_down = jnp.einsum("tf,td->fd", active_low, grad_down, preferred_element_type=jnp.float32)
    grad_active = jnp.einsum("td,fd->tf", grad_down, w_down, preferred_element_type=jnp.float32)
    grad_hidden = active_back(grad_active)[0].astype(jnp.bfloat16)
    sum_b_up = jnp.sum(grad_hidden.astype(jnp.float32), axis=0)
    sum_w_up = jnp.einsum("td,tf->df", second_low, grad_hidden, preferred_element_type=jnp.float32)
    grad_second = jnp.einsum(
        "tf,df->td", grad_hidden, w_up, preferred_element_type=jnp.float32
    ).reshape(count_rows, local, width)
    grad_middle_norm, sum_gain_two, grad_shift_two, grad_scale_two = second_back(grad_second)
    grad_middle = grad_y + grad_middle_norm
    grad_gate_one = grad_middle * branch
    grad_branch = (grad_middle * gate_one).astype(jnp.bfloat16).reshape(-1, width)
    sum_w_out = jnp.einsum("td,te->de", attended, grad_branch, preferred_element_type=jnp.float32)
    grad_attended = jnp.einsum(
        "te,de->td", grad_branch, w_out, preferred_element_type=jnp.float32
    ).astype(jnp.bfloat16)
    grad_mixed = lax.all_to_all(
        grad_attended.reshape(count_rows, local, shards, group * head_dim),
        "narrow",
        split_axis=2,
        concat_axis=1,
        tiled=True,
    )
    grad_mixed = head_view(grad_mixed)
    grad_query_h, grad_key_h, grad_value_h = lax.map(
        back_row, (query_h, key_h, value_h, logsum, grad_mixed, docs_per_row)
    )

    def from_heads(values):
        return values.reshape(count_rows, length, 1, group * head_dim)

    grad_query, grad_key, grad_value = (
        lax.all_to_all(from_heads(grad_query_h), "narrow", split_axis=1, concat_axis=2, tiled=True),
        lax.all_to_all(from_heads(grad_key_h), "narrow", split_axis=1, concat_axis=2, tiled=True),
        lax.all_to_all(from_heads(grad_value_h), "narrow", split_axis=1, concat_axis=2, tiled=True),
    )
    seq_shape = (count_rows, local, HEADS, head_dim)
    grad_query_raw = turn_back(grad_query.reshape(seq_shape).astype(jnp.float32))[0]
    grad_key_raw = turn_back(grad_key.reshape(seq_shape).astype(jnp.float32))[0]
    grad_projected = jnp.stack(
        [grad_query_raw, grad_key_raw, grad_value.reshape(seq_shape).astype(jnp.float32)], axis=2
    )
    grad_projected = grad_projected.astype(jnp.bfloat16).reshape(-1, 3 * width)
    sum_w_qkv = jnp.einsum(
        "td,te->de", first_low, grad_projected, preferred_element_type=jnp.float32
    )
    grad_first = jnp.einsum(
        "te,de->td", grad_projected, w_qkv, preferred_element_type=jnp.float32
    ).reshape(count_rows, local, width)
    grad_inputs_norm, sum_gain_one, grad_shift_one, grad_scale_one = first_back(grad_first)
    grad_inputs = grad_middle + grad_inputs_norm
    grad_per = jnp.concatenate(
        [
            grad_shift_one,
            grad_scale_one,
            grad_gate_one,
            grad_shift_two,
            grad_scale_two,
            grad_gate_two,
        ],
        axis=-1,
    )
    grad_mods = jnp.einsum("rls,rlm->rsm", onehot, grad_per, precision=HIGH)
    sum_b_ada = jnp.sum(grad_mods, axis=(0, 1))
    sum_w_ada_turned = jnp.einsum(
        "rsm,rsc->mc", grad_mods, condition.astype(jnp.float32), precision=HIGH
    )
    grad_cond_part = jnp.einsum("rsm,cm->rsc", grad_mods, w_ada.astype(jnp.float32), precision=HIGH)
    (
        share_ada,
        share_qkv,
        share_out,
        share_up,
        share_down,
        piece_ada,
        piece_one,
        piece_two,
        piece_up,
        piece_down,
    ) = (
        lax.psum_scatter(sum_w_ada_turned, "wide", scatter_dimension=0, tiled=True),
        lax.psum_scatter(sum_w_qkv, "wide", scatter_dimension=0, tiled=True),
        lax.psum_scatter(sum_w_out, "wide", scatter_dimension=0, tiled=True),
        lax.psum_scatter(sum_w_up, "wide", scatter_dimension=0, tiled=True),
        lax.psum_scatter(sum_w_down, "wide", scatter_dimension=0, tiled=True),
        lax.psum_scatter(sum_b_ada, "wide", scatter_dimension=0, tiled=True),
        lax.psum_scatter(sum_gain_one, "wide", scatter_dimension=0, tiled=True),
        lax.psum_scatter(sum_gain_two, "wide", scatter_dimension=0, tiled=True),
        lax.psum_scatter(sum_b_up, "wide", scatter_dimension=0, tiled=True),
        lax.psum_scatter(sum_b_down, "wide", scatter_dimension=0, tiled=True),
    )
    (
        total_ada,
        total_qkv,
        total_out,
        total_up,
        total_down,
        vector_ada,
        vector_one,
        vector_two,
        vector_up,
        vector_down,
        grad_condition,
    ) = lax.psum(
        (
            share_ada,
            share_qkv,
            share_out,
            share_up,
            share_down,
            piece_ada,
            piece_one,
            piece_two,
            piece_up,
            piece_down,
            grad_cond_part,
        ),
        "narrow",
    )
    return (
        output,
        grad_inputs,
        grad_condition,
        total_ada.T,
        vector_ada,
        vector_one,
        total_qkv,
        total_out,
        vector_two,
        total_up,
        vector_up,
        total_down,
        vector_down,
    )


def solution(mesh):
    in_specs = (
        P("wide", "narrow", None),
        P("wide", None, None),
        P("wide"),
        P(),
        P(),
        P(),
        P(),
        P(),
        P(),
        P(),
        P(),
        P(),
        P(),
        P("wide", "narrow", None),
    )
    out_specs = (
        P("wide", "narrow", None),
        P("wide", "narrow", None),
        P("wide", None, None),
        P(None, "wide"),
        P("wide"),
        P("wide"),
        P("wide", None),
        P("wide", None),
        P("wide"),
        P("wide", None),
        P("wide"),
        P("wide", None),
        P("wide"),
    )
    return jax.shard_map(body, mesh=mesh, in_specs=in_specs, out_specs=out_specs, check_vma=False)
```

profile of v0, /device:TPU:0, one launch (start us, length us, event | category | flops | bytes accessed | tf_op | source)
XLA Modules:
  0.0 912.9 jit_solution(2107163655373730929)
XLA Ops:
  12.2 5.9 copy.309
  32.1 5.2 all-to-all-start.2
  48.1 13.2 %all_to_all.102 = bf16[1,512,4,192]{1,3,0,2:T(8,128)(2,1)S(1)} all-to-all(bf16[1,512,4,192]{1,3,0,2:T(8,128)(2,1)S(1)} %get-tuple-element.723), channel_id=1, replica_groups=mesh['narrow'=4,'wide'=8] {'narrow'}, dimensions={2} | all-to-all | bytes 1572864 | tf_op jit(solution)/shard_map/all_to_all | solution.py:195
  78.5 46.4 %conditional.2 = (bf16[2048,3,64]{2,1,0:T(4,128)(2,1)}, f32[2048,3]{1,0:T(8,128)}) conditional(s32[]{:T(128)} %convert_element_type.263, (bf16[2048,3,64]{0,2,1:T(8,128)(2,1)}, bf16[2048,3,64]{0,2,1:T(8,128)(2,1)S(1)}, bf16[2048,3,64]{0,2,1:T(8,128)(2,1)S(1)}) %tuple.47, (bf16[2048,3,64]{0,2,1:T(8,128)(2,1)}, bf16[2048,3,64]{0,2,1:T(8,128)(2,1)S(1)}, ...), branch_computations={%region_2.7_spmd, %region_7.12_spmd} | conditional | flops 833811456 | bytes 60920124 | solution.py:126
  80.0 4.7 copy.290
  96.8 21.8 %while.51 = (s32[]{:T(128)}, bf16[2,512,2,3,64]{1,4,3,2,0:T(8,128)(2,1)}, f32[2,2,3,512]{3,2,1,0:T(4,128)}, bf16[2,512,2,3,64]{1,4,3,2,0:T(8,128)(2,1)}, bf16[10...) while((s32[]{:T(128)}, bf16[2,512,2,3,64]{1,4,3,2,0:T(8,128)(2,1)}, ...), condition=%wide.region_6.6_spmd, body=%wide.region_3.5_spmd.sunk | while | flops 833811456 | bytes 49860844 | solution.py:68
  132.0 13.6 %reduce.17 = bf16[2048,192]{1,0:T(8,128)(2,1)} reduce(bf16[2048,1,1,192]{3,2,1,0:T(2,128)(2,1)} %bitcast.455, bf16[]{:T(256)} %broadcast.557), dimensions={1,2}, to_apply=%bitcast.292.reduce_sub_computation | reduce | bytes 1572866
  167.1 5.7 copy.321
  186.8 11.7 %convert_reduce_fusion = (f32[3072]{0:T(1024)}, bf16[512,3072]{1,0:T(8,128)(2,1)S(1)}) fusion(f32[512,3072]{1,0:T(8,128)S(1)} %fusion.152, f32[3072]{0:T(1024)S(1)} %copy-done.87, bf16[512,768]{1,0:T(8,128)(2,1)S(1)} %copy-done.53, bf16[3072,768]{1,0:T(8,128)(2,1)} %param.37), kind=kOutput, calls=%fused_computation.105 | convolution fusion | flops 2458383360 | bytes 14966784 | tf_op jit(solution)/shard_map/td,fd->tf/dot_general | solution.py:234
  202.3 8.5 fusion.146
  216.0 11.2 %all_to_all.103 = bf16[1,512,4,192]{1,3,0,2:T(8,128)(2,1)S(1)} all-to-all(bf16[1,512,4,192]{1,3,0,2:T(8,128)(2,1)S(1)} %bitcast.488), channel_id=1, replica_groups=mesh['narrow'=4,'wide'=8] {'narrow'}, dimensions={2} | all-to-all | bytes 1572864 | tf_op jit(solution)/shard_map/all_to_all | solution.py:249
  229.3 84.0 %conditional.3 = (bf16[2048,3,64]{2,1,0:T(4,128)(2,1)}, bf16[2048,3,64]{2,1,0:T(4,128)(2,1)}, bf16[2048,3,64]{2,1,0:T(4,128)(2,1)S(1)}) conditional(s32[]{:T(128)} %convert_element_type.263, (bf16[2048,3,64]{0,2,1:T(8,128)(2,1)}, f32[2048,3]{1,0:T(8,128)S(1)}, bf16[2048,3,64]{0,2,1:T(8,128)(2,1)}, bf16[2048,3,64]{0,2,1:T(8,128)(2,1)S(1)}, ...), branch_computations={%region_16.20_spmd, %region_20.24_spmd} | conditional | flops 2053174272 | bytes 155857408 | solution.py:133
  241.5 4.7 copy.299
  252.5 44.9 %while.52 = (s32[]{:T(128)}, f32[1024,2,3,64]{0,3,2,1:T(8,128)S(1)}, f32[1024,2,3,64]{0,3,2,1:T(8,128)}, bf16[2,512,2,3,64]{1,4,3,2,0:T(8,128)(2,1)}, bf16[2,512...) while((s32[]{:T(128)}, ...), condition=%wide.region_19.19_spmd.clone, body=%wide.region_17.18_spmd.clone.sunk | while | flops 2053174272 | bytes 130642248 | solution.py:113
  258.4 6.4 multiply_reduce_fusion.12
  264.8 6.6 multiply_convert_fusion.9
  280.9 6.4 multiply_reduce_fusion.12
  287.3 6.6 multiply_convert_fusion.9
  320.0 12.7 %reduce.20 = bf16[2048,192]{1,0:T(8,128)(2,1)S(1)} reduce(bf16[2048,1,1,192]{3,2,1,0:T(2,128)(2,1)} %bitcast.458, bf16[]{:T(256)} %broadcast.557), dimensions={1,2}, to_apply=%bitcast.296.reduce_sub_computation | reduce | bytes 1572866
  345.8 13.6 %reduce.19 = bf16[2048,192]{1,0:T(8,128)(2,1)} reduce(bf16[2048,1,1,192]{3,2,1,0:T(2,128)(2,1)} %bitcast.459, bf16[]{:T(256)} %broadcast.557), dimensions={1,2}, to_apply=%bitcast.298.reduce_sub_computation | reduce | bytes 1572866
  374.1 11.6 %reduce.18 = bf16[2048,192]{1,0:T(8,128)(2,1)S(1)} reduce(bf16[2048,1,1,192]{3,2,1,0:T(2,128)(2,1)S(1)} %bitcast.456, bf16[]{:T(256)} %broadcast.557), dimensions={1,2}, to_apply=%bitcast.294.reduce_sub_computation | reduce | bytes 1572866
  419.1 4.9 copy.342
  448.5 5.0 fusion.120
  454.6 10.2 %fusion.142 = f32[3072,768]{1,0:T(8,128)} fusion(bf16[512,768]{1,0:T(8,128)(2,1)S(1)} %copy-done.54, f32[512,3072]{1,0:T(8,128)} %copy-done.28, f32[3072]{0:T(1024)S(1)} %copy-done.88), kind=kOutput, calls=%fused_computation.224 | convolution fusion | flops 2431647744 | bytes 16527360 | tf_op jit(solution)/shard_map/tf,td->fd/dot_general | solution.py:233
  466.0 6.9 fusion.154
  473.1 45.5 %reduce-scatter.6.cloned.1.call-done = f32[576,128]{1,0:T(8,128)} async-done(((f32[4608,128]{1,0:T(8,128)}), f32[576,128]{1,0:T(8,128)}) %reduce-scatter.6.cloned.1.call-update) | async-done | bytes 294928 | tf_op jit(solution)/shard_map/reduce_scatter | solution.py:313
  518.5 79.0 %reduce-scatter.8.cloned.1.call-done = f32[96,2304]{1,0:T(8,128)} async-done(((f32[768,2304]{1,0:T(8,128)}), f32[96,2304]{1,0:T(8,128)}) %reduce-scatter.8.cloned.1.call-update) | async-done | bytes 884752 | tf_op jit(solution)/shard_map/reduce_scatter | solution.py:314
  597.5 100.1 %reduce-scatter.14.cloned.1.call-done = f32[384,768]{1,0:T(8,128)} async-done(((f32[3072,768]{1,0:T(8,128)}), f32[384,768]{1,0:T(8,128)}) %reduce-scatter.14.cloned.1.call-update) | async-done | bytes 1179664 | tf_op jit(solution)/shard_map/reduce_scatter | solution.py:317
  697.5 100.0 %reduce-scatter.12.cloned.1.call-done = f32[96,3072]{1,0:T(8,128)} async-done(((f32[768,3072]{1,0:T(8,128)}), f32[96,3072]{1,0:T(8,128)}) %reduce-scatter.12.cloned.1.call-update) | async-done | bytes 1179664 | tf_op jit(solution)/shard_map/reduce_scatter | solution.py:316
  800.2 26.4 %all-reduce.9 = (f32[4608]{0:T(1024)S(1)}, f32[768]{0:T(1024)S(1)}, f32[768]{0:T(1024)S(1)}, f32[3072]{0:T(1024)S(1)}, f32[768]{0:T(1024)S(1)}) all-reduce(f32[4608]{0:T(1024)S(1)} %copy-done.65, f32[768]{0:T(1024)S(1)} %get-tuple-element.622, f32[768]{0:T(1024)S(1)} %copy-done.91, ...), channel_id=3, replica_groups=mesh['narrow'=4,'wide'=8] {'wide'}, use_global_device_ids=true, to_apply=%region_30.31.clone | all-reduce | flops 9984 | bytes 79872
  828.0 10.9 %all-reduce.10 = (f32[1,2,128]{2,1,0:T(2,128)}, f32[576]{0:T(1024)}, f32[96]{0:T(128)}, f32[96]{0:T(128)}, f32[384]{0:T(512)}, /*index=5*/f32[96]{0:T(128)}) all-reduce(f32[1,2,128]{2,1,0:T(2,128)S(1)} %convolution_bitcast_fusion.2, f32[576]{0:T(1024)S(1)} %dynamic-slice.2, ...), channel_id=1, replica_groups=mesh['narrow'=4,'wide'=8] {'narrow'}, use_global_device_ids=true, to_apply=%region_26.27 | all-reduce | flops 1504 | bytes 12032 | tf_op jit(solution)/shard_map/psum | solution.py:336
  838.9 60.2 %all-reduce.14.cloned.1.call-done = (f32[128,576]{0,1:T(8,128)}, f32[96,2304]{1,0:T(8,128)}, f32[96,768]{1,0:T(8,128)}, f32[96,3072]{1,0:T(8,128)}, f32[384,768]{1,0:T(8,128)}) async-done(((f32[128,576]{0,1:T(8,128)}, f32[96,2304]{1,0:T(8,128)}, f32[96,768]{1,0:T(8,128)}, f32[96,3072]{1,0:T(8,128)}, f32[384,768]{1,0:T(8,128)}), (f32[128,576]{0,1:T(8,128)}, f32[96,2304]{1,0:T(8,128)}, f32[96,768]{1,0:T(8,128)}, ...) | async-done | bytes 3833872 | tf_op jit(solution)/shard_map/psum | solution.py:336
  (386 shorter events, 291.1 us)
Async XLA Ops:
  7.2 170.2 %copy-start = (bf16[768,768]{1,0:T(8,128)(2,1)S(1)}, bf16[768,768]{1,0:T(8,128)(2,1)}, u32[]{:S(2)}) copy-start(bf16[768,768]{1,0:T(8,128)(2,1)} %param.33) | copy-start | bytes 3538948
  9.3 13.7 %copy-start.68 = (f32[512]{0:T(512)}, f32[512]{0:T(512)S(1)}, u32[]{:S(2)}) copy-start(f32[512]{0:T(512)S(1)} %broadcast_multiply_fusion.4) | copy-start | bytes 6148
  10.8 12.2 %copy-start.70 = (f32[512]{0:T(512)}, f32[512]{0:T(512)S(1)}, u32[]{:S(2)}) copy-start(f32[512]{0:T(512)S(1)} %fusion.136) | copy-start | bytes 6148
  32.1 16.0 %all-to-all-start.2 = ((bf16[1,512,4,192]{1,3,0,2:T(8,128)(2,1)}), bf16[1,512,4,192]{1,3,0,2:T(8,128)(2,1)S(1)}, u32[]{:S(2)}, u32[]{:S(2)}) async-start(bf16[1,512,4,192]{1,3,0,2:T(8,128)(2,1)} %bitcast.65), calls=%async_computation.2 | async-start | bytes 1572864 | tf_op jit(solution)/shard_map/all_to_all | solution.py:196
  61.3 12.9 %all-to-all-start = ((bf16[1,512,4,192]{1,3,0,2:T(8,128)(2,1)}), bf16[1,512,4,192]{1,3,0,2:T(8,128)(2,1)S(1)}, u32[]{:S(2)}, u32[]{:S(2)}) async-start(bf16[1,512,4,192]{1,3,0,2:T(8,128)(2,1)} %get-tuple-element.724), calls=%async_computation | async-start | bytes 1572864 | tf_op jit(solution)/shard_map/all_to_all | solution.py:194
  149.6 13.3 %all-to-all-start.3 = ((bf16[4,2,49152]{2,1,0:T(2,128)(2,1)}), bf16[4,2,49152]{2,1,0:T(2,128)(2,1)}, u32[]{:S(2)}, u32[]{:S(2)}) async-start(bf16[4,2,49152]{2,1,0:T(2,128)(2,1)} %reshape.986), calls=%async_computation.3 | async-start | bytes 1572864 | tf_op jit(solution)/shard_map/all_to_all | solution.py:204
  154.3 47.9 %copy-start.72 = (f32[768]{0:T(1024)}, f32[768]{0:T(1024)S(1)}, u32[]{:S(2)}) copy-start(f32[768]{0:T(1024)S(1)} %convert_element_type.270) | copy-start | bytes 9220
  155.0 47.3 %copy-start.84 = (f32[768]{0:T(1024)}, f32[768]{0:T(1024)S(1)}, u32[]{:S(2)}) copy-start(f32[768]{0:T(1024)S(1)} %convert_element_type.274) | copy-start | bytes 9220
  181.2 21.1 %copy-start.12 = (f32[1,512,768]{2,1,0:T(8,128)}, f32[1,512,768]{2,1,0:T(8,128)S(1)}, u32[]{:S(2)}) copy-start(f32[1,512,768]{2,1,0:T(8,128)S(1)} %get-tuple-element.709) | copy-start | bytes 4718596
  181.2 21.1 %copy-start.74 = (f32[512]{0:T(512)}, f32[512]{0:T(512)S(1)}, u32[]{:S(2)}) copy-start(f32[512]{0:T(512)S(1)} %broadcast_multiply_fusion.3) | copy-start | bytes 6148
  181.5 20.8 %copy-start.78 = (f32[512]{0:T(512)}, f32[512]{0:T(512)S(1)}, u32[]{:S(2)}) copy-start(f32[512]{0:T(512)S(1)} %fusion.137) | copy-start | bytes 6148
  184.1 14.4 %slice-start = ((s8[9437184]{0:T(1024)(128)(4,1)}), s8[4194304]{0:T(1024)(128)(4,1)S(1)}, s32[]{:S(2)}) async-start(s8[9437184]{0:T(1024)(128)(4,1)} %bitcast.436), calls=%async_computation.19 | async-start | bytes 8388608
  186.8 15.5 %copy-start.28 = (f32[512,3072]{1,0:T(8,128)}, f32[512,3072]{1,0:T(8,128)S(1)}, u32[]{:S(2)}) copy-start(f32[512,3072]{1,0:T(8,128)S(1)} %fusion.152) | copy-start | bytes 18874372
  186.8 11.8 %slice-start.1 = ((s8[9437184]{0:T(1024)(128)(4,1)}), s8[4194304]{0:T(1024)(128)(4,1)S(1)}, s32[]{:S(2)}) async-start(s8[9437184]{0:T(1024)(128)(4,1)} %bitcast.436), calls=%async_computation.20 | async-start | bytes 8388608
  186.8 11.8 %slice-start.2 = ((s8[9437184]{0:T(1024)(128)(4,1)}), s8[1048576]{0:T(1024)(128)(4,1)S(1)}, s32[]{:S(2)}) async-start(s8[9437184]{0:T(1024)(128)(4,1)} %bitcast.436), calls=%async_computation.21 | async-start | bytes 2097152
  216.0 13.3 %copy-start.21 = (f32[2048,3]{1,0:T(8,128)S(1)}, f32[2048,3]{1,0:T(8,128)}, u32[]{:S(2)}) copy-start(f32[2048,3]{1,0:T(8,128)} %get-tuple-element.285) | copy-start | bytes 73732
  335.0 28.5 %all-to-all-start.6 = ((bf16[4,2,49152]{2,1,0:T(2,128)(2,1)}), bf16[4,2,49152]{2,1,0:T(2,128)(2,1)}, u32[]{:S(2)}, u32[]{:S(2)}) async-start(bf16[4,2,49152]{2,1,0:T(2,128)(2,1)} %reshape.990), calls=%async_computation.6 | async-start | bytes 1572864 | tf_op jit(solution)/shard_map/all_to_all | solution.py:266
  363.5 32.9 %all-to-all-start.5 = ((bf16[4,2,49152]{2,1,0:T(2,128)(2,1)}), bf16[4,2,49152]{2,1,0:T(2,128)(2,1)}, u32[]{:S(2)}, u32[]{:S(2)}) async-start(bf16[4,2,49152]{2,1,0:T(2,128)(2,1)} %reshape.992), calls=%async_computation.5 | async-start | bytes 1572864 | tf_op jit(solution)/shard_map/all_to_all | solution.py:265
  367.7 105.4 %reduce-scatter.10.cloned.1.call-start = ((), (), s32[]{:S(2)}) async-start(), calls=%async_computation.15 | async-start | bytes 2654208 | tf_op jit(solution)/shard_map/reduce_scatter | solution.py:315
  396.4 20.0 %all-to-all-start.7 = ((bf16[4,2,49152]{2,1,0:T(2,128)(2,1)}), bf16[4,2,49152]{2,1,0:T(2,128)(2,1)S(1)}, u32[]{:S(2)}, u32[]{:S(2)}) async-start(bf16[4,2,49152]{2,1,0:T(2,128)(2,1)} %reshape.988), calls=%async_computation.7 | async-start | bytes 1572864 | tf_op jit(solution)/shard_map/all_to_all | solution.py:267
  400.5 118.0 %reduce-scatter.6.cloned.1.call-start = ((), (), s32[]{:S(2)}) async-start(), calls=%async_computation.13 | async-start | bytes 2654208 | tf_op jit(solution)/shard_map/reduce_scatter | solution.py:313
  448.5 149.0 %reduce-scatter.8.cloned.1.call-start = ((), (), s32[]{:S(2)}) async-start(), calls=%async_computation.14 | async-start | bytes 7962624 | tf_op jit(solution)/shard_map/reduce_scatter | solution.py:314
  453.5 244.0 %reduce-scatter.14.cloned.1.call-start = ((), (), s32[]{:S(2)}) async-start(), calls=%async_computation.17 | async-start | bytes 10616832 | tf_op jit(solution)/shard_map/reduce_scatter | solution.py:317
  464.9 332.7 %reduce-scatter.12.cloned.1.call-start = ((), (), s32[]{:S(2)}) async-start(), calls=%async_computation.16 | async-start | bytes 10616832 | tf_op jit(solution)/shard_map/reduce_scatter | solution.py:316
  472.9 324.7 %copy-start.95 = (u32[32]{0:T(128)S(1)}, u32[32]{0:T(128)}, u32[]{:S(2)}) copy-start(u32[32]{0:T(128)} %constant.187) | copy-start | bytes 388
  472.9 327.2 %copy-start.65 = (f32[4608]{0:T(1024)S(1)}, f32[4608]{0:T(1024)}, u32[]{:S(2)}) copy-start(f32[4608]{0:T(1024)} %get-tuple-element.747) | copy-start | bytes 55300
  472.9 327.2 %copy-start.86 = (f32[768]{0:T(1024)S(1)}, f32[768]{0:T(1024)}, u32[]{:S(2)}) copy-start(f32[768]{0:T(1024)} %get-tuple-element.700) | copy-start | bytes 9220
  472.9 327.2 %copy-start.89 = (f32[3072]{0:T(1024)S(1)}, f32[3072]{0:T(1024)}, u32[]{:S(2)}) copy-start(f32[3072]{0:T(1024)} %get-tuple-element.702) | copy-start | bytes 36868
  472.9 327.2 %copy-start.91 = (f32[768]{0:T(1024)S(1)}, f32[768]{0:T(1024)}, u32[]{:S(2)}) copy-start(f32[768]{0:T(1024)} %get-tuple-element.620) | copy-start | bytes 9220
  472.9 354.0 %copy-start.36 = (bf16[128,4608]{1,0:T(8,128)(2,1)S(1)}, bf16[128,4608]{1,0:T(8,128)(2,1)}, u32[]{:S(2)}) copy-start(bf16[128,4608]{1,0:T(8,128)(2,1)} %param.29) | copy-start | bytes 3538948
  473.0 354.0 %copy-start.61 = (f32[2,4608]{1,0:T(2,128)S(1)}, f32[2,4608]{1,0:T(2,128)}, u32[]{:S(2)}) copy-start(f32[2,4608]{1,0:T(2,128)} %copy-done.60) | copy-start | bytes 110596
  473.0 426.1 %all-reduce.14.cloned.1.call-start = ((), (), s32[]{:S(2)}) async-start(), calls=%async_computation.18 | async-start | bytes 7667712 | tf_op jit(solution)/shard_map/psum | solution.py:336
  (88 other events, 293.5 us)
Sparse Core Ops, SparseCore 0:
  371.4 69.9 reduce-scatter.9
  448.6 69.8 reduce-scatter.5
  520.8 76.5 reduce-scatter.7
  599.6 97.8 reduce-scatter.13
  699.7 97.8 reduce-scatter.11
  801.1 97.9 all-reduce.13
where the time goes:
time: 924 us; the launch traced here: 913 us
  waiting for transfers between devices  395 us (43%)
  local copies, waits for them, and re-layouts  191 us (21%)
  matrix products  119 us (13%)
  other arithmetic  95.6 us (10%)
  blocking collectives  61.7 us (7%)
  starting transfers between devices  26.7 us (3%)
  between operations  18.2 us (2%)
    reduce_scatter x1, waiting for transfers between devices, body(): lax.psum_scatter(sum_w_down, 'wide', scatter_dimension=0, tiled=True)  100 us
    reduce_scatter x1, waiting for transfers between devices, body(): lax.psum_scatter(sum_w_up, 'wide', scatter_dimension=0, tiled=True)  100 us
    reduce_scatter x1, waiting for transfers between devices, body(): lax.psum_scatter(sum_w_qkv, 'wide', scatter_dimension=0, tiled=True)  79 us
    psum x1, waiting for transfers between devices, body(): lax.psum((share_ada, share_qkv, share_out, share_up, share_down, piece_ad...  60.2 us
    unnamed x190, local copies, waits for them, and re-layouts  58.2 us
    unnamed x8, other arithmetic  53.8 us
    reduce_scatter x1, waiting for transfers between devices, body(): lax.psum_scatter(sum_w_ada_turned, 'wide', scatter_dimension=0, tiled=True)  45.5 us
    unnamed x1, blocking collectives  26.4 us
  transfers between devices with their start and end apart: 12, of which 8 were waited for; matrix products, arithmetic and copies ran while one was open for 15% of the time, Pallas kernels for 0%

commit v1 on v0

v1 whole, which is shorter than its diff:
```python
import functools

import jax
import jax.numpy as jnp
import numpy as np
from jax import lax
from jax.experimental import pallas as pl
from jax.experimental.pallas import tpu as pltpu
from jax.sharding import PartitionSpec as P

D = 768
HEADS = 12
HEAD_DIM = 64
FF = 3072
DOCS = 2
EPS = 1e-05
LOG2E = 1.4426950408889634
BIG = 1e30
OWN = 3
WCOLS = 640
ROWS_G = 432
COLS_G = 384
MESH = pl.DeviceIdType.MESH
F32 = jnp.float32
BF16 = jnp.bfloat16
NN = (((1,), (0,)), ((), ()))
NT = (((1,), (1,)), ((), ()))
TN = (((0,), (0,)), ((), ()))
VMEM = pltpu.VMEM
ANY = pl.ANY


def dg(a, b, dims):
    return lax.dot_general(a, b, dims, preferred_element_type=F32)


def place():
    n = lax.axis_index("narrow")
    w = lax.axis_index("wide")
    return n, n // 2, lax.rem(n, 2), w // 2, lax.rem(w, 2)


def sibling(n, z, c):
    return (n, 2 * z + 1 - c)


def plane_barrier(n, z, c):
    barrier = pltpu.get_barrier_semaphore()
    me = n * 2 + c
    for step in range(1, 8):
        other = lax.rem(me + step, 8)
        pl.semaphore_signal(
            barrier, inc=1, device_id=(other // 2, 2 * z + lax.rem(other, 2)), device_id_type=MESH
        )
    pl.semaphore_wait(barrier, 7)


def remote(src, dst, send, recv, device):
    return pltpu.make_async_remote_copy(
        src_ref=src, dst_ref=dst, send_sem=send, recv_sem=recv, device_id=device, device_id_type=MESH
    )


def send_or_keep(is_self, src, dst, send, recv, device):
    @pl.when(is_self)
    def _():
        pltpu.make_async_copy(src, dst, recv).start()

    @pl.when(jnp.logical_not(is_self))
    def _():
        remote(src, dst, send, recv, device).start()


def wait_send_unless(is_self, src, dst, send, recv, device):
    @pl.when(jnp.logical_not(is_self))
    def _():
        remote(src, dst, send, recv, device).wait_send()


def wait_bytes(ref, sem):
    pltpu.make_async_copy(ref, ref, sem).wait()


def lane(shape):
    return lax.broadcasted_iota(jnp.int32, shape, len(shape) - 1)


def by8(values):
    return values.reshape(values.shape[0] // 8, 8, values.shape[1])


def flat8(values):
    return values.reshape(values.shape[0] * 8, values.shape[2])


def sum8(values):
    return jnp.sum(by8(values), axis=0)


def norm_stats(values):
    mean = jnp.mean(values, axis=-1, keepdims=True)
    centred = values - mean
    spread = jnp.mean(centred * centred, axis=-1, keepdims=True)
    inv = lax.rsqrt(spread + EPS)
    return centred * inv, inv


def halves_turn(values):
    where = lax.rem(lane(values.shape), 64) < 32
    return jnp.where(where, pltpu.roll(values, 96, 1), pltpu.roll(values, 32, 1))


def cos_sin(table):
    lanes = lane(table.shape)
    other = pltpu.roll(table, 64, 1)
    cosine = jnp.where(lanes < 64, table, other)
    sine = jnp.where(lanes < 64, other, table)
    return cosine, jnp.where(lax.rem(lanes, 64) < 32, -sine, sine)


def split3(column):
    high = column.astype(BF16).astype(F32)
    rest = column - high
    middle = rest.astype(BF16).astype(F32)
    low = (rest - middle).astype(BF16).astype(F32)
    return high, middle, low


def forward_kernel(
    docs_ref,
    tokens_ref,
    cond_ref,
    w_ada_ref,
    b_ada_ref,
    gain_ref,
    w_qkv_hbm,
    table_hbm,
    att_ref,
    all_ref,
    q_ref,
    k_ref,
    v_ref,
    pat_ref,
    own_ref,
    tab_ref,
    mine,
    gathered,
    w_qkv,
    tables,
    osend,
    oland,
    docs_mine,
    docs_other,
    load_sem,
    docs_sem,
    a_send,
    a_recv,
    f_send,
    f_recv,
    o_send,
    o_recv,
    all_sem,
):
    n, ny, nx, z, c = place()
    local = tokens_ref.shape[0]
    half = local // 2
    length = local * 4
    loads = [
        pltpu.make_async_copy(w_qkv_hbm, w_qkv, load_sem.at[0]),
        pltpu.make_async_copy(table_hbm, tables, load_sem.at[1]),
    ]
    for load in loads:
        load.start()
    docs_mine[...] = jnp.full(docs_mine.shape, docs_ref[0], jnp.int32).astype(F32)
    plane_barrier(n, z, c)
    docs_copy = remote(docs_mine, docs_other, docs_sem.at[0], docs_sem.at[1], sibling(n, z, c))
    docs_copy.start()

    two = docs_ref[0] == DOCS
    parity = lax.rem(lax.broadcasted_iota(jnp.int32, (16, 128), 0), 2)
    odd = jnp.logical_and(parity == 1, two)
    cond = cond_ref[...].astype(F32)
    cond16 = jnp.where(odd, cond[1:2, :], cond[0:1, :]).astype(BF16)
    pat_ref[...] = dg(cond16, w_ada_ref[...], NN)[:8] + b_ada_ref[...].astype(F32)

    shift = pat_ref[:, 0:D]
    amp = gain_ref[...].astype(F32) * (1.0 + pat_ref[:, D : 2 * D])

    def a_copy(my, hh):
        target = 2 * my + c
        is_self = jnp.logical_and(target == n, c == hh)
        return (
            is_self,
            mine.at[pl.ds(hh * half, half)],
            gathered.at[pl.ds(pl.multiple_of(n * local + hh * half, half), half)],
            a_send.at[my * 2 + hh],
            a_recv.at[n],
            (target, 2 * z + hh),
        )

    for hh in range(2):
        normed, _ = norm_stats(tokens_ref[hh * half : (hh + 1) * half, :].astype(F32))
        mine[hh * half : (hh + 1) * half, :] = flat8(by8(normed) * amp[None] + shift[None]).astype(
            BF16
        )
        for my in range(2):
            send_or_keep(*a_copy(my, hh))

    for load in loads:
        load.wait()
    group = 2 * ny + c
    lanes_w = lane((D, 128))

    def columns(part, j, at):
        col = part * HEADS + group * OWN + j
        block = w_qkv[:, pl.ds(pl.multiple_of((col // 2) * 128, 128), 128)].astype(F32)
        return pltpu.roll(block, lax.rem(col + at, 2) * 64, 1)

    for j in range(OWN):
        own_ref[:, j * 128 : (j + 1) * 128] = jnp.where(
            lanes_w < 64, columns(1, j, 0), columns(2, j, 1)
        ).astype(BF16)
    own_ref[:, 384:512] = jnp.where(lanes_w < 64, columns(0, 0, 0), columns(0, 1, 1)).astype(BF16)
    own_ref[:, 512:640] = jnp.where(lanes_w < 64, columns(0, 2, 0), 0.0).astype(BF16)

    docs_copy.wait()
    docs_heads = jnp.where(nx == c, docs_mine[...], docs_other[...])
    tab_ref[...] = jnp.where(docs_heads[0:1] == DOCS, tables[1], tables[0])

    lanes = lane((8, 128))
    odd8 = jnp.logical_and(parity[:8] == 1, docs_heads == DOCS)
    tail_q = jnp.where(lanes == 64, jnp.where(odd8, 0.0, 1.0), 0.0)
    tail_q = jnp.where(lanes == 65, jnp.where(odd8, 1.0, 0.0), tail_q)
    tail_k = jnp.where(lanes == 64, jnp.where(odd8, -BIG, 0.0), 0.0)
    tail_k = jnp.where(lanes == 65, jnp.where(odd8, 0.0, -BIG), tail_k)
    tail_k = jnp.where(jnp.logical_and(lanes >= 66, lanes < 69), 1.0, tail_k)

    def with_tail(values, tail):
        shaped = by8(values)
        return flat8(jnp.where(lane(shaped.shape) < 64, shaped, tail[None])).astype(BF16)

    def project(source):
        def step(i, carry):
            rows = pl.ds(pl.multiple_of(source * local + i * half, half), half)
            wide = dg(gathered[rows, :], own_ref[...], NN)
            cosine, sine = cos_sin(tab_ref[rows, :])

            def rot(values):
                return values * cosine + halves_turn(values) * sine

            for j in range(OWN):
                block = wide[:, j * 128 : (j + 1) * 128]
                k_ref[j, rows, :] = with_tail(rot(block), tail_k)
                v_ref[j, rows, :] = jnp.where(
                    lane(block.shape) < 64, pltpu.roll(block, 64, 1), 1.0
                ).astype(BF16)
            first = rot(wide[:, 384:512]) * HEAD_DIM**-0.5
            q_ref[0, rows, :] = with_tail(first, tail_q)
            q_ref[1, rows, :] = with_tail(pltpu.roll(first, 64, 1), tail_q)
            q_ref[2, rows, :] = with_tail(rot(wide[:, 512:640]) * HEAD_DIM**-0.5, tail_q)
            return carry

        lax.fori_loop(0, 2, step, 0)

    def part(source, hh):
        return gathered.at[pl.ds(pl.multiple_of(source * local + hh * half, half), half)]

    def forward(source):
        wait_bytes(part(source, c), a_recv.at[source])
        remote(
            part(source, c), part(source, c), f_send.at[source], f_recv.at[source], sibling(n, z, c)
        ).start()

    sources = [n, lax.rem(n + 2, 4), n + 1 - 2 * nx, lax.rem(n + 3 - 2 * nx, 4)]

    def arrive(source):
        wait_bytes(part(source, 1 - c), f_recv.at[source])
        project(source)

    forward(sources[0])
    forward(sources[1])
    arrive(sources[0])
    forward(sources[2])
    arrive(sources[1])
    forward(sources[3])
    arrive(sources[2])
    arrive(sources[3])
    keep = pltpu.make_async_copy(gathered, all_ref, all_sem)
    keep.start()

    def o_copy(j, quarter):
        is_self = jnp.logical_and(quarter == n, nx == c)
        return (
            is_self,
            osend.at[j, quarter],
            oland.at[group * OWN + j],
            o_send.at[j, quarter],
            o_recv.at[group * OWN + j],
            (quarter, 2 * z + nx),
        )

    def attend(index, carry):
        j = index // 4
        quarter = lax.rem(n + 3 - lax.rem(index, 4), 4)
        start = quarter * local
        scores = []
        for u in range(2):
            rows = pl.ds(pl.multiple_of(start + u * half, half), half)
            scores.append(dg(q_ref[j, rows, :], k_ref[j], NT))
        outs = []
        for u in range(2):
            rows = pl.ds(pl.multiple_of(start + u * half, half), half)
            top = jnp.max(scores[u], axis=1, keepdims=True)
            weights = jnp.exp2((scores[u] - top) * LOG2E)
            total = jnp.sum(weights, axis=1, keepdims=True)
            mixed = dg((weights * (1.0 / total)).astype(BF16), v_ref[j], NN)
            high, middle, low = split3(top + jnp.log(total))
            query = q_ref[j, rows, :].astype(F32)
            lanes_q = lane(query.shape)
            query = jnp.where(lanes_q == 66, -high, query)
            query = jnp.where(lanes_q == 67, -middle, query)
            q_ref[j, rows, :] = jnp.where(lanes_q == 68, -low, query).astype(BF16)
            outs.append(mixed)
        osend[j, quarter] = jnp.where(
            lane(outs[0].shape) < 64, outs[0], pltpu.roll(outs[1], 64, 1)
        ).astype(BF16)
        send_or_keep(*o_copy(j, quarter))
        return carry

    lax.fori_loop(0, OWN * 4, attend, 0)

    for head in range(HEADS):
        wait_bytes(oland.at[head], o_recv.at[head])
    for pair in range(HEADS // 2):
        even = oland[2 * pair].astype(F32)
        odd_head = oland[2 * pair + 1].astype(F32)
        low = lane(even.shape) < 64
        cols = slice(pair * 128, (pair + 1) * 128)
        att_ref[0:half, cols] = jnp.where(low, even, pltpu.roll(odd_head, 64, 1)).astype(BF16)
        att_ref[half:local, cols] = jnp.where(low, pltpu.roll(even, 64, 1), odd_head).astype(BF16)

    for hh in range(2):
        for my in range(2):
            wait_send_unless(*a_copy(my, hh))
    for source in range(4):
        remote(
            part(source, c), part(source, c), f_send.at[source], f_recv.at[source], sibling(n, z, c)
        ).wait_send()

    def drain(index, carry):
        wait_send_unless(*o_copy(index // 4, lax.rem(index, 4)))
        return carry

    lax.fori_loop(0, OWN * 4, drain, 0)
    keep.wait()


def vm():
    return pl.BlockSpec(memory_space=VMEM)


def hbm():
    return pl.BlockSpec(memory_space=ANY)


def smem():
    return pl.BlockSpec(memory_space=pltpu.SMEM)


def params(collective_id, limit=56):
    return pltpu.CompilerParams(
        collective_id=collective_id, has_side_effects=True, vmem_limit_bytes=limit * 2**20
    )


def dma(*shape):
    return pltpu.SemaphoreType.DMA(shape)


def call_forward(docs, tokens, cond, w_ada, b_ada, gain, w_qkv, table):
    local = tokens.shape[0]
    length = 4 * local
    half = local // 2
    sds = jax.ShapeDtypeStruct
    return pl.pallas_call(
        forward_kernel,
        out_shape=(
            sds((local, D), BF16),
            sds((length, D), BF16),
            sds((OWN, length, 128), BF16),
            sds((OWN, length, 128), BF16),
            sds((OWN, length, 128), BF16),
            sds((8, 6 * D), F32),
            sds((D, WCOLS), BF16),
            sds((length, 128), F32),
        ),
        in_specs=[smem(), vm(), vm(), vm(), vm(), vm(), hbm(), hbm()],
        out_specs=(vm(), hbm(), vm(), vm(), vm(), vm(), vm(), vm()),
        scratch_shapes=[
            VMEM((local, D), BF16),
            VMEM((length, D), BF16),
            VMEM((D, 3 * D), BF16),
            VMEM((2, length, 128), F32),
            VMEM((OWN, 4, half, 128), BF16),
            VMEM((HEADS, half, 128), BF16),
            VMEM((8, 128), F32),
            VMEM((8, 128), F32),
            dma(2),
            dma(2),
            dma(4),
            dma(4),
            dma(4),
            dma(4),
            dma(OWN, 4),
            dma(HEADS),
            pltpu.SemaphoreType.DMA,
        ],
        compiler_params=params(0),
        cost_estimate=pl.CostEstimate(flops=10**10, bytes_accessed=2 * 10**7, transcendentals=10**7),
    )(docs, tokens, cond, w_ada, b_ada, gain, w_qkv, table)


def rotary_table(length):
    freq = 10000.0 ** (-np.arange(HEAD_DIM // 2, dtype=np.float64) * 2.0 / HEAD_DIM)
    tables = []
    for docs in (1, DOCS):
        angle = (np.arange(length) // docs)[:, None] * freq[None, :]
        cosine, sine = np.cos(angle), np.sin(angle)
        tables.append(np.concatenate([cosine, cosine, sine, sine], axis=1))
    return np.stack(tables).astype(np.float32)


SMALL = 4 * D + FF + D


def middle_kernel(
    tokens_ref,
    cot_ref,
    att_ref,
    pat_ref,
    gain_ref,
    w_out_ref,
    w_up_ref,
    b_up_ref,
    w_down_ref,
    b_down_ref,
    out_ref,
    gmid_ref,
    g_ref,
    small_ref,
    do_ref,
    second_ref,
    active_ref,
    slope_ref,
    down_ref,
    gsecond_ref,
    middle_ref,
    branch_ref,
    lhs_t,
    gdown_ref,
    dsend,
    dland,
    d_send,
    d_recv,
):
    n, ny, nx, z, c = place()
    group = 2 * ny + c
    local = tokens_ref.shape[0]
    half = local // 2
    tile = 768
    plane_barrier(n, z, c)

    def piece(index):
        return pat_ref[:, index * D : (index + 1) * D]

    def spread(values, pattern):
        return flat8(by8(values) * pattern[None])

    branch_ref[...] = dg(att_ref[...], w_out_ref[...], NN)
    middle = tokens_ref[...].astype(F32) + spread(branch_ref[...], piece(2))
    middle_ref[...] = middle
    amp = gain_ref[...].astype(F32) * (1.0 + piece(4))
    normed, _ = norm_stats(middle)
    second = flat8(by8(normed) * amp[None] + piece(3)[None]).astype(BF16)
    second_ref[...] = second
    down_ref[...] = jnp.broadcast_to(b_down_ref[...].astype(F32), down_ref.shape)

    def up(t, carry):
        cols = pl.ds(pl.multiple_of(t * tile, tile), tile)
        hidden = dg(second_ref[...], w_up_ref[:, cols], NN) + b_up_ref[:, cols].astype(F32)
        square = hidden * hidden
        bend = jnp.tanh(0.7978845608028654 * hidden * (1.0 + 0.044715 * square))
        part = 0.5 * (1.0 + bend)
        active_ref[:, cols] = (hidden * part).astype(BF16)
        slope_ref[:, cols] = part + (0.5 * 0.7978845608028654) * hidden * (1.0 - bend * bend) * (
            1.0 + 3.0 * 0.044715 * square
        )
        down_ref[...] += dg(active_ref[:, cols], w_down_ref[cols, :], NN)
        return carry

    lax.fori_loop(0, FF // tile, up, 0)

    cot = cot_ref[...].astype(F32)
    down = down_ref[...]
    out_ref[...] = (middle_ref[...] + spread(down, piece(5))).astype(BF16)
    small_ref[:, 3 * D : 4 * D] = sum8(cot * down)
    gdown = spread(cot, piece(5)).astype(BF16)
    gdown_ref[...] = gdown
    small_ref[:, 4 * D + FF :] = sum8(gdown.astype(F32))
    lhs_t[0] = second_ref[...].T
    lhs_t[1] = gdown.T
    gsecond_ref[...] = jnp.zeros_like(gsecond_ref)

    def back(t, carry):
        cols = pl.ds(pl.multiple_of(t * tile, tile), tile)
        ghidden = dg(gdown_ref[...], w_down_ref[cols, :], NT) * slope_ref[:, cols]
        low = ghidden.astype(BF16)
        small_ref[:, pl.ds(pl.multiple_of(4 * D + t * tile, tile), tile)] = sum8(low.astype(F32))
        gsecond_ref[...] += dg(low, w_up_ref[:, cols], NT)
        gup = dg(lhs_t[0], low, NN).astype(BF16)
        for hh in range(2):
            g_ref[:, t, hh * 96 : (hh + 1) * 96, :] = gup[:, hh * 384 : (hh + 1) * 384].reshape(
                8, 96, 384
            )
        gdw = dg(lhs_t[1], active_ref[:, cols], NN).astype(BF16)
        for hh in range(2):
            g_ref[2 * t + hh, :, 192:384, :] = gdw[:, hh * 384 : (hh + 1) * 384].reshape(4, 192, 384)
        return carry

    lax.fori_loop(0, FF // tile, back, 0)

    normed, inv = norm_stats(middle_ref[...])
    gsecond = gsecond_ref[...]
    small_ref[:, D : 2 * D] = sum8(gsecond)
    small_ref[:, 2 * D : 3 * D] = sum8(gsecond * normed)
    amp = gain_ref[...].astype(F32) * (1.0 + piece(4))
    grad = spread(gsecond, amp)
    mean = jnp.mean(grad, axis=-1, keepdims=True)
    along = jnp.mean(grad * normed, axis=-1, keepdims=True)
    gmid = cot_ref[...].astype(F32) + (grad - mean - normed * along) * inv
    gmid_ref[...] = gmid
    small_ref[:, 0:D] = sum8(gmid * branch_ref[...])
    gbranch = spread(gmid, piece(2)).astype(BF16)
    gatt = dg(gbranch, w_out_ref[...], NT)

    def d_copy(quarter_x, pick_y, cc, j):
        target = 2 * pick_y + c
        head = (2 * pick_y + cc) * OWN + j
        is_self = jnp.logical_and(target == n, c == cc)
        return (
            is_self,
            dsend.at[head],
            dland.at[j, n],
            d_send.at[head],
            d_recv.at[j, n],
            (target, 2 * z + cc),
        )

    copies = []
    for pair in range(HEADS // 2):
        top = gatt[0:half, pair * 128 : (pair + 1) * 128]
        bottom = gatt[half:local, pair * 128 : (pair + 1) * 128]
        low = lane(top.shape) < 64
        dsend[2 * pair] = jnp.where(low, top, pltpu.roll(bottom, 64, 1)).astype(BF16)
        dsend[2 * pair + 1] = jnp.where(low, pltpu.roll(top, 64, 1), bottom).astype(BF16)
    for head in range(HEADS):
        copies.append(d_copy(None, head // OWN // 2, (head // OWN) % 2, head % OWN))
        send_or_keep(*copies[-1])

    for hh in range(2):
        gout = dg(att_ref[...], gbranch[:, hh * 384 : (hh + 1) * 384], TN).astype(BF16)
        shaped = gout.reshape(8, 2, 48, 384)
        for rh in range(2):
            g_ref[:, rh * 2 + hh, 384:432, :] = shaped[:, rh]

    for j in range(OWN):
        for quarter in range(4):
            wait_bytes(dland.at[j, quarter], d_recv.at[j, quarter])
    do_ref[...] = dland[...]
    for copy in copies:
        wait_send_unless(*copy)


def call_middle(tokens, cot, att, pat, gain, w_out, w_up, b_up, w_down, b_down):
    local = tokens.shape[0]
    half = local // 2
    sds = jax.ShapeDtypeStruct
    return pl.pallas_call(
        middle_kernel,
        out_shape=(
            sds((local, D), BF16),
            sds((local, D), F32),
            sds((8, 4, ROWS_G, COLS_G), BF16),
            sds((8, SMALL), F32),
            sds((OWN, 4, half, 128), BF16),
        ),
        in_specs=[vm()] * 10,
        out_specs=(vm(),) * 5,
        scratch_shapes=[
            VMEM((local, D), BF16),
            VMEM((local, FF), BF16),
            VMEM((local, FF), F32),
            VMEM((local, D), F32),
            VMEM((local, D), F32),
            VMEM((local, D), F32),
            VMEM((local, D), F32),
            VMEM((2, D, local), BF16),
            VMEM((local, D), BF16),
            VMEM((HEADS, half, 128), BF16),
            VMEM((OWN, 4, half, 128), BF16),
            dma(HEADS),
            dma(OWN, 4),
        ],
        compiler_params=params(1, 60),
        cost_estimate=pl.CostEstimate(flops=2 * 10**10, bytes_accessed=3 * 10**7, transcendentals=10**7),
    )(tokens, cot, att, pat, gain, w_out, w_up, b_up, w_down, b_down)


def backward_kernel(
    tokens_ref,
    pat_ref,
    gain_ref,
    gmid_ref,
    do_ref,
    q_ref,
    k_ref,
    v_ref,
    all_ref,
    own_ref,
    tab_ref,
    gtok_ref,
    gq_ref,
    small_ref,
    packed,
    acc_k,
    acc_v,
    acc_w,
    kept,
    csend,
    cland,
    rsend,
    rland,
    c_send,
    c_recv,
    r_send,
    r_recv,
):
    n, ny, nx, z, c = place()
    local = tokens_ref.shape[0]
    half = local // 2
    length = 4 * local
    plane_barrier(n, z, c)
    lanes = lane((local, 128))

    def turned(values, rows):
        cosine, sine = cos_sin(tab_ref[rows, :])
        return values * cosine - halves_turn(values) * sine

    def rounded(values):
        return values.astype(BF16).astype(F32)

    for j in range(OWN):
        acc_k[...] = jnp.zeros_like(acc_k)
        acc_v[...] = jnp.zeros_like(acc_v)

        def quarter_step(i, carry):
            rows = pl.ds(pl.multiple_of(i * local, local), local)
            block = do_ref[j, i].astype(F32)
            grad = jnp.concatenate([block, pltpu.roll(block, 64, 1)], axis=0)
            grad = jnp.where(lanes < 64, grad, 0.0).astype(BF16)
            query = q_ref[j, rows, :]
            probs = jnp.exp2(dg(query, k_ref[j], NT) * LOG2E)
            gprobs = probs * dg(grad, v_ref[j], NT)
            scores = (gprobs - probs * jnp.sum(gprobs, axis=1, keepdims=True)).astype(BF16)
            probs = probs.astype(BF16)
            gquery = rounded(dg(scores, k_ref[j], NN) * HEAD_DIM**-0.5)
            at = 384 + 64 * j
            packed[rows, at : at + 64] = turned(gquery, rows)[:, :64].astype(BF16)
            acc_v[...] += dg(grad.T[:64], probs, NN)
            acc_k[...] += dg(query.T[:64], scores, NN)
            return carry

        lax.fori_loop(0, 4, quarter_step, 0)

        def finish(i, carry):
            rows = pl.ds(pl.multiple_of(i * local, local), local)
            both = jnp.concatenate([acc_k[:, rows], acc_v[:, rows]], axis=0).T
            both = rounded(both)
            packed[rows, j * 128 : (j + 1) * 128] = jnp.where(
                lanes < 64, turned(both, rows), both
            ).astype(BF16)
            return carry

        lax.fori_loop(0, 4, finish, 0)
    packed[:, 576:640] = jnp.zeros((length, 64), BF16)

    def rows_of(quarter, hh):
        return pl.ds(pl.multiple_of(quarter * local + hh * half, half), half)

    def c_copy(quarter):
        return remote(
            csend.at[quarter], cland.at[quarter], c_send.at[quarter], c_recv.at[quarter],
            sibling(n, z, c),
        )

    def r_copy(quarter):
        is_self = jnp.logical_and(quarter == n, nx == c)
        return (
            is_self,
            rsend.at[quarter],
            rland.at[ny, pl.ds(pl.multiple_of(c * half, half), half)],
            r_send.at[quarter],
            r_recv.at[ny, c],
            (quarter, 2 * z + nx),
        )

    def order(i):
        return lax.rem(n + 3 - i, 4)

    def give(i, carry):
        quarter = order(i)
        csend[quarter] = dg(packed[rows_of(quarter, 1 - c), :], own_ref[...], NT).astype(BF16)
        c_copy(quarter).start()
        return carry

    lax.fori_loop(0, 4, give, 0)

    def keep(i, carry):
        quarter = order(i)
        kept[quarter] = dg(packed[rows_of(quarter, c), :], own_ref[...], NT)
        return carry

    lax.fori_loop(0, 4, keep, 0)

    def add(i, carry):
        quarter = order(i)
        wait_bytes(cland.at[quarter], c_recv.at[quarter])
        rsend[quarter] = (kept[quarter] + cland[quarter].astype(F32)).astype(BF16)
        send_or_keep(*r_copy(quarter))
        return carry

    lax.fori_loop(0, 4, add, 0)

    acc_w[...] = jnp.zeros_like(acc_w)

    def weights(i, carry):
        rows = pl.ds(pl.multiple_of(i * local, local), local)
        acc_w[...] += dg(all_ref[rows, :], packed[rows, :], TN)
        return carry

    lax.fori_loop(0, 4, weights, 0)
    gq_ref[...] = acc_w[...].astype(BF16).reshape(gq_ref.shape)

    normed, inv = norm_stats(tokens_ref[...].astype(F32))
    for y in range(2):
        for hh in range(2):
            wait_bytes(rland.at[y, pl.ds(hh * half, half)], r_recv.at[y, hh])
    gfirst = rland[0].astype(F32) + rland[1].astype(F32)
    small_ref[:, 0:D] = sum8(gfirst)
    small_ref[:, D : 2 * D] = sum8(gfirst * normed)
    amp = gain_ref[...].astype(F32) * (1.0 + pat_ref[:, D : 2 * D])
    grad = flat8(by8(gfirst) * amp[None])
    mean = jnp.mean(grad, axis=-1, keepdims=True)
    along = jnp.mean(grad * normed, axis=-1, keepdims=True)
    gtok_ref[...] = gmid_ref[...] + (grad - mean - normed * along) * inv

    def drain(quarter, carry):
        c_copy(quarter).wait_send()
        wait_send_unless(*r_copy(quarter))
        return carry

    lax.fori_loop(0, 4, drain, 0)


def call_backward(tokens, pat, gain, gmid, do, q, k, v, everything, own, tab):
    local = tokens.shape[0]
    half = local // 2
    length = 4 * local
    sds = jax.ShapeDtypeStruct
    return pl.pallas_call(
        backward_kernel,
        out_shape=(
            sds((local, D), F32),
            sds((8, 96, WCOLS), BF16),
            sds((8, 2 * D), F32),
        ),
        in_specs=[vm()] * 11,
        out_specs=(vm(),) * 3,
        scratch_shapes=[
            VMEM((length, WCOLS), BF16),
            VMEM((64, length), F32),
            VMEM((64, length), F32),
            VMEM((D, WCOLS), F32),
            VMEM((4, half, D), F32),
            VMEM((4, half, D), BF16),
            VMEM((4, half, D), BF16),
            VMEM((4, half, D), BF16),
            VMEM((2, local, D), BF16),
            dma(4),
            dma(4),
            dma(4),
            dma(2, 2),
        ],
        compiler_params=params(2, 60),
        cost_estimate=pl.CostEstimate(flops=2 * 10**10, bytes_accessed=3 * 10**7, transcendentals=10**7),
    )(tokens, pat, gain, gmid, do, q, k, v, everything, own, tab)


def plain_sums(g, gq, own_ids):
    n, z, c = own_ids
    up = g[:, :, :192].reshape(8, 4, 2, 96, 384).transpose(0, 3, 1, 2, 4).reshape(D, FF)
    down = g[:, :, 192:384].reshape(8, D, 384).transpose(0, 2, 1).reshape(FF, D)
    out = g[:, :, 384:].reshape(8, 2, 2, 48, 384).transpose(0, 1, 3, 2, 4).reshape(D, D)
    flat = gq.reshape(D, WCOLS)
    pieces = [flat[:, 384:576]]
    pieces.append(jnp.concatenate([flat[:, j * 128 : j * 128 + 64] for j in range(OWN)], axis=1))
    pieces.append(jnp.concatenate([flat[:, j * 128 + 64 : j * 128 + 128] for j in range(OWN)], axis=1))
    group = 2 * (n // 2) + c
    whole = jnp.zeros((D, 3, 4, OWN * HEAD_DIM), F32)
    for part in range(3):
        whole = lax.dynamic_update_slice(
            whole, pieces[part].astype(F32)[:, None, None, :], (0, part, group, 0)
        )
    whole = whole.reshape(D, 3 * D)

    def total(values):
        share = lax.psum_scatter(values.astype(F32), "wide", scatter_dimension=0, tiled=True)
        return lax.psum(share, "narrow")

    return total(whole), total(out), total(up), total(down)


def body(
    tokens,
    condition,
    docs_per_row,
    w_ada,
    b_ada,
    gain_one,
    w_qkv,
    w_out,
    gain_two,
    w_up,
    b_up,
    w_down,
    b_down,
    cotangent,
):
    local = tokens.shape[1]
    x = tokens.reshape(local, D)
    cot = cotangent.reshape(local, D)
    cond = condition.reshape(DOCS, -1)
    table = jnp.asarray(rotary_table(4 * local))

    def line(vector):
        return vector.reshape(1, -1)

    att, everything, q, k, v, pat, own, tab = call_forward(
        docs_per_row, x, cond, w_ada, line(b_ada), line(gain_one), w_qkv, table
    )
    output, gmid, g, small_two, do = call_middle(
        x, cot, att, pat, line(gain_two), w_out, w_up, line(b_up), w_down, line(b_down)
    )
    gtok, gq, small_one = call_backward(
        x, pat, line(gain_one), gmid, do, q, k, v, everything, own, tab
    )
    n, w = lax.axis_index("narrow"), lax.axis_index("wide")
    sum_qkv, sum_out, sum_up, sum_down = plain_sums(g, gq, (n, w // 2, w % 2))

    small = jnp.concatenate([small_one, small_two], axis=1).reshape(4, 2, -1).sum(0)
    small = lax.psum(small, "narrow")
    shift_one, raw_one, gate_one, shift_two, raw_two, gate_two = jnp.split(small[:, : 6 * D], 6, axis=1)
    scales = pat[:2].reshape(2, 6, D)
    sum_gain_one = jnp.sum(raw_one * (1.0 + scales[:, 1]), axis=0)
    sum_gain_two = jnp.sum(raw_two * (1.0 + scales[:, 4]), axis=0)
    grads = jnp.concatenate(
        [
            shift_one,
            raw_one * gain_one.astype(F32),
            gate_one,
            shift_two,
            raw_two * gain_two.astype(F32),
            gate_two,
        ],
        axis=1,
    )
    two = docs_per_row[0] == DOCS
    grad_mods = jnp.stack(
        [jnp.where(two, grads[0], grads[0] + grads[1]), jnp.where(two, grads[1], 0.0)]
    )
    high = lax.Precision.HIGHEST
    grad_condition = jnp.einsum("sm,cm->sc", grad_mods, w_ada.astype(F32), precision=high)[None]
    part_ada = jnp.einsum("sm,sc->mc", grad_mods, cond.astype(F32), precision=high)

    def share(values):
        return lax.psum_scatter(values, "wide", scatter_dimension=0, tiled=True)

    sum_b_up = jnp.sum(small[:, 6 * D : 6 * D + FF], axis=0)
    sum_b_down = jnp.sum(small[:, 6 * D + FF :], axis=0)
    return (
        output[None],
        gtok[None],
        grad_condition,
        share(part_ada).T,
        share(jnp.sum(grad_mods, axis=0)),
        share(sum_gain_one),
        sum_qkv,
        sum_out,
        share(sum_gain_two),
        sum_up,
        share(sum_b_up),
        sum_down,
        share(sum_b_down),
    )


def solution(mesh):
    in_specs = (
        P("wide", "narrow", None),
        P("wide", None, None),
        P("wide"),
        P(),
        P(),
        P(),
        P(),
        P(),
        P(),
        P(),
        P(),
        P(),
        P(),
        P("wide", "narrow", None),
    )
    out_specs = (
        P("wide", "narrow", None),
        P("wide", "narrow", None),
        P("wide", None, None),
        P(None, "wide"),
        P("wide"),
        P("wide"),
        P("wide", None),
        P("wide", None),
        P("wide"),
        P("wide", None),
        P("wide"),
        P("wide", None),
        P("wide"),
    )
    return jax.shard_map(body, mesh=mesh, in_specs=in_specs, out_specs=out_specs, check_vma=False)
```

time: 924 us -> 706 us (0.76)
  Pallas kernels: 0 us -> 176 us
  matrix products: 119 us -> 6.33 us
  local copies, waits for them, and re-layouts: 191 us -> 86.4 us
  other arithmetic: 95.6 us -> 15.8 us
  waiting for transfers between devices: 395 us -> 362 us
  blocking collectives: 61.7 us -> 30.9 us
  starting transfers between devices: 26.7 us -> 0.46 us
    pallas_call x0 -> x3, Pallas kernels: none -> 176 us  [the longest x1 69.7 us: call_backward(): pl.pallas_call(backward_kernel, out_shape=(sds((local, D), F32), sds((8,...]
    dot_general x31 -> x2, matrix products: 119 us -> 6.33 us  [the longest x1 3.43 us: body(): jnp.einsum('sm,sc->mc', grad_mods, cond.astype(F32), precision=high)]
    reduce_scatter x5 -> x4, waiting for transfers between devices: 325 us -> 235 us  [the longest x3 235 us: total(): lax.psum_scatter(values.astype(F32), 'wide', scatter_dimension=0, tiled=T...]
    unnamed x8 -> x2, other arithmetic: 53.8 us -> 1.4 us
    psum x1, waiting for transfers between devices: 60.2 us -> 102 us  [body(): small = lax.psum(small, 'narrow')]
    while x51 -> x0, local copies, waits for them, and re-layouts: 30.4 us -> none  [the longest x4 17 us: attend(): mixed, logsum = lax.map(one_block, pieces)]
    unnamed x190 -> x52, local copies, waits for them, and re-layouts: 58.2 us -> 29.2 us
    cond x13 -> x0, local copies, waits for them, and re-layouts: 26.5 us -> none
  transfers between devices with their start and end apart: 12 -> 6, of which waited for: 8 -> 5; matrix products, arithmetic and copies ran while one was open for 15% -> 10% of each run, Pallas kernels for 0% -> 0%
where the time goes in v1:
time: 706 us; the launch traced here: 695 us
  waiting for transfers between devices  362 us (51%)
  Pallas kernels  176 us (25%)
  local copies, waits for them, and re-layouts  86.4 us (12%)
  blocking collectives  30.9 us (4%)
  between operations  17.2 us (2%)
  other arithmetic  15.8 us (2%)
    reduce_scatter x3, waiting for transfers between devices, total(): lax.psum_scatter(values.astype(F32), 'wide', scatter_dimension=0, tiled=T...  235 us
    psum x1, waiting for transfers between devices, body(): small = lax.psum(small, 'narrow')  102 us
    pallas_call x1, Pallas kernels, call_backward(): pl.pallas_call(backward_kernel, out_shape=(sds((local, D), F32), sds((8,...  69.7 us
    pallas_call x1, Pallas kernels, call_forward(): pl.pallas_call(forward_kernel, out_shape=(sds((local, D), BF16), sds((len...  59.3 us
    pallas_call x1, Pallas kernels, call_middle(): pl.pallas_call(middle_kernel, out_shape=(sds((local, D), BF16), sds((loca...  46.6 us
    convert_element_type x4, local copies, waits for them, and re-layouts, total(): values.astype(F32)  35 us
    unnamed x1, blocking collectives  30.9 us
    unnamed x52, local copies, waits for them, and re-layouts  29.2 us
  transfers between devices with their start and end apart: 6, of which 5 were waited for; matrix products, arithmetic and copies ran while one was open for 10% of the time, Pallas kernels for 0%

profile of v1, /device:TPU:0, one launch (start us, length us, event | category | flops | bytes accessed | tf_op | source)
XLA Modules:
  0.0 695.2 jit_solution(1688838428205268971)
XLA Ops:
  7.9 1.3 reshape.179.b_ada_ref
  9.2 1.3 reshape.180.gain_ref
  11.7 1.3 reshape.182.b_up_ref
  14.3 59.3 %shard_map.246 = (bf16[512,768]{1,0:T(8,128)(2,1)}, bf16[2048,768]{1,0:T(8,128)(2,1)}, bf16[3,2048,128]{2,1,0:T(8,128)(2,1)}, bf16[3,2048,128]{2,1,0:T(8,128)(2,...) custom-call(s32[1]{0:T(128)S(6)} %copy.88.docs_ref, ...), custom_call_target="tpu_custom_call" | custom-call | flops 10000000000 | bytes 20000000 | tf_op jit(solution)/shard_map/pallas_call | solution.py:385
  73.6 46.6 %shard_map.247 = (bf16[512,768]{1,0:T(8,128)(2,1)}, f32[512,768]{1,0:T(8,128)}, bf16[8,4,432,384]{3,2,1,0:T(8,128)(2,1)}, f32[8,6912]{1,0:T(8,128)}, bf16[3,4,256,128]{3,2,1,0:T(8,128)(2,1)}) custom-call(bf16[512,768]{1,0:T(8,128)(2,1)} %bitcast.72, bf16[512,768]{1,0:T(8,128)(2,1)} %bitcast.70, bf16[512,768]{1,0:T(8,128)(2,1)} %get-tuple-element.29.att_ref, ...), custom_call_target="tpu_custom_call" | custom-call | flops 20000000000 | bytes 30000000 | tf_op jit(solution)/shard_map/pallas_call | solution.py:588
  120.2 69.7 %shard_map.248 = (f32[512,768]{1,0:T(8,128)}, bf16[8,96,640]{2,1,0:T(8,128)(2,1)}, f32[8,1536]{1,0:T(8,128)}) custom-call(bf16[512,768]{1,0:T(8,128)(2,1)} %bitcast.73, f32[8,4608]{1,0:T(8,128)} %get-tuple-element.30.pat_ref, bf16[1,768]{1,0:T(2,128)(2,1)} %reshape.180.gain_ref, f32[512,768]{1,0:T(8,128)} %get-tuple-element.32.gmid_ref, ...), custom_call_target="tpu_custom_call" | custom-call | flops 20000000000 | bytes 30000000 | tf_op jit(solution)/shard_map/pallas_call | solution.py:780
  191.0 1.6 fusion.9
  193.6 3.6 broadcast_in_dim.30
  199.8 8.0 %copy.62 = f32[768,2304]{1,0:T(8,128)} copy(f32[768,2304]{0,1:T(8,128)} %bitcast.18) | data formatting | bytes 14155776
  207.9 1.4 slice.72
  210.8 1.6 copy.72
  212.4 7.1 %fusion.8 = (bf16[8,4,192,384]{3,2,1,0:T(8,128)(2,1)}, bf16[8,4,192,384]{3,2,1,0:T(8,128)(2,1)S(1)}) fusion(bf16[8,4,432,384]{3,2,1,0:T(8,128)(2,1)} %get-tuple-element.44), kind=kLoop, calls=%fused_computation.30 | loop fusion | bytes 18874368 | tf_op jit(solution)/shard_map/slice | solution.py:812
  220.8 11.1 %copy.59 = f32[8,96,4,2,384]{4,3,2,1,0:T(2,128)} copy(f32[8,96,4,2,384]{4,1,3,2,0:T(8,128)S(1)} %convert_bitcast_fusion.1) | data formatting | bytes 18874368 | tf_op jit(solution)/shard_map/convert_element_type | solution.py:827
  231.9 12.9 %reshape.190 = f32[768,3072]{1,0:T(8,128)} reshape(f32[8,96,4,2,384]{4,3,2,1,0:T(2,128)} %copy.59) | data formatting | bytes 18874368 | tf_op jit(solution)/shard_map/convert_element_type | solution.py:827
  244.9 6.6 convert_bitcast_fusion
  251.5 9.7 %copy.60 = f32[8,384,768]{2,1,0:T(8,128)} copy(f32[8,384,768]{1,2,0:T(8,128)} %convert_bitcast_fusion) | data formatting | bytes 18874368 | tf_op jit(solution)/shard_map/convert_element_type | solution.py:827
  263.2 24.6 %reduce-scatter.16.cloned.1.call-done = f32[96,2304]{1,0:T(8,128)} async-done(((f32[768,2304]{1,0:T(8,128)}), f32[96,2304]{1,0:T(8,128)}) %reduce-scatter.16.cloned.1.call-update) | async-done | bytes 884752
  287.7 2.6 copy.63
  290.3 34.5 %reduce-scatter.10.cloned.1.call-done = f32[96,768]{1,0:T(8,128)} async-done(((f32[768,768]{1,0:T(8,128)}), f32[96,768]{1,0:T(8,128)}) %reduce-scatter.10.cloned.1.call-update) | async-done | bytes 294928 | tf_op jit(solution)/shard_map/reduce_scatter | solution.py:827
  324.7 100.9 %reduce-scatter.12.cloned.1.call-done = f32[96,3072]{1,0:T(8,128)} async-done(((f32[768,3072]{1,0:T(8,128)}), f32[96,3072]{1,0:T(8,128)}) %reduce-scatter.12.cloned.1.call-update) | async-done | bytes 1179664 | tf_op jit(solution)/shard_map/reduce_scatter | solution.py:827
  425.6 100.1 %reduce-scatter.14.cloned.1.call-done = f32[384,768]{1,0:T(8,128)} async-done(((f32[3072,768]{1,0:T(8,128)}), f32[384,768]{1,0:T(8,128)}) %reduce-scatter.14.cloned.1.call-update) | async-done | bytes 1179664 | tf_op jit(solution)/shard_map/reduce_scatter | solution.py:827
  527.0 102.3 %all-reduce.9.cloned.1.call-done = (f32[2,8448]{1,0:T(2,128)}, f32[96,2304]{0,1:T(8,128)}, f32[96,768]{1,0:T(8,128)}, f32[96,3072]{1,0:T(8,128)}, f32[384,768]{1,0:T(8,128)}) async-done(((f32[2,8448]{1,0:T(2,128)}, f32[96,2304]{0,1:T(8,128)}, f32[96,768]{1,0:T(8,128)}, f32[96,3072]{1,0:T(8,128)}, f32[384,768]{1,0:T(8,128)}), (f32[2,8448]{1,0:T(2,128)}, f32[96,2304]{0,1:T(8,128)}, f32[96,768]{1,0:T(8,128)}, ...) | async-done | bytes 3606544 | tf_op jit(solution)/shard_map/psum | solution.py:871
  632.2 1.4 slice_reduce_fusion.1
  634.9 3.4 fusion
  640.9 1.3 copy.61
  643.1 30.9 %all-reduce.5 = (f32[4608]{0:T(1024)}, f32[768]{0:T(1024)}, f32[768]{0:T(1024)}, f32[3072]{0:T(1024)}, f32[768]{0:T(1024)}) all-reduce(f32[4608]{0:T(1024)} %get-tuple-element.84, f32[768]{0:T(1024)} %get-tuple-element.72, f32[768]{0:T(1024)} %get-tuple-element.73, ...), channel_id=3, replica_groups=mesh['narrow'=4,'wide'=8] {'wide'}, use_global_device_ids=true, to_apply=%region_3.4.clone | all-reduce | flops 9984 | bytes 79872
  674.0 1.3 dynamic-slice.3
  675.2 1.3 dynamic-slice.5
  676.5 1.3 dynamic-slice.9
  677.8 1.4 dynamic-slice.1
  679.1 1.3 dynamic-slice.7
  680.5 2.9 convolution_bitcast_fusion
  (77 shorter events, 23.6 us)
Async XLA Ops:
  7.2 280.5 %reduce-scatter.16.cloned.1.call-start = ((), (), s32[]{:S(2)}) async-start(), calls=%async_computation.9 | async-start | bytes 7962624
  207.9 116.9 %reduce-scatter.10.cloned.1.call-start = ((), (), s32[]{:S(2)}) async-start(), calls=%async_computation.6 | async-start | bytes 2654208 | tf_op jit(solution)/shard_map/reduce_scatter | solution.py:827
  212.4 213.2 %reduce-scatter.12.cloned.1.call-start = ((), (), s32[]{:S(2)}) async-start(), calls=%async_computation.7 | async-start | bytes 10616832 | tf_op jit(solution)/shard_map/reduce_scatter | solution.py:827
  244.9 280.8 %reduce-scatter.14.cloned.1.call-start = ((), (), s32[]{:S(2)}) async-start(), calls=%async_computation.8 | async-start | bytes 10616832 | tf_op jit(solution)/shard_map/reduce_scatter | solution.py:827
  261.2 0.9 copy-start.6
  261.2 0.9 copy-start.9
  261.3 368.1 %all-reduce.9.cloned.1.call-start = ((), (), s32[]{:S(2)}) async-start(), calls=%async_computation.10 | async-start | bytes 7802880 | tf_op jit(solution)/shard_map/psum | solution.py:871
  262.2 264.7 %copy-start.10 = (bf16[768]{0:T(1024)(128)(2,1)S(1)}, bf16[768]{0:T(1024)(128)(2,1)}, u32[]{:S(2)}) copy-start(bf16[768]{0:T(1024)(128)(2,1)} %param.20) | copy-start | bytes 4612
  262.2 264.7 %copy-start.11 = (bf16[768]{0:T(1024)(128)(2,1)S(1)}, bf16[768]{0:T(1024)(128)(2,1)}, u32[]{:S(2)}) copy-start(bf16[768]{0:T(1024)(128)(2,1)} %param.23) | copy-start | bytes 4612
  262.2 372.7 %copy-start.12 = (bf16[1,2,128]{2,1,0:T(2,128)(2,1)S(1)}, bf16[1,2,128]{2,1,0:T(2,128)(2,1)}, u32[]{:S(2)}) copy-start(bf16[1,2,128]{2,1,0:T(2,128)(2,1)} %param.16) | copy-start | bytes 1540
  525.7 112.7 %copy-start.13 = (u32[32]{0:T(128)S(1)}, u32[32]{0:T(128)}, u32[]{:S(2)}) copy-start(u32[32]{0:T(128)} %constant.52) | copy-start | bytes 388
  525.7 157.7 %reduce-scatter.8.cloned.1.call-start = ((), (), s32[]{:S(2)}) async-start(), calls=%async_computation.5 | async-start | bytes 2654208 | tf_op jit(solution)/shard_map/reduce_scatter | solution.py:896
  629.3 11.6 %copy-start.3 = (f32[96,2304]{0,1:T(8,128)S(1)}, f32[96,2304]{0,1:T(8,128)}, u32[]{:S(2)}) copy-start(f32[96,2304]{0,1:T(8,128)} %get-tuple-element.80) | copy-start | bytes 2654212
  634.3 0.6 copy-start.7
  634.3 0.6 copy-start.8
  634.9 48.5 %copy-start.4 = (bf16[512,768]{1,0:T(8,128)(2,1)S(1)}, bf16[512,768]{1,0:T(8,128)(2,1)}, u32[]{:S(2)}) copy-start(bf16[512,768]{1,0:T(8,128)(2,1)} %get-tuple-element.31) | copy-start | bytes 2359300
  638.3 45.9 %copy-start = (f32[512,768]{1,0:T(8,128)S(1)}, f32[512,768]{1,0:T(8,128)}, u32[]{:S(2)}) copy-start(f32[512,768]{1,0:T(8,128)} %get-tuple-element.40) | copy-start | bytes 4718596
  642.2 43.9 %copy-start.2 = (f32[96,3072]{1,0:T(8,128)S(1)}, f32[96,3072]{1,0:T(8,128)}, u32[]{:S(2)}) copy-start(f32[96,3072]{1,0:T(8,128)} %get-tuple-element.118) | copy-start | bytes 3538948
  683.4 2.0 copy-start.5
  683.4 3.8 copy-start.1
Sparse Core Ops, SparseCore 0:
  208.0 79.6 reduce-scatter.15
  290.0 34.6 reduce-scatter.9
  327.0 98.5 reduce-scatter.11
  427.8 97.8 reduce-scatter.13
  530.3 98.9 all-reduce.8
  638.5 37.1 reduce-scatter.7

commit v2 on v1

--- a/solution.py
+++ b/solution.py
@@ -616,7 +616,638 @@
     )(tokens, cot, att, pat, gain, w_out, w_up, b_up, w_down, b_down)
 
 
+CUT = 288
+CHUNK = 24
+
+
+def slot_of(other, me):
+    return lax.rem(other - me + 3, 4)
+
+
 def backward_kernel(
+    docs_ref,
+    tokens_ref,
+    cond_ref,
+    w_ada_ref,
+    pat_ref,
+    gain_ref,
+    gain_two_ref,
+    gmid_ref,
+    do_ref,
+    q_ref,
+    k_ref,
+    v_ref,
+    all_ref,
+    own_ref,
+    tab_ref,
+    small_two_ref,
+    g_hbm,
+    gtok_ref,
+    blocks_ref,
+    qkv_ref,
+    packet_ref,
+    gcond_ref,
+    packed,
+    acc_k,
+    acc_v,
+    acc_w,
+    kept,
+    csend,
+    cland,
+    rsend,
+    rland,
+    small_one,
+    g_own,
+    g_sum,
+    land_a1,
+    land_b1,
+    sum_a,
+    sum_b,
+    land_a2,
+    land_b2,
+    block,
+    land_block,
+    gq,
+    land_q0,
+    sum_q,
+    land_q1,
+    done_q,
+    land_q2,
+    pack,
+    land_s1,
+    pack_sum,
+    land_s2,
+    gc_mine,
+    land_gc,
+    c_send,
+    c_recv,
+    r_send,
+    r_recv,
+    g_load,
+    g_send,
+    g_recv,
+    a1_send,
+    a1_recv,
+    b1_send,
+    b1_recv,
+    a2_send,
+    a2_recv,
+    b2_send,
+    b2_recv,
+    ag_send,
+    ag_recv,
+    q0_sem,
+    q1_send,
+    q1_recv,
+    q2_send,
+    q2_recv,
+    s1_send,
+    s1_recv,
+    s2_send,
+    s2_recv,
+    gc_send,
+    gc_recv,
+):
+    n, ny, nx, z, c = place()
+    w = 2 * z + c
+    local = tokens_ref.shape[0]
+    half = local // 2
+    length = 4 * local
+    group = 2 * ny + c
+
+    barrier = pltpu.get_barrier_semaphore()
+
+    def greet(device):
+        pl.semaphore_signal(barrier, inc=1, device_id=device, device_id_type=MESH)
+
+    me = n * 2 + c
+    for step in range(1, 8):
+        other = lax.rem(me + step, 8)
+        greet((other // 2, 2 * z + lax.rem(other, 2)))
+    for step in range(1, 4):
+        greet((n, 2 * lax.rem(z + step, 4) + c))
+    for row in range(8):
+
+        @pl.when(jnp.logical_not(jnp.logical_and(z == n, row == w)))
+        def _():
+            greet((z, row))
+
+    pl.semaphore_wait(barrier, jnp.where(z == n, 17, 18))
+
+
+    def others(base):
+        return [lax.rem(base + step, 4) for step in (1, 2, 3)]
+
+    def g_copy(chip):
+        return remote(
+            g_hbm.at[chip, 1 - c], g_sum.at[chip], g_send.at[chip], g_recv.at[chip],
+            sibling(n, z, c),
+        )
+
+    def g_fetch(chip):
+        return pltpu.make_async_copy(g_hbm.at[chip, c], g_own.at[chip % 2], g_load.at[chip % 2])
+
+    def a1_copy(other):
+        slot = slot_of(other, n)
+        return remote(
+            g_sum.at[:, other, pl.ds(0, CUT)], land_a1.at[slot], a1_send.at[slot], a1_recv.at[slot],
+            (other, w),
+        )
+
+    def b1_copy(chip):
+        slot = slot_of(chip, z)
+        return remote(
+            g_sum.at[chip, :, pl.ds(CUT, ROWS_G - CUT)], land_b1.at[slot], b1_send.at[slot],
+            b1_recv.at[slot], (n, 2 * chip + c),
+        )
+
+    def a2_copy(chip):
+        slot = slot_of(chip, z)
+        return remote(
+            sum_a.at[chip], land_a2.at[slot], a2_send.at[slot], a2_recv.at[slot], (n, 2 * chip + c)
+        )
+
+    def b2_copy(other):
+        slot = slot_of(other, n)
+        return remote(
+            sum_b.at[other], land_b2.at[slot], b2_send.at[slot], b2_recv.at[slot], (other, w)
+        )
+
+    def ag_copy(other):
+        return remote(block, land_block.at[n], ag_send.at[slot_of(other, n)], ag_recv.at[n], (other, w))
+
+    def core_start():
+        for chip in range(4):
+            g_copy(chip).start()
+        g_fetch(0).start()
+
+    def core_finish():
+        for chip in range(4):
+            if chip < 3:
+                g_fetch(chip + 1).start()
+            g_fetch(chip).wait()
+            wait_bytes(g_sum.at[chip], g_recv.at[chip])
+            for part in range(4):
+                g_sum[chip, part] = (
+                    g_sum[chip, part].astype(F32) + g_own[chip % 2, part].astype(F32)
+                ).astype(BF16)
+        for i in range(3):
+            a1_copy(others(n)[i]).start()
+            b1_copy(others(z)[i]).start()
+
+    def second_a():
+        for slot in range(3):
+            wait_bytes(land_a1.at[slot], a1_recv.at[slot])
+        for chip in range(4):
+            total = g_sum[chip, n, 0:CUT].astype(F32)
+            for slot in range(3):
+                total = total + land_a1[slot, chip].astype(F32)
+            sum_a[chip] = total.astype(BF16)
+        for chip in others(z):
+            a2_copy(chip).start()
+
+    def second_b():
+        for slot in range(3):
+            wait_bytes(land_b1.at[slot], b1_recv.at[slot])
+        for part in range(4):
+            total = g_sum[z, part, CUT:ROWS_G].astype(F32)
+            for slot in range(3):
+                total = total + land_b1[slot, part].astype(F32)
+            sum_b[part] = total.astype(BF16)
+        for other in others(n):
+            b2_copy(other).start()
+
+    def last():
+        for slot in range(3):
+            wait_bytes(land_a2.at[slot], a2_recv.at[slot])
+            wait_bytes(land_b2.at[slot], b2_recv.at[slot])
+        top = sum_a[z].astype(F32)
+        bottom = sum_b[n].astype(F32)
+        for slot in range(3):
+            top = top + land_a2[slot].astype(F32)
+            bottom = bottom + land_b2[slot].astype(F32)
+        block[0:CUT] = top.astype(BF16)
+        block[CUT:ROWS_G] = bottom.astype(BF16)
+        for other in others(n):
+            ag_copy(other).start()
+
+
+    core_start()
+    lanes = lane((local, 128))
+
+    def turned(values, rows):
+        cosine, sine = cos_sin(tab_ref[rows, :])
+        return values * cosine - halves_turn(values) * sine
+
+    def rounded(values):
+        return values.astype(BF16).astype(F32)
+
+    for j in range(OWN):
+        acc_k[...] = jnp.zeros_like(acc_k)
+        acc_v[...] = jnp.zeros_like(acc_v)
+
+        def quarter_step(i, carry):
+            if j == 0:
+                pl.when(i == 3)(core_finish)
+            rows = pl.ds(pl.multiple_of(i * local, local), local)
+            packed_grad = do_ref[j, i].astype(F32)
+            grad = jnp.concatenate([packed_grad, pltpu.roll(packed_grad, 64, 1)], axis=0)
+            grad = jnp.where(lanes < 64, grad, 0.0).astype(BF16)
+            query = q_ref[j, rows, :]
+            probs = jnp.exp2(dg(query, k_ref[j], NT) * LOG2E)
+            gprobs = probs * dg(grad, v_ref[j], NT)
+            scores = (gprobs - probs * jnp.sum(gprobs, axis=1, keepdims=True)).astype(BF16)
+            probs = probs.astype(BF16)
+            gquery = rounded(dg(scores, k_ref[j], NN) * HEAD_DIM**-0.5)
+            at = 384 + 64 * j
+            packed[rows, at : at + 64] = turned(gquery, rows)[:, :64].astype(BF16)
+            acc_v[...] += dg(grad.T[:64], probs, NN)
+            acc_k[...] += dg(query.T[:64], scores, NN)
+            return carry
+
+        lax.fori_loop(0, 4, quarter_step, 0)
+
+        def finish(i, carry):
+            rows = pl.ds(pl.multiple_of(i * local, local), local)
+            both = rounded(jnp.concatenate([acc_k[:, rows], acc_v[:, rows]], axis=0).T)
+            packed[rows, j * 128 : (j + 1) * 128] = jnp.where(
+                lanes < 64, turned(both, rows), both
+            ).astype(BF16)
+            return carry
+
+        lax.fori_loop(0, 4, finish, 0)
+    packed[:, 576:640] = jnp.zeros((length, 64), BF16)
+
+
+    def rows_of(quarter, hh):
+        return pl.ds(pl.multiple_of(quarter * local + hh * half, half), half)
+
+    def c_copy(quarter):
+        return remote(
+            csend.at[quarter], cland.at[quarter], c_send.at[quarter], c_recv.at[quarter],
+            sibling(n, z, c),
+        )
+
+    def r_copy(quarter):
+        is_self = jnp.logical_and(quarter == n, nx == c)
+        return (
+            is_self,
+            rsend.at[quarter],
+            rland.at[ny, pl.ds(pl.multiple_of(c * half, half), half)],
+            r_send.at[quarter],
+            r_recv.at[ny, c],
+            (quarter, 2 * z + nx),
+        )
+
+    def order(i):
+        return lax.rem(n + 3 - i, 4)
+
+    def give(i, carry):
+        quarter = order(i)
+        csend[quarter] = dg(packed[rows_of(quarter, 1 - c), :], own_ref[...], NT).astype(BF16)
+        c_copy(quarter).start()
+        return carry
+
+    lax.fori_loop(0, 4, give, 0)
+
+    def keep(i, carry):
+        quarter = order(i)
+        kept[quarter] = dg(packed[rows_of(quarter, c), :], own_ref[...], NT)
+        return carry
+
+    lax.fori_loop(0, 4, keep, 0)
+
+    def add(i, carry):
+        quarter = order(i)
+        wait_bytes(cland.at[quarter], c_recv.at[quarter])
+        rsend[quarter] = (kept[quarter] + cland[quarter].astype(F32)).astype(BF16)
+        send_or_keep(*r_copy(quarter))
+        return carry
+
+    lax.fori_loop(0, 4, add, 0)
+
+
+    acc_w[...] = jnp.zeros_like(acc_w)
+
+    def weights(i, carry):
+        rows = pl.ds(pl.multiple_of(i * local, local), local)
+        acc_w[...] += dg(all_ref[rows, :], packed[rows, :], TN)
+        return carry
+
+    lax.fori_loop(0, 4, weights, 0)
+    gq[...] = acc_w[...].astype(BF16).reshape(gq.shape)
+    q0_copy = remote(
+        gq.at[:, 1 - nx], land_q0, q0_sem.at[0], q0_sem.at[1], (n + 1 - 2 * nx, w)
+    )
+    q0_copy.start()
+
+    def q1_copy(chip):
+        slot = slot_of(chip, z)
+        return remote(
+            sum_q.at[chip], land_q1.at[slot], q1_send.at[slot], q1_recv.at[slot], (n, 2 * chip + c)
+        )
+
+    def q2_copy(other):
+        is_self = jnp.logical_and(other == n, nx == c)
+        return (
+            is_self, done_q, land_q2.at[group], q2_send.at[other], q2_recv.at[group],
+            (other, 2 * z + nx),
+        )
+
+    second_a()
+    second_b()
+    normed, inv = norm_stats(tokens_ref[...].astype(F32))
+    q0_copy.wait()
+    for chip in range(4):
+        sum_q[chip] = (gq[chip, nx].astype(F32) + land_q0[chip].astype(F32)).astype(BF16)
+    for chip in others(z):
+        q1_copy(chip).start()
+
+    for y in range(2):
+        for hh in range(2):
+            wait_bytes(rland.at[y, pl.ds(hh * half, half)], r_recv.at[y, hh])
+    gfirst = rland[0].astype(F32) + rland[1].astype(F32)
+    small_one[:, 0:D] = sum8(gfirst)
+    small_one[:, D : 2 * D] = sum8(gfirst * normed)
+    amp = gain_ref[...].astype(F32) * (1.0 + pat_ref[:, D : 2 * D])
+    grad = flat8(by8(gfirst) * amp[None])
+    mean = jnp.mean(grad, axis=-1, keepdims=True)
+    along = jnp.mean(grad * normed, axis=-1, keepdims=True)
+    gtok_ref[...] = gmid_ref[...] + (grad - mean - normed * along) * inv
+
+
+    two = docs_ref[0] == DOCS
+    even_rows = lax.rem(lax.broadcasted_iota(jnp.int32, (8, D), 0), 2) == 0
+
+    def even_odd(values):
+        even = jnp.sum(jnp.where(even_rows, values, 0.0), axis=0, keepdims=True)
+        return even, jnp.sum(jnp.where(even_rows, 0.0, values), axis=0, keepdims=True)
+
+    pack[...] = jnp.zeros_like(pack)
+    gc_mine[...] = jnp.zeros_like(gc_mine)
+
+    def put(chunk, row, values, s):
+        pack[chunk, row : row + 1, 0:96] = values[:, 96 * s : 96 * s + 96]
+
+    raws = [
+        small_one[:, 0:D],
+        small_one[:, D : 2 * D],
+        small_two_ref[:, 0:D],
+        small_two_ref[:, D : 2 * D],
+        small_two_ref[:, 2 * D : 3 * D],
+        small_two_ref[:, 3 * D : 4 * D],
+    ]
+    gains = {1: gain_ref, 4: gain_two_ref}
+    for piece in range(6):
+        even, odd = even_odd(raws[piece])
+        if piece in gains:
+            scale = pat_ref[:, piece * D : (piece + 1) * D]
+            gain_sum = even * (1.0 + scale[0:1]) + odd * (1.0 + scale[1:2])
+            for s in range(8):
+                put(s, 12 if piece == 1 else 13, gain_sum, s)
+            gain = gains[piece][...].astype(F32)
+            even, odd = even * gain, odd * gain
+        first_doc = jnp.where(two, even, even + odd)
+        second_doc = jnp.where(two, odd, 0.0)
+        for s in range(8):
+            at = 8 * piece + s
+            put(at // 6, at % 6, first_doc, s)
+            put(at // 6, 6 + at % 6, second_doc, s)
+        pieces = [*split3(first_doc), *split3(second_doc)]
+        stacked = jnp.concatenate([*pieces, jnp.zeros((10, D), F32)], axis=0).astype(BF16)
+        part = dg(stacked, w_ada_ref[:, piece * D : (piece + 1) * D], NT)
+        gc_mine[0:1] += part[0:1] + part[1:2] + part[2:3]
+        gc_mine[1:2] += part[3:4] + part[4:5] + part[5:6]
+    for s in range(32):
+        col = 4 * D + 96 * s
+        row = jnp.sum(small_two_ref[:, col : col + 96], axis=0, keepdims=True)
+        pack[s // 4, 14 + s % 4 : 15 + s % 4, 0:96] = row
+    for s in range(8):
+        col = 4 * D + FF + 96 * s
+        pack[s, 18:19, 0:96] = jnp.sum(small_two_ref[:, col : col + 96], axis=0, keepdims=True)
+
+    def s1_copy(other):
+        return remote(
+            pack.at[pl.ds(2 * other, 2)], land_s1.at[n], s1_send.at[slot_of(other, n)],
+            s1_recv.at[n], (other, w),
+        )
+
+    def gc_copy(other):
+        return remote(
+            gc_mine, land_gc.at[n], gc_send.at[slot_of(other, n)], gc_recv.at[n], (other, w)
+        )
+
+    for other in others(n):
+        s1_copy(other).start()
+        gc_copy(other).start()
+    land_gc[n] = gc_mine[...]
+    land_s1[n] = pack[pl.ds(2 * n, 2)]
+    for other in others(n):
+        wait_bytes(land_s1.at[other], s1_recv.at[other])
+    total = land_s1[0] + land_s1[1] + land_s1[2] + land_s1[3]
+    pack_sum[...] = total
+    cond = cond_ref[...].astype(F32)
+    for i in range(2):
+        pack_sum[i, 19:21, :] = cond
+
+    def s2_copy(index):
+        i, other = index // 4, lax.rem(index, 4)
+        is_self = jnp.logical_and(other == n, w == 2 * n + i)
+        return (
+            is_self, pack_sum.at[i], land_s2.at[w], s2_send.at[index], s2_recv.at[w],
+            (other, 2 * n + i),
+        )
+
+    for index in range(8):
+        send_or_keep(*s2_copy(index))
+
+    for slot in range(3):
+        wait_bytes(land_q1.at[slot], q1_recv.at[slot])
+    total = sum_q[z].astype(F32)
+    for slot in range(3):
+        total = total + land_q1[slot].astype(F32)
+    done_q[...] = total.astype(BF16)
+    for other in range(4):
+        send_or_keep(*q2_copy(other))
+
+    last()
+
+    for other in others(n):
+        wait_bytes(land_gc.at[other], gc_recv.at[other])
+    gcond_ref[...] = land_gc[0] + land_gc[1] + land_gc[2] + land_gc[3]
+    for row in range(8):
+        wait_bytes(land_s2.at[row], s2_recv.at[row])
+    packet_ref[...] = land_s2[...]
+    for g in range(4):
+        wait_bytes(land_q2.at[g], q2_recv.at[g])
+    qkv_ref[...] = land_q2[...]
+    land_block[n] = block[...]
+    for other in others(n):
+        wait_bytes(land_block.at[other], ag_recv.at[other])
+    blocks_ref[...] = land_block[...]
+
+
+    def drain(quarter, carry):
+        c_copy(quarter).wait_send()
+        wait_send_unless(*r_copy(quarter))
+        g_copy(quarter).wait_send()
+        wait_send_unless(*q2_copy(quarter))
+        return carry
+
+    lax.fori_loop(0, 4, drain, 0)
+    for i in range(3):
+        other, chip = others(n)[i], others(z)[i]
+        a1_copy(other).wait_send()
+        b1_copy(chip).wait_send()
+        a2_copy(chip).wait_send()
+        b2_copy(other).wait_send()
+        ag_copy(other).wait_send()
+        q1_copy(chip).wait_send()
+        s1_copy(other).wait_send()
+        gc_copy(other).wait_send()
+    for index in range(8):
+        wait_send_unless(*s2_copy(index))
+
+
+def call_backward(
+    docs, tokens, cond, w_ada, pat, gain, gain_two, gmid, do, q, k, v, everything, own, tab, small_two, g
+):
+    local = tokens.shape[0]
+    half = local // 2
+    length = 4 * local
+    sds = jax.ShapeDtypeStruct
+    rest = ROWS_G - CUT
+    return pl.pallas_call(
+        backward_kernel,
+        out_shape=(
+            sds((local, D), F32),
+            sds((4, ROWS_G, COLS_G), BF16),
+            sds((4, 96, WCOLS), BF16),
+            sds((8, CHUNK, 128), F32),
+            sds((8, 128), F32),
+        ),
+        in_specs=[smem()] + [vm()] * 15 + [hbm()],
+        out_specs=(vm(),) * 5,
+        scratch_shapes=[
+            VMEM((length, WCOLS), BF16),
+            VMEM((64, length), F32),
+            VMEM((64, length), F32),
+            VMEM((D, WCOLS), F32),
+            VMEM((4, half, D), F32),
+            VMEM((4, half, D), BF16),
+            VMEM((4, half, D), BF16),
+            VMEM((4, half, D), BF16),
+            VMEM((2, local, D), BF16),
+            VMEM((8, 2 * D), F32),
+            VMEM((2, 4, ROWS_G, COLS_G), BF16),
+            VMEM((4, 4, ROWS_G, COLS_G), BF16),
+            VMEM((3, 4, CUT, COLS_G), BF16),
+            VMEM((3, 4, rest, COLS_G), BF16),
+            VMEM((4, CUT, COLS_G), BF16),
+            VMEM((4, rest, COLS_G), BF16),
+            VMEM((3, CUT, COLS_G), BF16),
+            VMEM((3, rest, COLS_G), BF16),
+            VMEM((ROWS_G, COLS_G), BF16),
+            VMEM((4, ROWS_G, COLS_G), BF16),
+            VMEM((4, 2, 96, WCOLS), BF16),
+            VMEM((4, 96, WCOLS), BF16),
+            VMEM((4, 96, WCOLS), BF16),
+            VMEM((3, 96, WCOLS), BF16),
+            VMEM((96, WCOLS), BF16),
+            VMEM((4, 96, WCOLS), BF16),
+            VMEM((8, CHUNK, 128), F32),
+            VMEM((4, 2, CHUNK, 128), F32),
+            VMEM((2, CHUNK, 128), F32),
+            VMEM((8, CHUNK, 128), F32),
+            VMEM((8, 128), F32),
+            VMEM((4, 8, 128), F32),
+        ]
+        + [
+            dma(k)
+            for k in (4, 4, 4)
+        ]
+        + [dma(2, 2), dma(2), dma(4), dma(4)]
+        + [dma(3)] * 8
+        + [dma(3), dma(4), dma(2), dma(3), dma(3), dma(4), dma(4), dma(3), dma(4), dma(8), dma(8)]
+        + [dma(3), dma(4)],
+        compiler_params=params(2, 62),
+        cost_estimate=pl.CostEstimate(flops=2 * 10**10, bytes_accessed=3 * 10**7, transcendentals=10**7),
+    )(
+        docs, tokens, cond, w_ada, pat, gain, gain_two, gmid, do, q, k, v, everything, own, tab,
+        small_two, g,
+    )
+
+
+def finish_kernel(
+    output_in, gtok_in, blocks, qkv, packet, output_out, gtok_out, gqkv, gout, gup, gdown, gada, gvec
+):
+    output_out[...] = output_in[...]
+    gtok_out[...] = gtok_in[...]
+    for part in range(4):
+        for hh in range(2):
+            at = part * 768 + hh * 384
+            gup[:, at : at + 384] = blocks[part, hh * 96 : (hh + 1) * 96, :].astype(F32)
+        rh, ch = part // 2, part % 2
+        gout[rh * 48 : (rh + 1) * 48, ch * 384 : (ch + 1) * 384] = blocks[part, 384:432, :].astype(F32)
+    for pair in range(2):
+        both = jnp.concatenate(
+            [blocks[2 * pair, 192:384, :], blocks[2 * pair + 1, 192:384, :]], axis=0
+        ).astype(F32)
+        gdown[:, pair * 384 : (pair + 1) * 384] = both.T
+
+    def head_block(part, head):
+        g, j = head // OWN, head % OWN
+        if part == 0:
+            at, upper = 384 + 128 * (j // 2), j % 2
+        else:
+            at, upper = 128 * j, part - 1
+        return qkv[g, :, at : at + 128].astype(F32), upper
+
+    for part in range(3):
+        for pair in range(HEADS // 2):
+            even, up = head_block(part, 2 * pair)
+            even = pltpu.roll(even, 64, 1) if up else even
+            odd, up = head_block(part, 2 * pair + 1)
+            odd = odd if up else pltpu.roll(odd, 64, 1)
+            at = part * D + pair * 128
+            gqkv[:, at : at + 128] = jnp.where(lane(even.shape) < 64, even, odd)
+
+    conds = [packet[:, 19, :], packet[:, 20, :]]
+    lhs = jnp.concatenate([conds[0]] * 3 + [conds[1]] * 3, axis=0).astype(BF16)
+    for k in range(6):
+        first, second = packet[:, k, :], packet[:, 6 + k, :]
+        rhs = jnp.concatenate([*split3(first), *split3(second)], axis=0).astype(BF16)
+        gada[:, 96 * k : 96 * k + 96] = dg(lhs, rhs, TN)[:, :96]
+        gvec[0:1, 96 * k : 96 * k + 96] = jnp.sum(first + second, axis=0, keepdims=True)[:, :96]
+    for row, at, k in ((1, 0, 12), (2, 0, 13), (3, 0, 14), (3, 1, 15), (3, 2, 16), (3, 3, 17), (4, 0, 18)):
+        gvec[row : row + 1, 96 * at : 96 * at + 96] = jnp.sum(packet[:, k, :], axis=0, keepdims=True)[
+            :, :96
+        ]
+
+
+def call_finish(output, gtok, blocks, qkv, packet):
+    local = output.shape[0]
+    sds = jax.ShapeDtypeStruct
+    return pl.pallas_call(
+        finish_kernel,
+        out_shape=(
+            sds((local, D), BF16),
+            sds((local, D), F32),
+            sds((96, 3 * D), F32),
+            sds((96, D), F32),
+            sds((96, FF), F32),
+            sds((384, D), F32),
+            sds((128, 576), F32),
+            sds((8, 576), F32),
+        ),
+        in_specs=[vm()] * 5,
+        out_specs=(vm(),) * 8,
+        compiler_params=pltpu.CompilerParams(vmem_limit_bytes=40 * 2**20),
+        cost_estimate=pl.CostEstimate(flops=10**7, bytes_accessed=10**7, transcendentals=0),
+    )(output, gtok, blocks, qkv, packet)
+
+
+def plain_backward_kernel(
     tokens_ref,
     pat_ref,
     gain_ref,
@@ -772,13 +1403,13 @@
     lax.fori_loop(0, 4, drain, 0)
 
 
-def call_backward(tokens, pat, gain, gmid, do, q, k, v, everything, own, tab):
+def call_plain_backward(tokens, pat, gain, gmid, do, q, k, v, everything, own, tab):
     local = tokens.shape[0]
     half = local // 2
     length = 4 * local
     sds = jax.ShapeDtypeStruct
     return pl.pallas_call(
-        backward_kernel,
+        plain_backward_kernel,
         out_shape=(
             sds((local, D), F32),
             sds((8, 96, WCOLS), BF16),
@@ -861,7 +1492,31 @@
     output, gmid, g, small_two, do = call_middle(
         x, cot, att, pat, line(gain_two), w_out, w_up, line(b_up), w_down, line(b_down)
     )
-    gtok, gq, small_one = call_backward(
+    if (lax.axis_size("narrow"), lax.axis_size("wide")) == (4, 8):
+        gtok, blocks, qkv, packet, gcond = call_backward(
+            docs_per_row, x, cond, w_ada, pat, line(gain_one), line(gain_two), gmid, do, q, k, v,
+            everything, own, tab, small_two, g.reshape(4, 2, 4, ROWS_G, COLS_G),
+        )
+        output, gtok, gqkv, gout, gup, gdown, gada, gvec = call_finish(
+            output, gtok, blocks, qkv, packet
+        )
+        return (
+            output[None],
+            gtok[None],
+            gcond[None, :DOCS],
+            gada,
+            gvec[0],
+            gvec[1, :96],
+            gqkv,
+            gout,
+            gvec[2, :96],
+            gup,
+            gvec[3, :384],
+            gdown,
+            gvec[4, :96],
+        )
+
+    gtok, gq, small_one = call_plain_backward(
         x, pat, line(gain_one), gmid, do, q, k, v, everything, own, tab
     )
     n, w = lax.axis_index("narrow"), lax.axis_index("wide")

time: 706 us -> 249 us (0.35); the launches traced: 695 us -> 247 us
  waiting for transfers between devices: 362 us -> 0 us
  local copies, waits for them, and re-layouts: 86.4 us -> 12.8 us
  Pallas kernels: 176 us -> 232 us
  blocking collectives: 30.9 us -> 0 us
  between operations: 17.2 us -> 1.36 us
  other arithmetic: 15.8 us -> 0 us
    reduce_scatter x4 -> x0, waiting for transfers between devices: 235 us -> none  [the longest x3 235 us: total(): lax.psum_scatter(values.astype(F32), 'wide', scatter_dimension=0, tiled=T...]
    psum x1 -> x0, waiting for transfers between devices: 102 us -> none  [body(): small = lax.psum(small, 'narrow')]
    pallas_call x1 -> x2, Pallas kernels: 69.7 us -> 126 us  [the longest x1 123 us: call_backward(): pl.pallas_call(backward_kernel, out_shape=(sds((local, D), F32), sds((4,...]
    convert_element_type x4 -> x0, local copies, waits for them, and re-layouts: 35 us -> none  [total(): values.astype(F32)]
    unnamed x1 -> x0, blocking collectives: 30.9 us -> none
    unnamed x7 -> x0, waiting for transfers between devices: 24.6 us -> none
    unnamed x52 -> x17, local copies, waits for them, and re-layouts: 29.2 us -> 5.52 us
    slice x5 -> x2, local copies, waits for them, and re-layouts: 12.1 us -> 1.2 us  [the longest x1 0.6 us: body(): gvec[0]]
  transfers between devices with their start and end apart: 6 -> 0, of which waited for: 5 -> 0; matrix products, arithmetic and copies ran while one was open for 10% -> 0% of each run, Pallas kernels for 0% -> 0%
where the time goes in v2:
time: 249 us; the launch traced here: 247 us
  Pallas kernels  232 us (93%)
  local copies, waits for them, and re-layouts  12.8 us (5%)
    pallas_call x1, Pallas kernels, call_backward(): pl.pallas_call(backward_kernel, out_shape=(sds((local, D), F32), sds((4,...  123 us
    pallas_call x1, Pallas kernels, call_forward(): pl.pallas_call(forward_kernel, out_shape=(sds((local, D), BF16), sds((len...  59.4 us
    pallas_call x1, Pallas kernels, call_middle(): pl.pallas_call(middle_kernel, out_shape=(sds((local, D), BF16), sds((loca...  46.5 us
    unnamed x17, local copies, waits for them, and re-layouts  5.52 us

profile of v2, /device:TPU:0, one launch (start us, length us, event | category | flops | bytes accessed | tf_op | source)
XLA Modules:
  0.0 246.6 jit_solution(5164962655764811019)
XLA Ops:
  1.3 1.3 reshape.58.b_ada_ref
  2.6 1.3 reshape.59.gain_ref
  3.9 0.0 copy-start.6
  3.9 0.0 copy-start.5
  3.9 0.0 copy-start.7
  3.9 59.4 %shard_map.246 = (bf16[512,768]{1,0:T(8,128)(2,1)}, bf16[2048,768]{1,0:T(8,128)(2,1)}, bf16[3,2048,128]{2,1,0:T(8,128)(2,1)}, bf16[3,2048,128]{2,1,0:T(8,128)(2,...) custom-call(s32[1]{0:T(128)S(6)} %copy.29.docs_ref, ...), custom_call_target="tpu_custom_call" | custom-call | flops 10000000000 | bytes 20000000 | tf_op jit(solution)/shard_map/pallas_call | solution.py:385
  63.3 0.0 copy-done.6
  63.3 0.6 reshape.60.gain_ref.gain_two_ref
  63.8 0.0 copy-done.5
  63.9 0.6 reshape.61.b_up_ref
  64.5 0.0 copy-done.7
  64.5 0.6 reshape.62.b_down_ref
  65.0 46.5 %shard_map.247 = (bf16[512,768]{1,0:T(8,128)(2,1)}, f32[512,768]{1,0:T(8,128)}, bf16[8,4,432,384]{3,2,1,0:T(8,128)(2,1)}, f32[8,6912]{1,0:T(8,128)}, bf16[3,4,256,128]{3,2,1,0:T(8,128)(2,1)}) custom-call(bf16[512,768]{1,0:T(8,128)(2,1)} %bitcast.17, bf16[512,768]{1,0:T(8,128)(2,1)} %bitcast.15, bf16[512,768]{1,0:T(8,128)(2,1)} %get-tuple-element.39.att_ref, ...), custom_call_target="tpu_custom_call" | custom-call | flops 20000000000 | bytes 30000000 | tf_op jit(solution)/shard_map/pallas_call | solution.py:588
  111.6 0.0 copy-start.2
  111.6 123.2 %shard_map.248 = (f32[512,768]{1,0:T(8,128)}, bf16[4,432,384]{2,1,0:T(8,128)(2,1)}, bf16[4,96,640]{2,1,0:T(8,128)(2,1)}, f32[8,24,128]{2,1,0:T(8,128)}, f32[8,128]{1,0:T(8,128)}) custom-call(s32[1]{0:T(128)S(6)} %copy.29.docs_ref, bf16[512,768]{1,0:T(8,128)(2,1)} %bitcast.18, bf16[2,128]{1,0:T(2,128)(2,1)} %bitcast.21, bf16[128,4608]{1,0:T(8,128)(2,1)} %w_ada_ref.3, ...), custom_call_target="tpu_custom_call" | custom-call | flops 20000000000 | bytes 30000000 | tf_op jit(solution)/shard_map/pallas_call | solution.py:1120
  234.9 0.0 copy-done.2
  234.9 0.0 copy-start
  234.9 1.4 copy-done
  236.3 0.0 copy-start.1
  236.3 1.3 copy-done.1
  237.6 0.0 copy-start.3
  237.6 1.0 copy-done.3
  238.6 0.0 copy-start.4
  238.6 0.9 copy-done.4
  239.5 3.2 %shard_map.249 = (bf16[512,768]{1,0:T(8,128)(2,1)}, f32[512,768]{1,0:T(8,128)}, f32[96,2304]{1,0:T(8,128)}, f32[96,768]{1,0:T(8,128)}, f32[96,3072]{1,0:T(8,128)...) custom-call(bf16[512,768]{1,0:T(8,128)(2,1)S(1)} %copy-done.2, f32[512,768]{1,0:T(8,128)S(1)} %copy-done, ...), custom_call_target="tpu_custom_call" | custom-call | flops 10000000 | bytes 10000000 | tf_op jit(solution)/shard_map/pallas_call | solution.py:1231
  242.7 1.2 slice_bitcast_fusion
  244.0 0.9 copy.28
  244.9 0.6 slice_reduce_fusion
  245.5 0.5 slice_bitcast_fusion.1
  246.0 0.6 slice_reduce_fusion.1
Async XLA Ops:
  3.9 59.4 %copy-start.6 = (bf16[768]{0:T(1024)(128)(2,1)S(1)}, bf16[768]{0:T(1024)(128)(2,1)}, u32[]{:S(2)}) copy-start(bf16[768]{0:T(1024)(128)(2,1)} %param.23) | copy-start | bytes 4612
  3.9 60.0 %copy-start.5 = (bf16[3072]{0:T(1024)(128)(2,1)S(1)}, bf16[3072]{0:T(1024)(128)(2,1)}, u32[]{:S(2)}) copy-start(bf16[3072]{0:T(1024)(128)(2,1)} %param.25) | copy-start | bytes 18436
  3.9 60.6 %copy-start.7 = (bf16[768]{0:T(1024)(128)(2,1)S(1)}, bf16[768]{0:T(1024)(128)(2,1)}, u32[]{:S(2)}) copy-start(bf16[768]{0:T(1024)(128)(2,1)} %param.27) | copy-start | bytes 4612
  111.6 123.3 %copy-start.2 = (bf16[512,768]{1,0:T(8,128)(2,1)S(1)}, bf16[512,768]{1,0:T(8,128)(2,1)}, u32[]{:S(2)}) copy-start(bf16[512,768]{1,0:T(8,128)(2,1)} %get-tuple-element.41.output_in) | copy-start | bytes 2359300
  234.9 1.4 copy-start
  236.3 1.3 copy-start.1
  237.6 1.0 copy-start.3
  238.6 0.9 copy-start.4

commit v3 on v1

--- a/solution.py
+++ b/solution.py
@@ -18,6 +18,8 @@
 BIG = 1e30
 OWN = 3
 WCOLS = 640
+KV_AT = (0, 128, 384)
+Q_AT = (256, 320, 512)
 ROWS_G = 432
 COLS_G = 384
 MESH = pl.DeviceIdType.MESH
@@ -217,10 +219,10 @@
         return pltpu.roll(block, lax.rem(col + at, 2) * 64, 1)
 
     for j in range(OWN):
-        own_ref[:, j * 128 : (j + 1) * 128] = jnp.where(
+        own_ref[:, KV_AT[j] : KV_AT[j] + 128] = jnp.where(
             lanes_w < 64, columns(1, j, 0), columns(2, j, 1)
         ).astype(BF16)
-    own_ref[:, 384:512] = jnp.where(lanes_w < 64, columns(0, 0, 0), columns(0, 1, 1)).astype(BF16)
+    own_ref[:, 256:384] = jnp.where(lanes_w < 64, columns(0, 0, 0), columns(0, 1, 1)).astype(BF16)
     own_ref[:, 512:640] = jnp.where(lanes_w < 64, columns(0, 2, 0), 0.0).astype(BF16)
 
     docs_copy.wait()
@@ -249,12 +251,12 @@
                 return values * cosine + halves_turn(values) * sine
 
             for j in range(OWN):
-                block = wide[:, j * 128 : (j + 1) * 128]
+                block = wide[:, KV_AT[j] : KV_AT[j] + 128]
                 k_ref[j, rows, :] = with_tail(rot(block), tail_k)
                 v_ref[j, rows, :] = jnp.where(
                     lane(block.shape) < 64, pltpu.roll(block, 64, 1), 1.0
                 ).astype(BF16)
-            first = rot(wide[:, 384:512]) * HEAD_DIM**-0.5
+            first = rot(wide[:, 256:384]) * HEAD_DIM**-0.5
             q_ref[0, rows, :] = with_tail(first, tail_q)
             q_ref[1, rows, :] = with_tail(pltpu.roll(first, 64, 1), tail_q)
             q_ref[2, rows, :] = with_tail(rot(wide[:, 512:640]) * HEAD_DIM**-0.5, tail_q)
@@ -616,7 +618,945 @@
     )(tokens, cot, att, pat, gain, w_out, w_up, b_up, w_down, b_down)
 
 
-def backward_kernel(
+CUT = 320
+CHUNK = 24
+PARTS_Q = ((0, 384), (384, 256))
+
+
+def slot_of(other, me):
+    return lax.rem(other - me + 3, 4)
+
+
+def fused_kernel(
+    docs_ref,
+    tokens_ref,
+    cot_ref,
+    att_ref,
+    cond_ref,
+    pat_ref,
+    gain_one_ref,
+    gain_ref,
+    b_up_ref,
+    b_down_ref,
+    w_ada_hbm,
+    w_out_hbm,
+    w_up_hbm,
+    w_down_hbm,
+    q_hbm,
+    k_hbm,
+    v_hbm,
+    all_hbm,
+    own_hbm,
+    tab_hbm,
+    out_ref,
+    gtok_ref,
+    blocks_ref,
+    qkv_a_ref,
+    qkv_b_ref,
+    packet_ref,
+    gcond_ref,
+    small_ref,
+    small_one,
+    dsend,
+    dland,
+    g_own,
+    g_land,
+    land_x1,
+    land_y1,
+    land_x2,
+    land_y2,
+    land_b1,
+    land_a2,
+    land_b2,
+    block,
+    land_block,
+    cland,
+    rland,
+    gq_a,
+    gq_b,
+    land_qx_a,
+    land_qx_b,
+    land_qz_a,
+    land_qz_b,
+    land_q_a,
+    land_q_b,
+    pack,
+    land_s1,
+    pack_sum,
+    land_s2,
+    gc_mine,
+    land_gc,
+    load_sem,
+    d_send,
+    d_recv,
+    g_send,
+    g_recv,
+    one_sem,
+    two_sem,
+    b1_send,
+    b1_recv,
+    a2_send,
+    a2_recv,
+    b2_send,
+    b2_recv,
+    ag_send,
+    ag_recv,
+    c_send,
+    c_recv,
+    r_send,
+    r_recv,
+    qx_sem,
+    qz_send,
+    qz_recv,
+    qp_send,
+    qp_recv,
+    s1_send,
+    s1_recv,
+    s2_send,
+    s2_recv,
+    gc_send,
+    gc_recv,
+):
+    n, ny, nx, z, c = place()
+    w = 2 * z + c
+    local = tokens_ref.shape[0]
+    half = local // 2
+    length = local * 4
+    group = 2 * ny + c
+    tile = 768
+    across = n + 1 - 2 * nx
+    along_y = lax.rem(n + 2, 4)
+
+    barrier = pltpu.get_barrier_semaphore()
+
+    def greet(device):
+        pl.semaphore_signal(barrier, inc=1, device_id=device, device_id_type=MESH)
+
+    me = n * 2 + c
+    for step in range(1, 8):
+        other = lax.rem(me + step, 8)
+        greet((other // 2, 2 * z + lax.rem(other, 2)))
+    for step in range(1, 4):
+        greet((n, 2 * lax.rem(z + step, 4) + c))
+    for row in range(8):
+
+        @pl.when(jnp.logical_not(jnp.logical_and(z == n, row == w)))
+        def _():
+            greet((z, row))
+
+    def others(base):
+        return [lax.rem(base + step, 4) for step in (1, 2, 3)]
+
+    def piece(index):
+        return pat_ref[:, index * D : (index + 1) * D]
+
+    def spread(values, pattern):
+        return flat8(by8(values) * pattern[None])
+
+
+    def core_up(g_give, t):
+        return remote(
+            g_give.at[:, t // 2, t % 2, pl.ds(0, 192)],
+            g_land.at[:, t // 2, t % 2, pl.ds(0, 192)],
+            g_send.at[t],
+            g_recv.at[t],
+            sibling(n, z, c),
+        )
+
+    def core_down(g_give, t):
+        return remote(
+            g_give.at[t, :, :, pl.ds(192, 192)],
+            g_land.at[t, :, :, pl.ds(192, 192)],
+            g_send.at[4 + t],
+            g_recv.at[4 + t],
+            sibling(n, z, c),
+        )
+
+    def core_out(g_give):
+        return remote(
+            g_give.at[:, :, :, pl.ds(384, 48)],
+            g_land.at[:, :, :, pl.ds(384, 48)],
+            g_send.at[8],
+            g_recv.at[8],
+            sibling(n, z, c),
+        )
+
+    def d_copy(head):
+        pick_y, cc, j = head // OWN // 2, head // OWN % 2, head % OWN
+        target = 2 * pick_y + c
+        is_self = jnp.logical_and(target == n, c == cc)
+        return (
+            is_self,
+            dsend.at[head],
+            dland.at[j, n],
+            d_send.at[head],
+            d_recv.at[j, n],
+            (target, 2 * z + cc),
+        )
+
+
+    def middle(
+        w_out, w_up, w_down, active, slope, acc, branch_ref, lhs_t, low_ref, g_give
+    ):
+        loads = [
+            pltpu.make_async_copy(src, dst, load_sem.at[i])
+            for i, (src, dst) in enumerate(((w_out_hbm, w_out), (w_up_hbm, w_up), (w_down_hbm, w_down)))
+        ]
+        for load in loads:
+            load.start()
+        loads[0].wait()
+        branch_ref[...] = dg(att_ref[...], w_out[...], NN)
+
+        def middle_values():
+            return tokens_ref[...].astype(F32) + spread(branch_ref[...], piece(2))
+
+        normed, _ = norm_stats(middle_values())
+        amp = gain_ref[...].astype(F32) * (1.0 + piece(4))
+        low_ref[...] = flat8(by8(normed) * amp[None] + piece(3)[None]).astype(BF16)
+        acc[...] = jnp.broadcast_to(b_down_ref[...].astype(F32), acc.shape)
+        loads[1].wait()
+        loads[2].wait()
+
+        def up(t, carry):
+            cols = pl.ds(pl.multiple_of(t * tile, tile), tile)
+            hidden = dg(low_ref[...], w_up[:, cols], NN) + b_up_ref[:, cols].astype(F32)
+            square = hidden * hidden
+            bend = jnp.tanh(0.7978845608028654 * hidden * (1.0 + 0.044715 * square))
+            part = 0.5 * (1.0 + bend)
+            active[:, cols] = (hidden * part).astype(BF16)
+            slope[:, cols] = part + (0.5 * 0.7978845608028654) * hidden * (1.0 - bend * bend) * (
+                1.0 + 3.0 * 0.044715 * square
+            )
+            acc[...] += dg(active[:, cols], w_down[cols, :], NN)
+            return carry
+
+        lax.fori_loop(0, FF // tile, up, 0)
+
+        cot = cot_ref[...].astype(F32)
+        down = acc[...]
+        out_ref[...] = (middle_values() + spread(down, piece(5))).astype(BF16)
+        small_ref[:, 3 * D : 4 * D] = sum8(cot * down)
+        lhs_t[0] = low_ref[...].T
+        gdown = spread(cot, piece(5)).astype(BF16)
+        low_ref[...] = gdown
+        small_ref[:, 4 * D + FF :] = sum8(gdown.astype(F32))
+        lhs_t[1] = gdown.T
+        acc[...] = jnp.zeros_like(acc)
+
+        def back(t, carry):
+            cols = pl.ds(pl.multiple_of(t * tile, tile), tile)
+            ghidden = dg(low_ref[...], w_down[cols, :], NT) * slope[:, cols]
+            low = ghidden.astype(BF16)
+            small_ref[:, pl.ds(pl.multiple_of(4 * D + t * tile, tile), tile)] = sum8(low.astype(F32))
+            acc[...] += dg(low, w_up[:, cols], NT)
+            gup = dg(lhs_t[0], low, NN).astype(BF16).reshape(4, 2, 96, tile)
+            mine = jnp.where(c == 0, gup[:, 0], gup[:, 1])
+            other = jnp.where(c == 0, gup[:, 1], gup[:, 0])
+            for hh in range(2):
+                rows, lanes_h = slice(hh * 96, (hh + 1) * 96), slice(hh * 384, (hh + 1) * 384)
+                g_own[:, t // 2, t % 2, rows, :] = mine[:, :, lanes_h]
+                g_give[:, t // 2, t % 2, rows, :] = other[:, :, lanes_h]
+            core_up(g_give, t).start()
+            gdw = dg(lhs_t[1], active[:, cols], NN).astype(BF16)
+            mine = jnp.where(c == 0, gdw[:, :384], gdw[:, 384:])
+            other = jnp.where(c == 0, gdw[:, 384:], gdw[:, :384])
+            g_own[t, :, :, 192:384, :] = mine.reshape(2, 2, 192, 384)
+            g_give[t, :, :, 192:384, :] = other.reshape(2, 2, 192, 384)
+            core_down(g_give, t).start()
+            return carry
+
+        lax.fori_loop(0, FF // tile, back, 0)
+
+        normed, inv = norm_stats(middle_values())
+        gsecond = acc[...]
+        small_ref[:, D : 2 * D] = sum8(gsecond)
+        small_ref[:, 2 * D : 3 * D] = sum8(gsecond * normed)
+        grad = spread(gsecond, gain_ref[...].astype(F32) * (1.0 + piece(4)))
+        mean = jnp.mean(grad, axis=-1, keepdims=True)
+        along = jnp.mean(grad * normed, axis=-1, keepdims=True)
+        gmid = cot_ref[...].astype(F32) + (grad - mean - normed * along) * inv
+        gtok_ref[...] = gmid
+        small_ref[:, 0:D] = sum8(gmid * branch_ref[...])
+        gbranch = spread(gmid, piece(2)).astype(BF16)
+        gatt = dg(gbranch, w_out[...], NT)
+        for pair in range(HEADS // 2):
+            top = gatt[0:half, pair * 128 : (pair + 1) * 128]
+            bottom = gatt[half:local, pair * 128 : (pair + 1) * 128]
+            lower = lane(top.shape) < 64
+            dsend[2 * pair] = jnp.where(lower, top, pltpu.roll(bottom, 64, 1)).astype(BF16)
+            dsend[2 * pair + 1] = jnp.where(lower, pltpu.roll(top, 64, 1), bottom).astype(BF16)
+        for j in range(OWN):
+            for g in range(4):
+                send_or_keep(*d_copy(g * OWN + j))
+
+        for hh in range(2):
+            gout = dg(att_ref[...], gbranch[:, hh * 384 : (hh + 1) * 384], TN).astype(BF16)
+            shaped = gout.reshape(4, 2, 2, 48, 384)
+            g_own[:, :, hh, 384:432, :] = jnp.where(c == 0, shaped[:, 0], shaped[:, 1])
+            g_give[:, :, hh, 384:432, :] = jnp.where(c == 0, shaped[:, 1], shaped[:, 0])
+        core_out(g_give).start()
+        for t in range(4):
+            core_up(g_give, t).wait_send()
+            core_down(g_give, t).wait_send()
+        core_out(g_give).wait_send()
+
+    pl.semaphore_wait(barrier, jnp.where(z == n, 17, 18))
+    pl.run_scoped(
+        middle,
+        VMEM((D, D), BF16),
+        VMEM((D, FF), BF16),
+        VMEM((FF, D), BF16),
+        VMEM((local, FF), BF16),
+        VMEM((local, FF), F32),
+        VMEM((local, D), F32),
+        VMEM((local, D), F32),
+        VMEM((2, D, local), BF16),
+        VMEM((local, D), BF16),
+        VMEM((4, 2, 2, ROWS_G, COLS_G), BF16),
+    )
+
+
+    top = pl.ds(0, CUT)
+    rest = pl.ds(CUT, ROWS_G - CUT)
+
+    def one_x():
+        return remote(g_own.at[pl.ds(0, 2), :, 1 - nx, top], land_x1, one_sem.at[0], one_sem.at[1], (across, w))
+
+    def one_y():
+        return remote(
+            g_own.at[pl.ds(2, 2), 1 - ny, :, top], land_y1, one_sem.at[2], one_sem.at[3], (along_y, w)
+        )
+
+    def two_y():
+        return remote(
+            g_own.at[pl.ds(0, 2), 1 - ny, nx, top], land_y2, two_sem.at[0], two_sem.at[1], (along_y, w)
+        )
+
+    def two_x():
+        return remote(
+            g_own.at[pl.ds(2, 2), ny, 1 - nx, top], land_x2, two_sem.at[2], two_sem.at[3], (across, w)
+        )
+
+    def b1_copy(chip):
+        slot = slot_of(chip, z)
+        return remote(
+            g_own.at[chip, :, :, rest], land_b1.at[slot], b1_send.at[slot], b1_recv.at[slot],
+            (n, 2 * chip + c),
+        )
+
+    def a2_copy(chip):
+        slot = slot_of(chip, z)
+        return remote(
+            g_own.at[chip, ny, nx, top], land_a2.at[slot], a2_send.at[slot], a2_recv.at[slot],
+            (n, 2 * chip + c),
+        )
+
+    def b2_copy(other):
+        slot = slot_of(other, n)
+        return remote(
+            g_own.at[z, other // 2, lax.rem(other, 2), rest], land_b2.at[slot], b2_send.at[slot],
+            b2_recv.at[slot], (other, w),
+        )
+
+    def ag_copy(other):
+        return remote(block, land_block.at[n], ag_send.at[slot_of(other, n)], ag_recv.at[n], (other, w))
+
+    def core_finish():
+        for t in range(4):
+            wait_bytes(g_land.at[:, t // 2, t % 2, pl.ds(0, 192)], g_recv.at[t])
+            wait_bytes(g_land.at[t, :, :, pl.ds(192, 192)], g_recv.at[4 + t])
+        wait_bytes(g_land.at[:, :, :, pl.ds(384, 48)], g_recv.at[8])
+
+        def add(i, carry):
+            chip, y, x = i // 4, lax.rem(i // 2, 2), lax.rem(i, 2)
+            g_own[chip, y, x] = (
+                g_own[chip, y, x].astype(F32) + g_land[chip, y, x].astype(F32)
+            ).astype(BF16)
+            return carry
+
+        lax.fori_loop(0, 16, add, 0)
+        one_x().start()
+        one_y().start()
+        for chip in others(z):
+            b1_copy(chip).start()
+
+    def stage_two():
+        one_x().wait_recv()
+        one_y().wait_recv()
+        for i in range(2):
+            for k in range(2):
+                g_own[i, k, nx, 0:CUT] = (
+                    g_own[i, k, nx, 0:CUT].astype(F32) + land_x1[i, k].astype(F32)
+                ).astype(BF16)
+                g_own[2 + i, ny, k, 0:CUT] = (
+                    g_own[2 + i, ny, k, 0:CUT].astype(F32) + land_y1[i, k].astype(F32)
+                ).astype(BF16)
+        two_y().start()
+        two_x().start()
+
+    def stage_a2():
+        two_y().wait_recv()
+        two_x().wait_recv()
+        for i in range(2):
+            g_own[i, ny, nx, 0:CUT] = (
+                g_own[i, ny, nx, 0:CUT].astype(F32) + land_y2[i].astype(F32)
+            ).astype(BF16)
+            g_own[2 + i, ny, nx, 0:CUT] = (
+                g_own[2 + i, ny, nx, 0:CUT].astype(F32) + land_x2[i].astype(F32)
+            ).astype(BF16)
+        for chip in others(z):
+            a2_copy(chip).start()
+
+    def stage_b2():
+        for slot in range(3):
+            wait_bytes(land_b1.at[slot], b1_recv.at[slot])
+        for part in range(4):
+            total = g_own[z, part // 2, part % 2, CUT:ROWS_G].astype(F32)
+            for slot in range(3):
+                total = total + land_b1[slot, part // 2, part % 2].astype(F32)
+            g_own[z, part // 2, part % 2, CUT:ROWS_G] = total.astype(BF16)
+        for other in others(n):
+            b2_copy(other).start()
+
+    def last():
+        for slot in range(3):
+            wait_bytes(land_a2.at[slot], a2_recv.at[slot])
+            wait_bytes(land_b2.at[slot], b2_recv.at[slot])
+        upper = g_own[z, ny, nx, 0:CUT].astype(F32)
+        lower = g_own[z, ny, nx, CUT:ROWS_G].astype(F32)
+        for slot in range(3):
+            upper = upper + land_a2[slot].astype(F32)
+            lower = lower + land_b2[slot].astype(F32)
+        block[0:CUT] = upper.astype(BF16)
+        block[CUT:ROWS_G] = lower.astype(BF16)
+        for other in others(n):
+            ag_copy(other).start()
+
+
+    bufs_q = ((gq_a, land_qx_a, land_qz_a, land_q_a), (gq_b, land_qx_b, land_qz_b, land_q_b))
+
+    def qx_copy(p):
+        gq, land_x, _, _ = bufs_q[p]
+        return remote(gq.at[:, 1 - nx], land_x, qx_sem.at[p, 0], qx_sem.at[p, 1], (across, w))
+
+    def qz_copy(p, chip):
+        gq, _, land_z, _ = bufs_q[p]
+        slot = slot_of(chip, z)
+        return remote(
+            gq.at[chip, nx], land_z.at[slot], qz_send.at[p, slot], qz_recv.at[p, slot],
+            (n, 2 * chip + c),
+        )
+
+    def qp_copy(p, other):
+        gq, _, _, land = bufs_q[p]
+        is_self = jnp.logical_and(other == n, nx == c)
+        return (
+            is_self, gq.at[z, nx], land.at[group], qp_send.at[p, other], qp_recv.at[p, group],
+            (other, 2 * z + nx),
+        )
+
+    def q_z(p):
+        gq, land_x, _, _ = bufs_q[p]
+        qx_copy(p).wait_recv()
+        for chip in range(4):
+            gq[chip, nx] = (gq[chip, nx].astype(F32) + land_x[chip].astype(F32)).astype(BF16)
+        for chip in others(z):
+            qz_copy(p, chip).start()
+
+    def q_plane(p):
+        gq, _, land_z, _ = bufs_q[p]
+        for slot in range(3):
+            wait_bytes(land_z.at[slot], qz_recv.at[p, slot])
+        total = gq[z, nx].astype(F32)
+        for slot in range(3):
+            total = total + land_z[slot].astype(F32)
+        gq[z, nx] = total.astype(BF16)
+        for other in range(4):
+            send_or_keep(*qp_copy(p, other))
+
+
+    def s1_copy(other):
+        return remote(
+            pack.at[pl.ds(2 * other, 2)], land_s1.at[n], s1_send.at[slot_of(other, n)],
+            s1_recv.at[n], (other, w),
+        )
+
+    def gc_copy(other):
+        return remote(
+            gc_mine, land_gc.at[n], gc_send.at[slot_of(other, n)], gc_recv.at[n], (other, w)
+        )
+
+    def s2_copy(index):
+        i, other = index // 4, lax.rem(index, 4)
+        is_self = jnp.logical_and(other == n, w == 2 * n + i)
+        return (
+            is_self, pack_sum.at[i], land_s2.at[w], s2_send.at[index], s2_recv.at[w],
+            (other, 2 * n + i),
+        )
+
+    def small_sums(w_ada_ref):
+
+        two = docs_ref[0] == DOCS
+        even_rows = lax.rem(lax.broadcasted_iota(jnp.int32, (8, D), 0), 2) == 0
+
+        def even_odd(values):
+            even = jnp.sum(jnp.where(even_rows, values, 0.0), axis=0, keepdims=True)
+            return even, jnp.sum(jnp.where(even_rows, 0.0, values), axis=0, keepdims=True)
+
+        pack[...] = jnp.zeros_like(pack)
+        gc_mine[...] = jnp.zeros_like(gc_mine)
+
+        def put(chunk, row, values, s):
+            pack[chunk, row : row + 1, 0:96] = values[:, 96 * s : 96 * s + 96]
+
+        raws = [
+            small_one[:, 0:D],
+            small_one[:, D : 2 * D],
+            small_ref[:, 0:D],
+            small_ref[:, D : 2 * D],
+            small_ref[:, 2 * D : 3 * D],
+            small_ref[:, 3 * D : 4 * D],
+        ]
+        gains = {1: gain_one_ref, 4: gain_ref}
+        for piece in range(6):
+            even, odd = even_odd(raws[piece])
+            if piece in gains:
+                scale = pat_ref[:, piece * D : (piece + 1) * D]
+                gain_sum = even * (1.0 + scale[0:1]) + odd * (1.0 + scale[1:2])
+                for s in range(8):
+                    put(s, 12 if piece == 1 else 13, gain_sum, s)
+                gain = gains[piece][...].astype(F32)
+                even, odd = even * gain, odd * gain
+            first_doc = jnp.where(two, even, even + odd)
+            second_doc = jnp.where(two, odd, 0.0)
+            for s in range(8):
+                at = 8 * piece + s
+                put(at // 6, at % 6, first_doc, s)
+                put(at // 6, 6 + at % 6, second_doc, s)
+            pieces = [*split3(first_doc), *split3(second_doc)]
+            stacked = jnp.concatenate([*pieces, jnp.zeros((10, D), F32)], axis=0).astype(BF16)
+            part = dg(stacked, w_ada_ref[:, piece * D : (piece + 1) * D], NT)
+            gc_mine[0:1] += part[0:1] + part[1:2] + part[2:3]
+            gc_mine[1:2] += part[3:4] + part[4:5] + part[5:6]
+        for s in range(32):
+            col = 4 * D + 96 * s
+            row = jnp.sum(small_ref[:, col : col + 96], axis=0, keepdims=True)
+            pack[s // 4, 14 + s % 4 : 15 + s % 4, 0:96] = row
+        for s in range(8):
+            col = 4 * D + FF + 96 * s
+            pack[s, 18:19, 0:96] = jnp.sum(small_ref[:, col : col + 96], axis=0, keepdims=True)
+
+        for other in others(n):
+            s1_copy(other).start()
+            gc_copy(other).start()
+        land_gc[n] = gc_mine[...]
+        land_s1[n] = pack[pl.ds(2 * n, 2)]
+        for other in others(n):
+            wait_bytes(land_s1.at[other], s1_recv.at[other])
+        total = land_s1[0] + land_s1[1] + land_s1[2] + land_s1[3]
+        pack_sum[...] = total
+        cond = cond_ref[...].astype(F32)
+        for i in range(2):
+            pack_sum[i, 19:21, :] = cond
+
+        for index in range(8):
+            send_or_keep(*s2_copy(index))
+
+
+    def heads(
+        q_ref, k_ref, v_ref, all_ref, own_ref, tab_ref, w_ada_ref, packed, acc_k, acc_v, acc_w, kept, csend
+    ):
+        def c_copy(quarter):
+            return remote(
+                csend.at[quarter], cland.at[quarter], c_send.at[quarter], c_recv.at[quarter],
+                sibling(n, z, c),
+            )
+
+        def r_copy(quarter):
+            is_self = jnp.logical_and(quarter == n, nx == c)
+            return (
+                is_self,
+                csend.at[quarter],
+                rland.at[ny, pl.ds(pl.multiple_of(c * half, half), half)],
+                r_send.at[quarter],
+                r_recv.at[ny, c],
+                (quarter, 2 * z + nx),
+            )
+
+        loads = [
+            pltpu.make_async_copy(src, dst, load_sem.at[i])
+            for i, (src, dst) in enumerate(
+                (
+                    (q_hbm, q_ref),
+                    (k_hbm, k_ref),
+                    (v_hbm, v_ref),
+                    (tab_hbm, tab_ref),
+                    (all_hbm, all_ref),
+                    (own_hbm, own_ref),
+                    (w_ada_hbm, w_ada_ref),
+                )
+            )
+        ]
+        for load in loads:
+            load.start()
+        core_finish()
+        for load in loads[:4]:
+            load.wait()
+        lanes_h = lane((half, 128))
+        lanes = lane((local, 128))
+
+        def turned(values, rows):
+            cosine, sine = cos_sin(tab_ref[rows, :])
+            return values * cosine - halves_turn(values) * sine
+
+        def rounded(values):
+            return values.astype(BF16).astype(F32)
+
+        def weights(p):
+            gq = bufs_q[p][0]
+            at, width = PARTS_Q[p]
+            if p == 0:
+                loads[4].wait()
+            acc_w[:, 0:width] = dg(all_ref[0:local, :], packed[0:local, at : at + width], TN)
+
+            def step(i, carry):
+                rows = pl.ds(pl.multiple_of(i * local, local), local)
+                acc_w[:, 0:width] += dg(all_ref[rows, :], packed[rows, at : at + width], TN)
+                return carry
+
+            lax.fori_loop(1, 4, step, 0)
+            gq[...] = acc_w[:, 0:width].astype(BF16).reshape(gq.shape)
+            qx_copy(p).start()
+
+        hooks = {(1, 4): stage_two, (2, 2): stage_a2, (2, 4): stage_b2, (2, 6): lambda: q_z(0)}
+        for j in range(OWN):
+            for quarter in range(4):
+                wait_bytes(dland.at[j, quarter], d_recv.at[j, quarter])
+            acc_k[...] = jnp.zeros_like(acc_k)
+            acc_v[...] = jnp.zeros_like(acc_v)
+
+            def step(i, carry):
+                for (at_j, at_i), hook in hooks.items():
+                    if at_j == j:
+                        pl.when(i == at_i)(hook)
+                rows = pl.ds(pl.multiple_of(i * half, half), half)
+                grad = pltpu.roll(dland[j, i // 2].astype(F32), lax.rem(i, 2) * 64, 1)
+                grad = jnp.where(lanes_h < 64, grad, 0.0).astype(BF16)
+                query = q_ref[j, rows, :]
+                probs = jnp.exp2(dg(query, k_ref[j], NT) * LOG2E)
+                gprobs = probs * dg(grad, v_ref[j], NT)
+                scores = (gprobs - probs * jnp.sum(gprobs, axis=1, keepdims=True)).astype(BF16)
+                probs = probs.astype(BF16)
+                gquery = rounded(dg(scores, k_ref[j], NN) * HEAD_DIM**-0.5)
+                packed[rows, Q_AT[j] : Q_AT[j] + 64] = turned(gquery, rows)[:, :64].astype(BF16)
+                acc_v[...] += dg(grad.T[:64], probs, NN)
+                acc_k[...] += dg(query.T[:64], scores, NN)
+                return carry
+
+            lax.fori_loop(0, 8, step, 0)
+
+            def finish(i, carry):
+                rows = pl.ds(pl.multiple_of(i * local, local), local)
+                both = rounded(jnp.concatenate([acc_k[:, rows], acc_v[:, rows]], axis=0).T)
+                packed[rows, KV_AT[j] : KV_AT[j] + 128] = jnp.where(
+                    lanes < 64, turned(both, rows), both
+                ).astype(BF16)
+                return carry
+
+            lax.fori_loop(0, 4, finish, 0)
+            if j == 1:
+                weights(0)
+        packed[:, 576:640] = jnp.zeros((length, 64), BF16)
+
+        def rows_of(quarter, hh):
+            return pl.ds(pl.multiple_of(quarter * local + hh * half, half), half)
+
+        def order(i):
+            return lax.rem(n + 3 - i, 4)
+
+        loads[5].wait()
+
+        def give(i, carry):
+            quarter = order(i)
+            csend[quarter] = dg(packed[rows_of(quarter, 1 - c), :], own_ref[...], NT).astype(BF16)
+            c_copy(quarter).start()
+            return carry
+
+        lax.fori_loop(0, 4, give, 0)
+
+        def keep(i, carry):
+            quarter = order(i)
+            kept[quarter] = dg(packed[rows_of(quarter, c), :], own_ref[...], NT)
+            return carry
+
+        lax.fori_loop(0, 4, keep, 0)
+
+        def add(i, carry):
+            quarter = order(i)
+            c_copy(quarter).wait()
+            csend[quarter] = (kept[quarter] + cland[quarter].astype(F32)).astype(BF16)
+            send_or_keep(*r_copy(quarter))
+            return carry
+
+        lax.fori_loop(0, 4, add, 0)
+        weights(1)
+        last()
+        q_z(1)
+        normed, inv = norm_stats(tokens_ref[...].astype(F32))
+        q_plane(0)
+
+        for y in range(2):
+            for hh in range(2):
+                wait_bytes(rland.at[y, pl.ds(hh * half, half)], r_recv.at[y, hh])
+        gfirst = rland[0].astype(F32) + rland[1].astype(F32)
+        small_one[:, 0:D] = sum8(gfirst)
+        small_one[:, D : 2 * D] = sum8(gfirst * normed)
+        grad = spread(gfirst, gain_one_ref[...].astype(F32) * (1.0 + piece(1)))
+        mean = jnp.mean(grad, axis=-1, keepdims=True)
+        along = jnp.mean(grad * normed, axis=-1, keepdims=True)
+        gtok_ref[...] += (grad - mean - normed * along) * inv
+        loads[6].wait()
+        small_sums(w_ada_ref)
+
+        q_plane(1)
+        for quarter in range(4):
+            wait_send_unless(*r_copy(quarter))
+
+    pl.run_scoped(
+        heads,
+        VMEM((OWN, length, 128), BF16),
+        VMEM((OWN, length, 128), BF16),
+        VMEM((OWN, length, 128), BF16),
+        VMEM((length, D), BF16),
+        VMEM((D, WCOLS), BF16),
+        VMEM((length, 128), F32),
+        VMEM(w_ada_hbm.shape, BF16),
+        VMEM((length, WCOLS), BF16),
+        VMEM((64, length), F32),
+        VMEM((64, length), F32),
+        VMEM((D, 384), F32),
+        VMEM((4, half, D), F32),
+        VMEM((4, half, D), BF16),
+    )
+
+    for other in others(n):
+        wait_bytes(land_gc.at[other], gc_recv.at[other])
+    gcond_ref[...] = land_gc[0] + land_gc[1] + land_gc[2] + land_gc[3]
+    for row in range(8):
+        wait_bytes(land_s2.at[row], s2_recv.at[row])
+    packet_ref[...] = land_s2[...]
+    land_block[n] = block[...]
+    for other in others(n):
+        wait_bytes(land_block.at[other], ag_recv.at[other])
+    move = pltpu.make_async_copy(land_block, blocks_ref, load_sem.at[0])
+    move.start()
+    for p in range(2):
+        for g in range(4):
+            wait_bytes(bufs_q[p][3].at[g], qp_recv.at[p, g])
+    moves = [
+        move,
+        pltpu.make_async_copy(land_q_a, qkv_a_ref, load_sem.at[1]),
+        pltpu.make_async_copy(land_q_b, qkv_b_ref, load_sem.at[2]),
+    ]
+    for later in moves[1:]:
+        later.start()
+
+
+    for later in moves:
+        later.wait()
+    for head in range(HEADS):
+        wait_send_unless(*d_copy(head))
+    for copy in (one_x(), one_y(), two_x(), two_y(), qx_copy(0), qx_copy(1)):
+        copy.wait_send()
+
+    def drain(quarter, carry):
+        for p in range(2):
+            wait_send_unless(*qp_copy(p, quarter))
+        return carry
+
+    lax.fori_loop(0, 4, drain, 0)
+    for i in range(3):
+        other, chip = others(n)[i], others(z)[i]
+        b1_copy(chip).wait_send()
+        a2_copy(chip).wait_send()
+        b2_copy(other).wait_send()
+        ag_copy(other).wait_send()
+        qz_copy(0, chip).wait_send()
+        qz_copy(1, chip).wait_send()
+        s1_copy(other).wait_send()
+        gc_copy(other).wait_send()
+    for index in range(8):
+        wait_send_unless(*s2_copy(index))
+
+
+def call_fused(
+    docs, tokens, cot, att, cond, pat, gain_one, gain_two, b_up, b_down, w_ada, w_out, w_up, w_down,
+    q, k, v, everything, own, tab,
+):
+    local = tokens.shape[0]
+    half = local // 2
+    sds = jax.ShapeDtypeStruct
+    rest = ROWS_G - CUT
+    wide_a, wide_b = PARTS_Q[0][1], PARTS_Q[1][1]
+
+    def low(*shape):
+        return VMEM(shape, BF16)
+
+    return pl.pallas_call(
+        fused_kernel,
+        out_shape=(
+            sds((local, D), BF16),
+            sds((local, D), F32),
+            sds((4, ROWS_G, COLS_G), BF16),
+            sds((4, 96, wide_a), BF16),
+            sds((4, 96, wide_b), BF16),
+            sds((8, CHUNK, 128), F32),
+            sds((8, 128), F32),
+        ),
+        in_specs=[smem()] + [vm()] * 9 + [hbm()] * 10,
+        out_specs=(vm(), vm(), hbm(), hbm(), hbm(), vm(), vm()),
+        scratch_shapes=[
+            VMEM((8, SMALL), F32),
+            VMEM((8, 2 * D), F32),
+            low(HEADS, half, 128),
+            low(OWN, 4, half, 128),
+            low(4, 2, 2, ROWS_G, COLS_G),
+            low(4, 2, 2, ROWS_G, COLS_G),
+            low(2, 2, CUT, COLS_G),
+            low(2, 2, CUT, COLS_G),
+            low(2, CUT, COLS_G),
+            low(2, CUT, COLS_G),
+            low(3, 2, 2, rest, COLS_G),
+            low(3, CUT, COLS_G),
+            low(3, rest, COLS_G),
+            low(ROWS_G, COLS_G),
+            low(4, ROWS_G, COLS_G),
+            low(4, half, D),
+            low(2, local, D),
+            low(4, 2, 96, wide_a),
+            low(4, 2, 96, wide_b),
+            low(4, 96, wide_a),
+            low(4, 96, wide_b),
+            low(3, 96, wide_a),
+            low(3, 96, wide_b),
+            low(4, 96, wide_a),
+            low(4, 96, wide_b),
+            VMEM((8, CHUNK, 128), F32),
+            VMEM((4, 2, CHUNK, 128), F32),
+            VMEM((2, CHUNK, 128), F32),
+            VMEM((8, CHUNK, 128), F32),
+            VMEM((8, 128), F32),
+            VMEM((4, 8, 128), F32),
+            dma(7),
+            dma(HEADS),
+            dma(OWN, 4),
+            dma(9),
+            dma(9),
+            dma(4),
+            dma(4),
+            dma(3),
+            dma(3),
+            dma(3),
+            dma(3),
+            dma(3),
+            dma(3),
+            dma(3),
+            dma(4),
+            dma(4),
+            dma(4),
+            dma(4),
+            dma(2, 2),
+            dma(2, 2),
+            dma(2, 3),
+            dma(2, 3),
+            dma(2, 4),
+            dma(2, 4),
+            dma(3),
+            dma(4),
+            dma(8),
+            dma(8),
+            dma(3),
+            dma(4),
+        ],
+        compiler_params=params(3, 63),
+        cost_estimate=pl.CostEstimate(flops=4 * 10**10, bytes_accessed=5 * 10**7, transcendentals=10**7),
+    )(
+        docs, tokens, cot, att, cond, pat, gain_one, gain_two, b_up, b_down, w_ada, w_out, w_up, w_down,
+        q, k, v, everything, own, tab,
+    )
+
+
+def finish_kernel(
+    output_in, gtok_in, blocks, qkv_a, qkv_b, packet, output_out, gtok_out, gqkv, gout, gup, gdown, gada, gvec
+):
+    output_out[...] = output_in[...]
+    gtok_out[...] = gtok_in[...]
+    for part in range(4):
+        for hh in range(2):
+            at = part * 768 + hh * 384
+            gup[:, at : at + 384] = blocks[part, hh * 96 : (hh + 1) * 96, :].astype(F32)
+        rh, ch = part // 2, part % 2
+        gout[rh * 48 : (rh + 1) * 48, ch * 384 : (ch + 1) * 384] = blocks[part, 384:432, :].astype(F32)
+    for pair in range(2):
+        both = jnp.concatenate(
+            [blocks[2 * pair, 192:384, :], blocks[2 * pair + 1, 192:384, :]], axis=0
+        ).astype(F32)
+        gdown[:, pair * 384 : (pair + 1) * 384] = both.T
+
+    def head_block(part, head):
+        g, j = head // OWN, head % OWN
+        if part == 0:
+            at, upper = Q_AT[j] // 128 * 128, j % 2
+        else:
+            at, upper = KV_AT[j], part - 1
+        qkv, start = (qkv_a, 0) if at < PARTS_Q[1][0] else (qkv_b, PARTS_Q[1][0])
+        return qkv[g, :, at - start : at - start + 128].astype(F32), upper
+
+    for part in range(3):
+        for pair in range(HEADS // 2):
+            even, up = head_block(part, 2 * pair)
+            even = pltpu.roll(even, 64, 1) if up else even
+            odd, up = head_block(part, 2 * pair + 1)
+            odd = odd if up else pltpu.roll(odd, 64, 1)
+            at = part * D + pair * 128
+            gqkv[:, at : at + 128] = jnp.where(lane(even.shape) < 64, even, odd)
+
+    conds = [packet[:, 19, :], packet[:, 20, :]]
+    lhs = jnp.concatenate([conds[0]] * 3 + [conds[1]] * 3, axis=0).astype(BF16)
+    for k in range(6):
+        first, second = packet[:, k, :], packet[:, 6 + k, :]
+        rhs = jnp.concatenate([*split3(first), *split3(second)], axis=0).astype(BF16)
+        gada[:, 96 * k : 96 * k + 96] = dg(lhs, rhs, TN)[:, :96]
+        gvec[0:1, 96 * k : 96 * k + 96] = jnp.sum(first + second, axis=0, keepdims=True)[:, :96]
+    for row, at, k in ((1, 0, 12), (2, 0, 13), (3, 0, 14), (3, 1, 15), (3, 2, 16), (3, 3, 17), (4, 0, 18)):
+        gvec[row : row + 1, 96 * at : 96 * at + 96] = jnp.sum(packet[:, k, :], axis=0, keepdims=True)[
+            :, :96
+        ]
+
+
+def call_finish(output, gtok, blocks, qkv_a, qkv_b, packet):
+    local = output.shape[0]
+    sds = jax.ShapeDtypeStruct
+    return pl.pallas_call(
+        finish_kernel,
+        out_shape=(
+            sds((local, D), BF16),
+            sds((local, D), F32),
+            sds((96, 3 * D), F32),
+            sds((96, D), F32),
+            sds((96, FF), F32),
+            sds((384, D), F32),
+            sds((128, 576), F32),
+            sds((8, 576), F32),
+        ),
+        in_specs=[vm()] * 6,
+        out_specs=(vm(),) * 8,
+        compiler_params=pltpu.CompilerParams(vmem_limit_bytes=40 * 2**20),
+        cost_estimate=pl.CostEstimate(flops=10**7, bytes_accessed=10**7, transcendentals=0),
+    )(output, gtok, blocks, qkv_a, qkv_b, packet)
+
+
+def plain_backward_kernel(
     tokens_ref,
     pat_ref,
     gain_ref,
@@ -674,7 +1614,7 @@
             scores = (gprobs - probs * jnp.sum(gprobs, axis=1, keepdims=True)).astype(BF16)
             probs = probs.astype(BF16)
             gquery = rounded(dg(scores, k_ref[j], NN) * HEAD_DIM**-0.5)
-            at = 384 + 64 * j
+            at = Q_AT[j]
             packed[rows, at : at + 64] = turned(gquery, rows)[:, :64].astype(BF16)
             acc_v[...] += dg(grad.T[:64], probs, NN)
             acc_k[...] += dg(query.T[:64], scores, NN)
@@ -686,7 +1626,7 @@
             rows = pl.ds(pl.multiple_of(i * local, local), local)
             both = jnp.concatenate([acc_k[:, rows], acc_v[:, rows]], axis=0).T
             both = rounded(both)
-            packed[rows, j * 128 : (j + 1) * 128] = jnp.where(
+            packed[rows, KV_AT[j] : KV_AT[j] + 128] = jnp.where(
                 lanes < 64, turned(both, rows), both
             ).astype(BF16)
             return carry
@@ -772,13 +1712,13 @@
     lax.fori_loop(0, 4, drain, 0)
 
 
-def call_backward(tokens, pat, gain, gmid, do, q, k, v, everything, own, tab):
+def call_plain_backward(tokens, pat, gain, gmid, do, q, k, v, everything, own, tab):
     local = tokens.shape[0]
     half = local // 2
     length = 4 * local
     sds = jax.ShapeDtypeStruct
     return pl.pallas_call(
-        backward_kernel,
+        plain_backward_kernel,
         out_shape=(
             sds((local, D), F32),
             sds((8, 96, WCOLS), BF16),
@@ -812,9 +1752,9 @@
     down = g[:, :, 192:384].reshape(8, D, 384).transpose(0, 2, 1).reshape(FF, D)
     out = g[:, :, 384:].reshape(8, 2, 2, 48, 384).transpose(0, 1, 3, 2, 4).reshape(D, D)
     flat = gq.reshape(D, WCOLS)
-    pieces = [flat[:, 384:576]]
-    pieces.append(jnp.concatenate([flat[:, j * 128 : j * 128 + 64] for j in range(OWN)], axis=1))
-    pieces.append(jnp.concatenate([flat[:, j * 128 + 64 : j * 128 + 128] for j in range(OWN)], axis=1))
+    pieces = []
+    for starts in (Q_AT, KV_AT, [at + HEAD_DIM for at in KV_AT]):
+        pieces.append(jnp.concatenate([flat[:, at : at + HEAD_DIM] for at in starts], axis=1))
     group = 2 * (n // 2) + c
     whole = jnp.zeros((D, 3, 4, OWN * HEAD_DIM), F32)
     for part in range(3):
@@ -858,10 +1798,34 @@
     att, everything, q, k, v, pat, own, tab = call_forward(
         docs_per_row, x, cond, w_ada, line(b_ada), line(gain_one), w_qkv, table
     )
+    if (lax.axis_size("narrow"), lax.axis_size("wide")) == (4, 8):
+        output, gtok, blocks, qkv_a, qkv_b, packet, gcond = call_fused(
+            docs_per_row, x, cot, att, cond, pat, line(gain_one), line(gain_two), line(b_up),
+            line(b_down), w_ada, w_out, w_up, w_down, q, k, v, everything, own, tab,
+        )
+        output, gtok, gqkv, gout, gup, gdown, gada, gvec = call_finish(
+            output, gtok, blocks, qkv_a, qkv_b, packet
+        )
+        return (
+            output[None],
+            gtok[None],
+            gcond[None, :DOCS],
+            gada,
+            gvec[0],
+            gvec[1, :96],
+            gqkv,
+            gout,
+            gvec[2, :96],
+            gup,
+            gvec[3, :384],
+            gdown,
+            gvec[4, :96],
+        )
+
     output, gmid, g, small_two, do = call_middle(
         x, cot, att, pat, line(gain_two), w_out, w_up, line(b_up), w_down, line(b_down)
     )
-    gtok, gq, small_one = call_backward(
+    gtok, gq, small_one = call_plain_backward(
         x, pat, line(gain_one), gmid, do, q, k, v, everything, own, tab
     )
     n, w = lax.axis_index("narrow"), lax.axis_index("wide")

time: 706 us -> 229 us (0.32); the launches traced: 695 us -> 228 us
  waiting for transfers between devices: 362 us -> 0 us
  local copies, waits for them, and re-layouts: 86.4 us -> 16.9 us
  Pallas kernels: 176 us -> 210 us
  blocking collectives: 30.9 us -> 0 us
  between operations: 17.2 us -> 1.32 us
  other arithmetic: 15.8 us -> 0 us
    reduce_scatter x4 -> x0, waiting for transfers between devices: 235 us -> none  [the longest x3 235 us: total(): lax.psum_scatter(values.astype(F32), 'wide', scatter_dimension=0, tiled=T...]
    psum x1 -> x0, waiting for transfers between devices: 102 us -> none  [body(): small = lax.psum(small, 'narrow')]
    convert_element_type x4 -> x0, local copies, waits for them, and re-layouts: 35 us -> none  [total(): values.astype(F32)]
    pallas_call x2, Pallas kernels: 116 us -> 150 us  [the longest x1 147 us: call_fused(): pl.pallas_call(fused_kernel, out_shape=(sds((local, D), BF16), sds((local...]
    unnamed x1 -> x0, blocking collectives: 30.9 us -> none
    unnamed x7 -> x0, waiting for transfers between devices: 24.6 us -> none
    unnamed x52 -> x13, local copies, waits for them, and re-layouts: 29.2 us -> 7.5 us
    slice x5 -> x2, local copies, waits for them, and re-layouts: 12.1 us -> 1.2 us  [the longest x1 0.6 us: body(): gvec[0]]
  transfers between devices with their start and end apart: 6 -> 0, of which waited for: 5 -> 0; matrix products, arithmetic and copies ran while one was open for 10% -> 0% of each run, Pallas kernels for 0% -> 0%
where the time goes in v3:
time: 229 us; the launch traced here: 228 us
  Pallas kernels  210 us (92%)
  local copies, waits for them, and re-layouts  16.9 us (7%)
    pallas_call x1, Pallas kernels, call_fused(): pl.pallas_call(fused_kernel, out_shape=(sds((local, D), BF16), sds((local...  147 us
    pallas_call x1, Pallas kernels, call_forward(): pl.pallas_call(forward_kernel, out_shape=(sds((local, D), BF16), sds((len...  59.3 us
    unnamed x13, local copies, waits for them, and re-layouts  7.5 us
    reshape x5, local copies, waits for them, and re-layouts, line(): return vector.reshape(1, -1)  6.4 us

profile of v3, /device:TPU:0, one launch (start us, length us, event | category | flops | bytes accessed | tf_op | source)
XLA Modules:
  0.0 227.9 jit_solution(1640207208118360238)
XLA Ops:
  1.3 1.3 reshape.55.gain_ref.gain_one_ref
  2.6 1.3 reshape.56.gain_ref
  3.8 1.3 reshape.58.b_down_ref
  5.1 1.3 reshape.57.b_up_ref
  6.4 1.3 reshape.54.b_ada_ref
  7.7 59.3 %shard_map.246 = (bf16[512,768]{1,0:T(8,128)(2,1)}, bf16[2048,768]{1,0:T(8,128)(2,1)}, bf16[3,2048,128]{2,1,0:T(8,128)(2,1)}, bf16[3,2048,128]{2,1,0:T(8,128)(2,...) custom-call(s32[1]{0:T(128)S(6)} %copy.29.docs_ref, ...), custom_call_target="tpu_custom_call" | custom-call | flops 10000000000 | bytes 20000000 | tf_op jit(solution)/shard_map/pallas_call | solution.py:387
  67.0 147.2 %shard_map.247 = (bf16[512,768]{1,0:T(8,128)(2,1)}, f32[512,768]{1,0:T(8,128)}, bf16[4,432,384]{2,1,0:T(8,128)(2,1)}, bf16[4,96,384]{2,1,0:T(8,128)(2,1)}, bf16[...) custom-call(s32[1]{0:T(128)S(6)} %copy.29.docs_ref, bf16[512,768]{1,0:T(8,128)(2,1)} %bitcast.15, ...), custom_call_target="tpu_custom_call" | custom-call | flops 40000000000 | bytes 50000000 | tf_op jit(solution)/shard_map/pallas_call | solution.py:1405
  214.2 1.2 slice_bitcast_fusion
  215.5 0.0 copy-start
  215.5 1.4 copy-done
  216.9 0.0 copy-start.1
  216.9 1.3 copy-done.1
  218.2 0.0 copy-start.2
  218.2 1.1 copy-done.2
  219.3 0.0 copy-start.3
  219.3 1.0 copy-done.3
  220.3 0.0 copy-start.4
  220.3 0.9 copy-done.4
  221.2 0.0 copy-start.5
  221.2 0.9 copy-done.5
  222.1 3.2 %shard_map.248 = (bf16[512,768]{1,0:T(8,128)(2,1)}, f32[512,768]{1,0:T(8,128)}, f32[96,2304]{1,0:T(8,128)}, f32[96,768]{1,0:T(8,128)}, f32[96,3072]{1,0:T(8,128)...) custom-call(bf16[512,768]{1,0:T(8,128)(2,1)S(1)} %copy-done.2, f32[512,768]{1,0:T(8,128)S(1)} %copy-done, ...), custom_call_target="tpu_custom_call" | custom-call | flops 10000000 | bytes 10000000 | tf_op jit(solution)/shard_map/pallas_call | solution.py:1540
  225.4 0.5 slice_bitcast_fusion.1
  225.9 0.6 slice_reduce_fusion.1
  226.5 0.6 slice_reduce_fusion
  227.1 0.9 copy.28
Async XLA Ops:
  215.5 1.4 copy-start
  216.9 1.3 copy-start.1
  218.2 1.1 copy-start.2
  219.3 1.0 copy-start.3
  220.3 0.9 copy-start.4
  221.2 0.9 copy-start.5

commit v4 on v3

--- a/solution.py
+++ b/solution.py
@@ -81,6 +81,10 @@
 
 def wait_bytes(ref, sem):
     pltpu.make_async_copy(ref, ref, sem).wait()
+
+
+def row_of(ref):
+    return ref[...].astype(F32).reshape(1, ref.shape[0])
 
 
 def lane(shape):
@@ -183,10 +187,10 @@
     odd = jnp.logical_and(parity == 1, two)
     cond = cond_ref[...].astype(F32)
     cond16 = jnp.where(odd, cond[1:2, :], cond[0:1, :]).astype(BF16)
-    pat_ref[...] = dg(cond16, w_ada_ref[...], NN)[:8] + b_ada_ref[...].astype(F32)
+    pat_ref[...] = dg(cond16, w_ada_ref[...], NN)[:8] + row_of(b_ada_ref)
 
     shift = pat_ref[:, 0:D]
-    amp = gain_ref[...].astype(F32) * (1.0 + pat_ref[:, D : 2 * D])
+    amp = row_of(gain_ref) * (1.0 + pat_ref[:, D : 2 * D])
 
     def a_copy(my, hh):
         target = 2 * my + c
@@ -481,15 +485,15 @@
     branch_ref[...] = dg(att_ref[...], w_out_ref[...], NN)
     middle = tokens_ref[...].astype(F32) + spread(branch_ref[...], piece(2))
     middle_ref[...] = middle
-    amp = gain_ref[...].astype(F32) * (1.0 + piece(4))
+    amp = row_of(gain_ref) * (1.0 + piece(4))
     normed, _ = norm_stats(middle)
     second = flat8(by8(normed) * amp[None] + piece(3)[None]).astype(BF16)
     second_ref[...] = second
-    down_ref[...] = jnp.broadcast_to(b_down_ref[...].astype(F32), down_ref.shape)
+    down_ref[...] = jnp.broadcast_to(row_of(b_down_ref), down_ref.shape)
 
     def up(t, carry):
         cols = pl.ds(pl.multiple_of(t * tile, tile), tile)
-        hidden = dg(second_ref[...], w_up_ref[:, cols], NN) + b_up_ref[:, cols].astype(F32)
+        hidden = dg(second_ref[...], w_up_ref[:, cols], NN) + b_up_ref[cols].astype(F32).reshape(1, tile)
         square = hidden * hidden
         bend = jnp.tanh(0.7978845608028654 * hidden * (1.0 + 0.044715 * square))
         part = 0.5 * (1.0 + bend)
@@ -535,7 +539,7 @@
     gsecond = gsecond_ref[...]
     small_ref[:, D : 2 * D] = sum8(gsecond)
     small_ref[:, 2 * D : 3 * D] = sum8(gsecond * normed)
-    amp = gain_ref[...].astype(F32) * (1.0 + piece(4))
+    amp = row_of(gain_ref) * (1.0 + piece(4))
     grad = spread(gsecond, amp)
     mean = jnp.mean(grad, axis=-1, keepdims=True)
     along = jnp.mean(grad * normed, axis=-1, keepdims=True)
@@ -811,15 +815,15 @@
             return tokens_ref[...].astype(F32) + spread(branch_ref[...], piece(2))
 
         normed, _ = norm_stats(middle_values())
-        amp = gain_ref[...].astype(F32) * (1.0 + piece(4))
+        amp = row_of(gain_ref) * (1.0 + piece(4))
         low_ref[...] = flat8(by8(normed) * amp[None] + piece(3)[None]).astype(BF16)
-        acc[...] = jnp.broadcast_to(b_down_ref[...].astype(F32), acc.shape)
+        acc[...] = jnp.broadcast_to(row_of(b_down_ref), acc.shape)
         loads[1].wait()
         loads[2].wait()
 
         def up(t, carry):
             cols = pl.ds(pl.multiple_of(t * tile, tile), tile)
-            hidden = dg(low_ref[...], w_up[:, cols], NN) + b_up_ref[:, cols].astype(F32)
+            hidden = dg(low_ref[...], w_up[:, cols], NN) + b_up_ref[cols].astype(F32).reshape(1, tile)
             square = hidden * hidden
             bend = jnp.tanh(0.7978845608028654 * hidden * (1.0 + 0.044715 * square))
             part = 0.5 * (1.0 + bend)
@@ -842,6 +846,7 @@
         small_ref[:, 4 * D + FF :] = sum8(gdown.astype(F32))
         lhs_t[1] = gdown.T
         acc[...] = jnp.zeros_like(acc)
+        pl.semaphore_wait(barrier, jnp.where(z == n, 17, 18))
 
         def back(t, carry):
             cols = pl.ds(pl.multiple_of(t * tile, tile), tile)
@@ -871,7 +876,7 @@
         gsecond = acc[...]
         small_ref[:, D : 2 * D] = sum8(gsecond)
         small_ref[:, 2 * D : 3 * D] = sum8(gsecond * normed)
-        grad = spread(gsecond, gain_ref[...].astype(F32) * (1.0 + piece(4)))
+        grad = spread(gsecond, row_of(gain_ref) * (1.0 + piece(4)))
         mean = jnp.mean(grad, axis=-1, keepdims=True)
         along = jnp.mean(grad * normed, axis=-1, keepdims=True)
         gmid = cot_ref[...].astype(F32) + (grad - mean - normed * along) * inv
@@ -900,7 +905,6 @@
             core_down(g_give, t).wait_send()
         core_out(g_give).wait_send()
 
-    pl.semaphore_wait(barrier, jnp.where(z == n, 17, 18))
     pl.run_scoped(
         middle,
         VMEM((D, D), BF16),
@@ -1125,7 +1129,7 @@
                 gain_sum = even * (1.0 + scale[0:1]) + odd * (1.0 + scale[1:2])
                 for s in range(8):
                     put(s, 12 if piece == 1 else 13, gain_sum, s)
-                gain = gains[piece][...].astype(F32)
+                gain = row_of(gains[piece])
                 even, odd = even * gain, odd * gain
             first_doc = jnp.where(two, even, even + odd)
             second_doc = jnp.where(two, odd, 0.0)
@@ -1149,6 +1153,7 @@
         for other in others(n):
             s1_copy(other).start()
             gc_copy(other).start()
+        last()
         land_gc[n] = gc_mine[...]
         land_s1[n] = pack[pl.ds(2 * n, 2)]
         for other in others(n):
@@ -1228,7 +1233,7 @@
             gq[...] = acc_w[:, 0:width].astype(BF16).reshape(gq.shape)
             qx_copy(p).start()
 
-        hooks = {(1, 4): stage_two, (2, 2): stage_a2, (2, 4): stage_b2, (2, 6): lambda: q_z(0)}
+        hooks = {(1, 6): stage_two, (2, 4): stage_a2, (2, 5): stage_b2, (2, 7): lambda: q_z(0)}
         for j in range(OWN):
             for quarter in range(4):
                 wait_bytes(dland.at[j, quarter], d_recv.at[j, quarter])
@@ -1300,10 +1305,9 @@
 
         lax.fori_loop(0, 4, add, 0)
         weights(1)
-        last()
-        q_z(1)
         normed, inv = norm_stats(tokens_ref[...].astype(F32))
         q_plane(0)
+        q_z(1)
 
         for y in range(2):
             for hh in range(2):
@@ -1311,7 +1315,7 @@
         gfirst = rland[0].astype(F32) + rland[1].astype(F32)
         small_one[:, 0:D] = sum8(gfirst)
         small_one[:, D : 2 * D] = sum8(gfirst * normed)
-        grad = spread(gfirst, gain_one_ref[...].astype(F32) * (1.0 + piece(1)))
+        grad = spread(gfirst, row_of(gain_one_ref) * (1.0 + piece(1)))
         mean = jnp.mean(grad, axis=-1, keepdims=True)
         along = jnp.mean(grad * normed, axis=-1, keepdims=True)
         gtok_ref[...] += (grad - mean - normed * along) * inv
@@ -1487,10 +1491,16 @@
 
 
 def finish_kernel(
-    output_in, gtok_in, blocks, qkv_a, qkv_b, packet, output_out, gtok_out, gqkv, gout, gup, gdown, gada, gvec
+    output_in, gtok_in, blocks, qkv_a, qkv_b, packet, gcond_in, output_out, gtok_out, gcond_out, gqkv, gout, gup, gdown, gada, gvec_ada,
+    gvec_one, gvec_two, gvec_up, gvec_down, wide, pass_sem
 ):
-    output_out[...] = output_in[...]
-    gtok_out[...] = gtok_in[...]
+    passed = [
+        pltpu.make_async_copy(output_in, output_out, pass_sem.at[0]),
+        pltpu.make_async_copy(gtok_in, gtok_out, pass_sem.at[1]),
+    ]
+    for copy in passed:
+        copy.start()
+    gcond_out[0] = gcond_in[0:DOCS]
     for part in range(4):
         for hh in range(2):
             at = part * 768 + hh * 384
@@ -1526,15 +1536,19 @@
     for k in range(6):
         first, second = packet[:, k, :], packet[:, 6 + k, :]
         rhs = jnp.concatenate([*split3(first), *split3(second)], axis=0).astype(BF16)
-        gada[:, 96 * k : 96 * k + 96] = dg(lhs, rhs, TN)[:, :96]
-        gvec[0:1, 96 * k : 96 * k + 96] = jnp.sum(first + second, axis=0, keepdims=True)[:, :96]
+        gada[96 * k : 96 * k + 96, :] = dg(rhs, lhs, TN)[:96]
+        wide[0:1, 96 * k : 96 * k + 96] = jnp.sum(first + second, axis=0, keepdims=True)[:, :96]
     for row, at, k in ((1, 0, 12), (2, 0, 13), (3, 0, 14), (3, 1, 15), (3, 2, 16), (3, 3, 17), (4, 0, 18)):
-        gvec[row : row + 1, 96 * at : 96 * at + 96] = jnp.sum(packet[:, k, :], axis=0, keepdims=True)[
+        wide[row : row + 1, 96 * at : 96 * at + 96] = jnp.sum(packet[:, k, :], axis=0, keepdims=True)[
             :, :96
         ]
-
-
-def call_finish(output, gtok, blocks, qkv_a, qkv_b, packet):
+    for ref, row in ((gvec_ada, 0), (gvec_one, 1), (gvec_two, 2), (gvec_up, 3), (gvec_down, 4)):
+        ref[...] = wide[row : row + 1, 0 : ref.shape[0]].reshape(ref.shape)
+    for copy in passed:
+        copy.wait()
+
+
+def call_finish(output, gtok, blocks, qkv_a, qkv_b, packet, gcond):
     local = output.shape[0]
     sds = jax.ShapeDtypeStruct
     return pl.pallas_call(
@@ -1542,18 +1556,24 @@
         out_shape=(
             sds((local, D), BF16),
             sds((local, D), F32),
+            sds((1, DOCS, 128), F32),
             sds((96, 3 * D), F32),
             sds((96, D), F32),
             sds((96, FF), F32),
             sds((384, D), F32),
-            sds((128, 576), F32),
-            sds((8, 576), F32),
+            sds((576, 128), F32),
+            sds((576,), F32),
+            sds((96,), F32),
+            sds((96,), F32),
+            sds((384,), F32),
+            sds((96,), F32),
         ),
-        in_specs=[vm()] * 6,
-        out_specs=(vm(),) * 8,
-        compiler_params=pltpu.CompilerParams(vmem_limit_bytes=40 * 2**20),
+        in_specs=[vm()] * 7,
+        out_specs=(hbm(), hbm()) + (vm(),) * 11,
+        scratch_shapes=[VMEM((8, 576), F32), dma(2)],
+        compiler_params=pltpu.CompilerParams(vmem_limit_bytes=62 * 2**20),
         cost_estimate=pl.CostEstimate(flops=10**7, bytes_accessed=10**7, transcendentals=0),
-    )(output, gtok, blocks, qkv_a, qkv_b, packet)
+    )(output, gtok, blocks, qkv_a, qkv_b, packet, gcond)
 
 
 def plain_backward_kernel(
@@ -1698,7 +1718,7 @@
     gfirst = rland[0].astype(F32) + rland[1].astype(F32)
     small_ref[:, 0:D] = sum8(gfirst)
     small_ref[:, D : 2 * D] = sum8(gfirst * normed)
-    amp = gain_ref[...].astype(F32) * (1.0 + pat_ref[:, D : 2 * D])
+    amp = row_of(gain_ref) * (1.0 + pat_ref[:, D : 2 * D])
     grad = flat8(by8(gfirst) * amp[None])
     mean = jnp.mean(grad, axis=-1, keepdims=True)
     along = jnp.mean(grad * normed, axis=-1, keepdims=True)
@@ -1792,41 +1812,39 @@
     cond = condition.reshape(DOCS, -1)
     table = jnp.asarray(rotary_table(4 * local))
 
-    def line(vector):
-        return vector.reshape(1, -1)
-
     att, everything, q, k, v, pat, own, tab = call_forward(
-        docs_per_row, x, cond, w_ada, line(b_ada), line(gain_one), w_qkv, table
+        docs_per_row, x, cond, w_ada, b_ada, gain_one, w_qkv, table
     )
     if (lax.axis_size("narrow"), lax.axis_size("wide")) == (4, 8):
         output, gtok, blocks, qkv_a, qkv_b, packet, gcond = call_fused(
-            docs_per_row, x, cot, att, cond, pat, line(gain_one), line(gain_two), line(b_up),
-            line(b_down), w_ada, w_out, w_up, w_down, q, k, v, everything, own, tab,
-        )
-        output, gtok, gqkv, gout, gup, gdown, gada, gvec = call_finish(
-            output, gtok, blocks, qkv_a, qkv_b, packet
-        )
+            docs_per_row, x, cot, att, cond, pat, gain_one, gain_two, b_up,
+            b_down, w_ada, w_out, w_up, w_down, q, k, v, everything, own, tab,
+        )
+        output, gtok, gcond, gqkv, gout, gup, gdown, gada, *vectors = call_finish(
+            output, gtok, blocks, qkv_a, qkv_b, packet, gcond
+        )
+        gvec_ada, gvec_one, gvec_two, gvec_up, gvec_down = vectors
         return (
             output[None],
             gtok[None],
-            gcond[None, :DOCS],
-            gada,
-            gvec[0],
-            gvec[1, :96],
+            gcond,
+            gada.T,
+            gvec_ada,
+            gvec_one,
             gqkv,
             gout,
-            gvec[2, :96],
+            gvec_two,
             gup,
-            gvec[3, :384],
+            gvec_up,
             gdown,
-            gvec[4, :96],
+            gvec_down,
         )
 
     output, gmid, g, small_two, do = call_middle(
-        x, cot, att, pat, line(gain_two), w_out, w_up, line(b_up), w_down, line(b_down)
+        x, cot, att, pat, gain_two, w_out, w_up, b_up, w_down, b_down
     )
     gtok, gq, small_one = call_plain_backward(
-        x, pat, line(gain_one), gmid, do, q, k, v, everything, own, tab
+        x, pat, gain_one, gmid, do, q, k, v, everything, own, tab
     )
     n, w = lax.axis_index("narrow"), lax.axis_index("wide")
     sum_qkv, sum_out, sum_up, sum_down = plain_sums(g, gq, (n, w // 2, w % 2))

time: 229 us -> 205 us (0.90)
  local copies, waits for them, and re-layouts: 16.9 us -> 0 us
  Pallas kernels: 210 us -> 203 us
    pallas_call x1, Pallas kernels: 147 us -> 137 us  [call_fused(): pl.pallas_call(fused_kernel, out_shape=(sds((local, D), BF16), sds((local...]
    unnamed x13 -> x0, local copies, waits for them, and re-layouts: 7.5 us -> none
    reshape x5 -> x0, local copies, waits for them, and re-layouts: 6.4 us -> none  [line(): return vector.reshape(1, -1)]
    pallas_call x1, Pallas kernels: 3.22 us -> 5.55 us  [call_finish(): pl.pallas_call(finish_kernel, out_shape=(sds((local, D), BF16), sds((loca...]
where the time goes in v4:
time: 205 us; the launch traced here: 204 us
  Pallas kernels  203 us (99%)
    pallas_call x1, Pallas kernels, call_fused(): pl.pallas_call(fused_kernel, out_shape=(sds((local, D), BF16), sds((local...  137 us
    pallas_call x1, Pallas kernels, call_forward(): pl.pallas_call(forward_kernel, out_shape=(sds((local, D), BF16), sds((len...  59.7 us
    pallas_call x1, Pallas kernels, call_finish(): pl.pallas_call(finish_kernel, out_shape=(sds((local, D), BF16), sds((loca...  5.55 us

profile of v4, /device:TPU:0, one launch (start us, length us, event | category | flops | bytes accessed | tf_op | source)
XLA Modules:
  0.0 204.1 jit_solution(16456244454553038188)
XLA Ops:
  1.3 59.7 %shard_map.246 = (bf16[512,768]{1,0:T(8,128)(2,1)}, bf16[2048,768]{1,0:T(8,128)(2,1)}, bf16[3,2048,128]{2,1,0:T(8,128)(2,1)}, bf16[3,2048,128]{2,1,0:T(8,128)(2,...) custom-call(s32[1]{0:T(128)S(6)} %copy.28.docs_ref, ...), custom_call_target="tpu_custom_call" | custom-call | flops 10000000000 | bytes 20000000 | tf_op jit(solution)/shard_map/pallas_call | solution.py:391
  61.0 137.4 %shard_map.247 = (bf16[512,768]{1,0:T(8,128)(2,1)}, f32[512,768]{1,0:T(8,128)}, bf16[4,432,384]{2,1,0:T(8,128)(2,1)}, bf16[4,96,384]{2,1,0:T(8,128)(2,1)}, bf16[...) custom-call(s32[1]{0:T(128)S(6)} %copy.28.docs_ref, bf16[512,768]{1,0:T(8,128)(2,1)} %bitcast.8, ...), custom_call_target="tpu_custom_call" | custom-call | flops 40000000000 | bytes 50000000 | tf_op jit(solution)/shard_map/pallas_call | solution.py:1409
  198.4 5.6 %shard_map.248 = (bf16[512,768]{1,0:T(8,128)(2,1)}, f32[512,768]{1,0:T(8,128)}, f32[1,2,128]{2,1,0:T(2,128)}, f32[96,2304]{1,0:T(8,128)}, f32[96,768]{1,0:T(8,12...) custom-call(bf16[512,768]{1,0:T(8,128)(2,1)} %get-tuple-element.49.o, ...), custom_call_target="tpu_custom_call" | custom-call | flops 10000000 | bytes 10000000 | tf_op jit(solution)/shard_map/pallas_call | solution.py:1554

commit v5 on v4

--- a/solution.py
+++ b/solution.py
@@ -46,7 +46,7 @@
     return (n, 2 * z + 1 - c)
 
 
-def plane_barrier(n, z, c):
+def plane_barrier(n, z, c, wait=True):
     barrier = pltpu.get_barrier_semaphore()
     me = n * 2 + c
     for step in range(1, 8):
@@ -54,7 +54,8 @@
         pl.semaphore_signal(
             barrier, inc=1, device_id=(other // 2, 2 * z + lax.rem(other, 2)), device_id_type=MESH
         )
-    pl.semaphore_wait(barrier, 7)
+    if wait:
+        pl.semaphore_wait(barrier, 7)
 
 
 def remote(src, dst, send, recv, device):
@@ -142,11 +143,16 @@
     w_qkv_hbm,
     table_hbm,
     att_ref,
-    all_ref,
+    all_hbm,
+    q_hbm,
+    k_hbm,
+    v_hbm,
+    pat_ref,
+    own_hbm,
+    tab_hbm,
     q_ref,
     k_ref,
     v_ref,
-    pat_ref,
     own_ref,
     tab_ref,
     mine,
@@ -165,7 +171,7 @@
     f_recv,
     o_send,
     o_recv,
-    all_sem,
+    keep_sem,
 ):
     n, ny, nx, z, c = place()
     local = tokens_ref.shape[0]
@@ -178,9 +184,8 @@
     for load in loads:
         load.start()
     docs_mine[...] = jnp.full(docs_mine.shape, docs_ref[0], jnp.int32).astype(F32)
-    plane_barrier(n, z, c)
+    plane_barrier(n, z, c, wait=False)
     docs_copy = remote(docs_mine, docs_other, docs_sem.at[0], docs_sem.at[1], sibling(n, z, c))
-    docs_copy.start()
 
     two = docs_ref[0] == DOCS
     parity = lax.rem(lax.broadcasted_iota(jnp.int32, (16, 128), 0), 2)
@@ -209,6 +214,9 @@
         mine[hh * half : (hh + 1) * half, :] = flat8(by8(normed) * amp[None] + shift[None]).astype(
             BF16
         )
+        if hh == 0:
+            pl.semaphore_wait(pltpu.get_barrier_semaphore(), 7)
+            docs_copy.start()
         for my in range(2):
             send_or_keep(*a_copy(my, hh))
 
@@ -291,8 +299,21 @@
     forward(sources[3])
     arrive(sources[2])
     arrive(sources[3])
-    keep = pltpu.make_async_copy(gathered, all_ref, all_sem)
-    keep.start()
+    keeps = [
+        pltpu.make_async_copy(src, dst, keep_sem.at[i])
+        for i, (src, dst) in enumerate(
+            (
+                (gathered, all_hbm),
+                (k_ref, k_hbm),
+                (v_ref, v_hbm),
+                (own_ref, own_hbm),
+                (tab_ref, tab_hbm),
+                (q_ref, q_hbm),
+            )
+        )
+    ]
+    for keep in keeps[:5]:
+        keep.start()
 
     def o_copy(j, quarter):
         is_self = jnp.logical_and(quarter == n, nx == c)
@@ -334,6 +355,7 @@
         return carry
 
     lax.fori_loop(0, OWN * 4, attend, 0)
+    keeps[5].start()
 
     for head in range(HEADS):
         wait_bytes(oland.at[head], o_recv.at[head])
@@ -358,7 +380,8 @@
         return carry
 
     lax.fori_loop(0, OWN * 4, drain, 0)
-    keep.wait()
+    for keep in keeps:
+        keep.wait()
 
 
 def vm():
@@ -401,8 +424,13 @@
             sds((length, 128), F32),
         ),
         in_specs=[smem(), vm(), vm(), vm(), vm(), vm(), hbm(), hbm()],
-        out_specs=(vm(), hbm(), vm(), vm(), vm(), vm(), vm(), vm()),
+        out_specs=(vm(), hbm(), hbm(), hbm(), hbm(), vm(), hbm(), hbm()),
         scratch_shapes=[
+            VMEM((OWN, length, 128), BF16),
+            VMEM((OWN, length, 128), BF16),
+            VMEM((OWN, length, 128), BF16),
+            VMEM((D, WCOLS), BF16),
+            VMEM((length, 128), F32),
             VMEM((local, D), BF16),
             VMEM((length, D), BF16),
             VMEM((D, 3 * D), BF16),
@@ -419,7 +447,7 @@
             dma(4),
             dma(OWN, 4),
             dma(HEADS),
-            pltpu.SemaphoreType.DMA,
+            dma(6),
         ],
         compiler_params=params(0),
         cost_estimate=pl.CostEstimate(flops=10**10, bytes_accessed=2 * 10**7, transcendentals=10**7),
@@ -894,9 +922,9 @@
             for g in range(4):
                 send_or_keep(*d_copy(g * OWN + j))
 
+        both = dg(att_ref[...], gbranch, TN).astype(BF16)
         for hh in range(2):
-            gout = dg(att_ref[...], gbranch[:, hh * 384 : (hh + 1) * 384], TN).astype(BF16)
-            shaped = gout.reshape(4, 2, 2, 48, 384)
+            shaped = both[:, hh * 384 : (hh + 1) * 384].reshape(4, 2, 2, 48, 384)
             g_own[:, :, hh, 384:432, :] = jnp.where(c == 0, shaped[:, 0], shaped[:, 1])
             g_give[:, :, hh, 384:432, :] = jnp.where(c == 0, shaped[:, 1], shaped[:, 0])
         core_out(g_give).start()
@@ -1098,7 +1126,7 @@
             (other, 2 * n + i),
         )
 
-    def small_sums(w_ada_ref):
+    def small_part(w_ada_ref, pieces_now):
 
         two = docs_ref[0] == DOCS
         even_rows = lax.rem(lax.broadcasted_iota(jnp.int32, (8, D), 0), 2) == 0
@@ -1107,8 +1135,6 @@
             even = jnp.sum(jnp.where(even_rows, values, 0.0), axis=0, keepdims=True)
             return even, jnp.sum(jnp.where(even_rows, 0.0, values), axis=0, keepdims=True)
 
-        pack[...] = jnp.zeros_like(pack)
-        gc_mine[...] = jnp.zeros_like(gc_mine)
 
         def put(chunk, row, values, s):
             pack[chunk, row : row + 1, 0:96] = values[:, 96 * s : 96 * s + 96]
@@ -1122,7 +1148,7 @@
             small_ref[:, 3 * D : 4 * D],
         ]
         gains = {1: gain_one_ref, 4: gain_ref}
-        for piece in range(6):
+        for piece in pieces_now:
             even, odd = even_odd(raws[piece])
             if piece in gains:
                 scale = pat_ref[:, piece * D : (piece + 1) * D]
@@ -1137,11 +1163,16 @@
                 at = 8 * piece + s
                 put(at // 6, at % 6, first_doc, s)
                 put(at // 6, 6 + at % 6, second_doc, s)
-            pieces = [*split3(first_doc), *split3(second_doc)]
-            stacked = jnp.concatenate([*pieces, jnp.zeros((10, D), F32)], axis=0).astype(BF16)
+            terms = [*split3(first_doc), *split3(second_doc)]
+            stacked = jnp.concatenate([*terms, jnp.zeros((10, D), F32)], axis=0).astype(BF16)
             part = dg(stacked, w_ada_ref[:, piece * D : (piece + 1) * D], NT)
             gc_mine[0:1] += part[0:1] + part[1:2] + part[2:3]
             gc_mine[1:2] += part[3:4] + part[4:5] + part[5:6]
+
+    def small_early(w_ada_ref):
+        pack[...] = jnp.zeros_like(pack)
+        gc_mine[...] = jnp.zeros_like(gc_mine)
+        small_part(w_ada_ref, (2, 3, 4, 5))
         for s in range(32):
             col = 4 * D + 96 * s
             row = jnp.sum(small_ref[:, col : col + 96], axis=0, keepdims=True)
@@ -1150,6 +1181,9 @@
             col = 4 * D + FF + 96 * s
             pack[s, 18:19, 0:96] = jnp.sum(small_ref[:, col : col + 96], axis=0, keepdims=True)
 
+
+    def small_sums(w_ada_ref):
+        small_part(w_ada_ref, (0, 1))
         for other in others(n):
             s1_copy(other).start()
             gc_copy(other).start()
@@ -1305,6 +1339,8 @@
 
         lax.fori_loop(0, 4, add, 0)
         weights(1)
+        loads[6].wait()
+        small_early(w_ada_ref)
         normed, inv = norm_stats(tokens_ref[...].astype(F32))
         q_plane(0)
         q_z(1)
@@ -1319,7 +1355,6 @@
         mean = jnp.mean(grad, axis=-1, keepdims=True)
         along = jnp.mean(grad * normed, axis=-1, keepdims=True)
         gtok_ref[...] += (grad - mean - normed * along) * inv
-        loads[6].wait()
         small_sums(w_ada_ref)
 
         q_plane(1)
@@ -1491,8 +1526,8 @@
 
 
 def finish_kernel(
-    output_in, gtok_in, blocks, qkv_a, qkv_b, packet, gcond_in, output_out, gtok_out, gcond_out, gqkv, gout, gup, gdown, gada, gvec_ada,
-    gvec_one, gvec_two, gvec_up, gvec_down, wide, pass_sem
+    output_in, gtok_in, blocks, qkv_a, qkv_b, packet, gcond_in, output_out, gtok_out, gcond_out, gqkv_out, gout_out, gup_out, gdown_out, gada_out, gvec_ada,
+    gvec_one, gvec_two, gvec_up, gvec_down, wide, pass_sem, gqkv, gout, gup, gdown, gada, send_sem
 ):
     passed = [
         pltpu.make_async_copy(output_in, output_out, pass_sem.at[0]),
@@ -1501,17 +1536,27 @@
     for copy in passed:
         copy.start()
     gcond_out[0] = gcond_in[0:DOCS]
+    sends = [
+        pltpu.make_async_copy(src, dst, send_sem.at[i])
+        for i, (src, dst) in enumerate(
+            ((gup, gup_out), (gout, gout_out), (gdown, gdown_out), (gqkv, gqkv_out), (gada, gada_out))
+        )
+    ]
     for part in range(4):
         for hh in range(2):
             at = part * 768 + hh * 384
             gup[:, at : at + 384] = blocks[part, hh * 96 : (hh + 1) * 96, :].astype(F32)
         rh, ch = part // 2, part % 2
         gout[rh * 48 : (rh + 1) * 48, ch * 384 : (ch + 1) * 384] = blocks[part, 384:432, :].astype(F32)
+    sends[0].start()
+    sends[1].start()
     for pair in range(2):
         both = jnp.concatenate(
             [blocks[2 * pair, 192:384, :], blocks[2 * pair + 1, 192:384, :]], axis=0
         ).astype(F32)
         gdown[:, pair * 384 : (pair + 1) * 384] = both.T
+
+    sends[2].start()
 
     def head_block(part, head):
         g, j = head // OWN, head % OWN
@@ -1531,6 +1576,7 @@
             at = part * D + pair * 128
             gqkv[:, at : at + 128] = jnp.where(lane(even.shape) < 64, even, odd)
 
+    sends[3].start()
     conds = [packet[:, 19, :], packet[:, 20, :]]
     lhs = jnp.concatenate([conds[0]] * 3 + [conds[1]] * 3, axis=0).astype(BF16)
     for k in range(6):
@@ -1542,9 +1588,10 @@
         wide[row : row + 1, 96 * at : 96 * at + 96] = jnp.sum(packet[:, k, :], axis=0, keepdims=True)[
             :, :96
         ]
+    sends[4].start()
     for ref, row in ((gvec_ada, 0), (gvec_one, 1), (gvec_two, 2), (gvec_up, 3), (gvec_down, 4)):
         ref[...] = wide[row : row + 1, 0 : ref.shape[0]].reshape(ref.shape)
-    for copy in passed:
+    for copy in passed + sends:
         copy.wait()
 
 
@@ -1569,8 +1616,17 @@
             sds((96,), F32),
         ),
         in_specs=[vm()] * 7,
-        out_specs=(hbm(), hbm()) + (vm(),) * 11,
-        scratch_shapes=[VMEM((8, 576), F32), dma(2)],
+        out_specs=(hbm(), hbm(), vm()) + (hbm(),) * 5 + (vm(),) * 5,
+        scratch_shapes=[
+            VMEM((8, 576), F32),
+            dma(2),
+            VMEM((96, 3 * D), F32),
+            VMEM((96, D), F32),
+            VMEM((96, FF), F32),
+            VMEM((384, D), F32),
+            VMEM((576, 128), F32),
+            dma(5),
+        ],
         compiler_params=pltpu.CompilerParams(vmem_limit_bytes=62 * 2**20),
         cost_estimate=pl.CostEstimate(flops=10**7, bytes_accessed=10**7, transcendentals=0),
     )(output, gtok, blocks, qkv_a, qkv_b, packet, gcond)

time: 205 us -> 203 us (level)
  Pallas kernels: 203 us -> 199 us
    pallas_call x1, Pallas kernels: 59.7 us -> 57 us  [call_forward(): pl.pallas_call(forward_kernel, out_shape=(sds((local, D), BF16), sds((len...]
where the time goes in v5:
time: 203 us; the launch traced here: 201 us
  Pallas kernels  199 us (98%)
    pallas_call x1, Pallas kernels, call_fused(): pl.pallas_call(fused_kernel, out_shape=(sds((local, D), BF16), sds((local...  137 us
    pallas_call x1, Pallas kernels, call_forward(): pl.pallas_call(forward_kernel, out_shape=(sds((local, D), BF16), sds((len...  57 us
    pallas_call x1, Pallas kernels, call_finish(): pl.pallas_call(finish_kernel, out_shape=(sds((local, D), BF16), sds((loca...  5.5 us

profile of v5, /device:TPU:0, one launch (start us, length us, event | category | flops | bytes accessed | tf_op | source)
XLA Modules:
  0.0 201.0 jit_solution(14949480048809812533)
XLA Ops:
  1.3 57.0 %shard_map.246 = (bf16[512,768]{1,0:T(8,128)(2,1)}, bf16[2048,768]{1,0:T(8,128)(2,1)}, bf16[3,2048,128]{2,1,0:T(8,128)(2,1)}, bf16[3,2048,128]{2,1,0:T(8,128)(2,...) custom-call(s32[1]{0:T(128)S(6)} %copy.28.docs_ref, ...), custom_call_target="tpu_custom_call" | custom-call | flops 10000000000 | bytes 20000000 | tf_op jit(solution)/shard_map/pallas_call | solution.py:414
  58.3 136.9 %shard_map.247 = (bf16[512,768]{1,0:T(8,128)(2,1)}, f32[512,768]{1,0:T(8,128)}, bf16[4,432,384]{2,1,0:T(8,128)(2,1)}, bf16[4,96,384]{2,1,0:T(8,128)(2,1)}, bf16[...) custom-call(s32[1]{0:T(128)S(6)} %copy.28.docs_ref, bf16[512,768]{1,0:T(8,128)(2,1)} %bitcast.8, ...), custom_call_target="tpu_custom_call" | custom-call | flops 40000000000 | bytes 50000000 | tf_op jit(solution)/shard_map/pallas_call | solution.py:1444
  195.3 5.5 %shard_map.248 = (bf16[512,768]{1,0:T(8,128)(2,1)}, f32[512,768]{1,0:T(8,128)}, f32[1,2,128]{2,1,0:T(2,128)}, f32[96,2304]{1,0:T(8,128)}, f32[96,768]{1,0:T(8,12...) custom-call(bf16[512,768]{1,0:T(8,128)(2,1)} %get-tuple-element.49.o, ...), custom_call_target="tpu_custom_call" | custom-call | flops 10000000 | bytes 10000000 | tf_op jit(solution)/shard_map/pallas_call | solution.py:1601
